TPU v7x, 32 devices: a whole 2x2x4 slice. The times are simulated.
32 devices in a mesh: layer: 2 (over y), row: 16 (over z, x, core).
Axes of the slice: x: 2, y: 2, z: 4, core: 2. Of those that a mesh axis runs over, the one named last changes fastest.
Arguments:
- query_grads: bfloat16 [4, 512, 4096], P('layer', 'row'), may hold values from -6 to 6
- train_grads: bfloat16 [4, 8192, 4096], P('layer', 'row'), may hold values from -0.023925781 to 0.023925781
- left_inverse: float32 [4, 64, 64], P('layer'), may hold values from -0.75 to 0.75
- right_inverse: float32 [4, 64, 64], P('layer'), may hold values from -0.75 to 0.75
Outputs:
- scores: float32 [512, 8192], P('layer', 'row')
All inputs are finite; a program needn't handle non-finite values.
Results may differ from a plain program's by a relative error of at most 0.0029.
Values may be sent and summed in bfloat16 or wider, within the bound.
No kernel may reach another device: no remote copies, remote signals or barrier semaphores. Data moves between devices by JAX's collectives and lax.ppermute only.
A program may use at most 128 MiB of HBM per device.

v0:
```python
import jax
import jax.numpy as jnp
from jax import lax
from jax.sharding import PartitionSpec as P


def on_device(query_grads, train_grads, left_inverse, right_inverse):
    layers, rows, feat = query_grads.shape
    proj = left_inverse.shape[1]
    square = query_grads.astype(jnp.float32).reshape(layers, rows, proj, proj)
    rotated = jnp.einsum(
        "lab,lqbc,lcd->lqad", left_inverse, square, right_inverse, precision=lax.Precision.HIGHEST
    )
    rotated = rotated.reshape(layers, rows, feat).astype(jnp.bfloat16)
    partial_value = jnp.einsum(
        "lqf,ltf->qt",
        lax.all_gather(rotated, "row", axis=1, tiled=True),
        train_grads,
        preferred_element_type=jnp.float32,
    )
    return lax.psum_scatter(partial_value, "layer", scatter_dimension=0, tiled=True)


def solution(mesh):
    placed = (
        P("layer", "row", None),
        P("layer", "row", None),
        P("layer", None, None),
        P("layer", None, None),
    )
    return jax.shard_map(
        on_device, mesh=mesh, in_specs=placed, out_specs=P("layer", "row"), check_vma=False
    )
```

profile of v0, /device:TPU:0, one launch (start us, length us, event | category | flops | bytes accessed | tf_op | source)
XLA Modules:
  0.0 128.7 jit_solution(12139460078628174909)
XLA Ops:
  6.5 0.0 copy-start
  6.5 0.0 all-gather.2.cloned.1.call-start
  6.5 2.1 %reshape.5 = bf16[2,32,64,64]{3,2,1,0:T(8,128)(2,1)S(1)} reshape(bf16[2,32,4096]{2,1,0:T(8,128)(2,1)} %param.4) | data formatting | bytes 1048576 | tf_op jit(solution)/shard_map/reshape | solution.py:10
  8.6 0.0 copy-done
  8.6 1.0 fusion.1
  9.6 2.7 %convolution_convert_fusion = bf16[2,32,64,64]{3,2,1,0:T(8,128)(2,1)S(1)} fusion(f32[2,32,64,64]{2,3,1,0:T(8,128)S(1)} %fusion.1, f32[2,64,64]{2,1,0:T(8,128)} %param.7), kind=kOutput, calls=%fused_computation | convolution fusion | flops 201588736 | bytes 1605632 | tf_op jit(solution)/shard_map/lab,lqbc,lcd->lqad/dot_general | solution.py:11
  12.4 1.6 %convert_element_type.8 = bf16[2,32,4096]{2,1,0:T(8,128)(2,1)} reshape(bf16[2,32,64,64]{3,2,1,0:T(8,128)(2,1)S(1)} %convolution_convert_fusion) | data formatting | bytes 1048576 | tf_op jit(solution)/shard_map/convert_element_type | solution.py:14
  14.0 0.0 all-gather.2.cloned.1.call-update
  14.0 0.0 reduce-scatter.2.cloned.1.call-start
  14.1 77.7 %all-gather.2.cloned.1.call-done = bf16[2,512,4096]{2,1,0:T(8,128)(2,1)} async-done(((bf16[2,32,4096]{2,1,0:T(8,128)(2,1)}), bf16[2,512,4096]{2,1,0:T(8,128)(2,1)}) %all-gather.2.cloned.1.call-update) | async-done | bytes 8388624 | tf_op jit(solution)/shard_map/all_gather | solution.py:17
  91.8 11.3 %convolution_bitcast_fusion = f32[512,512]{1,0:T(8,128)} fusion(bf16[2,512,4096]{2,1,0:T(8,128)(2,1)} %all-gather.2.cloned.1.call-done, bf16[2,512,4096]{2,1,0:T(8,128)(2,1)} %param.5), kind=kOutput, calls=%fused_computation.1 | convolution fusion | flops 4294967296 | bytes 17825792 | tf_op jit(solution)/shard_map/lqf,ltf->qt/dot_general | solution.py:15
  103.1 0.0 reduce-scatter.2.cloned.1.call-update
  103.1 18.7 %reduce-scatter.2.cloned.1.call-done = f32[256,512]{1,0:T(8,128)} async-done(((f32[512,512]{1,0:T(8,128)}), f32[256,512]{1,0:T(8,128)}) %reduce-scatter.2.cloned.1.call-update) | async-done | bytes 524304 | tf_op jit(solution)/shard_map/reduce_scatter | solution.py:21
Async XLA Ops:
  6.5 2.1 %copy-start = (f32[2,64,64]{2,1,0:T(8,128)S(1)}, f32[2,64,64]{2,1,0:T(8,128)}, u32[]{:S(2)}) copy-start(f32[2,64,64]{2,1,0:T(8,128)} %param.6) | copy-start | bytes 98308
  6.5 85.2 %all-gather.2.cloned.1.call-start = ((), (), s32[]{:S(2)}) async-start(), calls=%async_computation.1 | async-start | bytes 8912896 | tf_op jit(solution)/shard_map/all_gather | solution.py:17
  14.0 107.8 %reduce-scatter.2.cloned.1.call-start = ((), (), s32[]{:S(2)}) async-start(), calls=%async_computation.2 | async-start | bytes 1572864 | tf_op jit(solution)/shard_map/reduce_scatter | solution.py:21
Sparse Core Ops, SparseCore 0:
  14.1 77.6 all-gather.1
  103.2 18.5 reduce-scatter.1
where the time goes:
time: 129 us
  waiting for transfers between devices  96.5 us (75%)
  matrix products  15 us (12%)
  between operations  13.4 us (10%)
  local copies, waits for them, and re-layouts  3.7 us (3%)
    all_gather x1, waiting for transfers between devices, on_device(): lax.all_gather(rotated, 'row', axis=1, tiled=True)  77.7 us
    reduce_scatter x1, waiting for transfers between devices, on_device(): lax.psum_scatter(partial_value, 'layer', scatter_dimension=0, tiled=True)  18.7 us
    dot_general x1, matrix products, on_device(): jnp.einsum('lqf,ltf->qt', lax.all_gather(rotated, 'row', axis=1, tiled=Tr...  11.3 us
    dot_general x2, matrix products, on_device(): jnp.einsum('lab,lqbc,lcd->lqad', left_inverse, square, right_inverse, pre...  3.71 us
  transfers between devices with their start and end apart: 2, of which 2 were waited for; matrix products, arithmetic and copies ran while one was open for 0% of the time, Pallas kernels for 0%

commit v1 on v0

--- a/solution.py
+++ b/solution.py
@@ -1,7 +1,289 @@
 import jax
 import jax.numpy as jnp
 from jax import lax
+from jax.experimental import pallas as pl
+from jax.experimental.pallas import tpu as pltpu
 from jax.sharding import PartitionSpec as P
+
+AXES = ("layer", "row")
+VMEM = pl.BlockSpec(memory_space=pltpu.VMEM)
+
+
+def halves(v):
+    top = v.astype(jnp.bfloat16)
+    return top, (v - top.astype(jnp.float32)).astype(jnp.bfloat16)
+
+
+def dot(a, b):
+    return jnp.dot(a, b, preferred_element_type=jnp.float32)
+
+
+def precondition_kernel(query, left, right, out, turned, mixed):
+    layers, rows, feat = query.shape
+    proj = left.shape[1]
+    half = proj // 2
+    pairs = feat // 128
+    i = lax.broadcasted_iota(jnp.int32, (2 * proj, 2 * proj), 0) // proj
+    j = lax.broadcasted_iota(jnp.int32, (2 * proj, 2 * proj), 1) // proj
+    diagonal = i == j
+    i = lax.broadcasted_iota(jnp.int32, (proj, proj), 0)
+    j = lax.broadcasted_iota(jnp.int32, (proj, proj), 1)
+    pick = (j == 2 * lax.rem(i, half) + i // half).astype(jnp.bfloat16)
+    pick_t = (i == 2 * lax.rem(j, half) + j // half).astype(jnp.bfloat16)
+    step = 8
+    low = lax.rem(lax.broadcasted_iota(jnp.int32, (pairs, step * 128), 1), 128) < proj
+    for l in range(layers):
+        wide = jnp.concatenate([right[l], right[l]], axis=1)
+        wide = jnp.where(diagonal, jnp.concatenate([wide, wide], axis=0), 0.0)
+        rr = jnp.concatenate(halves(wide), axis=0)
+        lh, ll = (dot(dot(pick, m).astype(jnp.bfloat16), pick_t).astype(jnp.bfloat16) for m in halves(left[l]))
+        lll = jnp.concatenate([lh, ll, lh], axis=1)
+        x = jnp.concatenate([query[l, :, k * 128:(k + 1) * 128] for k in range(pairs)], axis=0)
+        turned[l] = dot(jnp.concatenate([x, x], axis=1), rr)
+        for q0 in range(0, rows, step):
+            u = jnp.concatenate([turned[l, pl.ds(q, pairs, stride=rows), :] for q in range(q0, q0 + step)], axis=1)
+            v = jnp.concatenate(
+                [pltpu.roll(turned[l, pl.ds(q, pairs, stride=rows), :], proj, 1) for q in range(q0, q0 + step)], axis=1
+            )
+            wh, wl = halves(jnp.concatenate([jnp.where(low, u, v), jnp.where(low, v, u)], axis=0))
+            z = dot(lll, jnp.concatenate([wh, wh, wl], axis=0))
+            z = jnp.where(low, z[:half], z[half:])
+            for n in range(step):
+                mixed[l, pl.ds(q0 + n, pairs, stride=rows), :] = z[:, n * 128:(n + 1) * 128]
+        for m in range(pairs):
+            out[l, :, m * 128:(m + 1) * 128] = mixed[l, m * rows:(m + 1) * rows].astype(jnp.bfloat16)
+
+
+def precondition(query, left, right):
+    layers, rows, feat = query.shape
+    scratch = pltpu.VMEM((layers, rows * feat // 128, 128), jnp.float32)
+    return pl.pallas_call(
+        precondition_kernel,
+        out_shape=jax.ShapeDtypeStruct(query.shape, jnp.bfloat16),
+        in_specs=[VMEM] * 3,
+        out_specs=VMEM,
+        scratch_shapes=[scratch, scratch],
+        compiler_params=pltpu.CompilerParams(vmem_limit_bytes=16 << 20),
+        cost_estimate=pl.CostEstimate(flops=2 << 30, bytes_accessed=4 << 20, transcendentals=0),
+        name="precondition",
+    )(query, left, right)
+
+
+def transpose_kernel(train, pass_in, out, pass_out, buffer, sems):
+    del pass_in, pass_out
+    layers, rows, feat = train.shape
+    wide = buffer.shape[2]
+    steps = [(l, k) for l in range(layers) for k in range(0, feat, wide)]
+    deep = buffer.shape[0]
+
+    def copy(n):
+        l, k = steps[n]
+        return pltpu.make_async_copy(train.at[l, :, pl.ds(k, wide)], buffer.at[n % deep], sems.at[n % deep])
+
+    for n in range(deep - 1):
+        copy(n).start()
+    for n, (l, k) in enumerate(steps):
+        if n + deep - 1 < len(steps):
+            copy(n + deep - 1).start()
+        copy(n).wait()
+        out[l, k:k + wide, :] = buffer[n % deep].T
+
+
+def transpose(train, passed):
+    layers, rows, feat = train.shape
+    wide, deep = 512, 4
+    hbm = pl.BlockSpec(memory_space=pl.ANY)
+    return pl.pallas_call(
+        transpose_kernel,
+        out_shape=(jax.ShapeDtypeStruct((layers, feat, rows), train.dtype), jax.ShapeDtypeStruct(passed.shape, passed.dtype)),
+        in_specs=[hbm, hbm],
+        out_specs=(VMEM, hbm),
+        scratch_shapes=[pltpu.VMEM((deep, rows, wide), train.dtype), pltpu.SemaphoreType.DMA((deep,))],
+        input_output_aliases={1: 1},
+        compiler_params=pltpu.CompilerParams(vmem_limit_bytes=24 << 20),
+        cost_estimate=pl.CostEstimate(flops=4 << 30, bytes_accessed=16 << 20, transcendentals=0),
+        name="transpose",
+    )(train, passed)
+
+
+def score(turned, queries):
+    total = None
+    for l in range(turned.shape[0]):
+        rows = jnp.concatenate([q[l] for q in queries], axis=0)
+        term = dot(rows, turned[l])
+        total = term if total is None else total + term
+    return total
+
+
+def chip_at(offset):
+    row = lax.axis_index("row")
+    chip, core = row // 2, lax.rem(row, 2)
+    up, column = chip // 2, lax.rem(chip, 2)
+    place = jnp.where(column == 0, up, 7 - up) - offset * (1 - 2 * core)
+    place = lax.rem(place + 8, 8)
+    return jnp.where(place < 4, 2 * place, 2 * (7 - place) + 1)
+
+
+def foreign(offset):
+    return chip_at(offset) // 4 != lax.axis_index("layer")
+
+
+def put(out, at, offset, block):
+    rows = block.shape[0] // 2
+    core = lax.rem(lax.axis_index("row"), 2)
+    if offset < 0:
+        core = 1 - core
+    start = (at - 4 * lax.axis_index("layer")) * 2 * rows
+    out[pl.ds(pl.multiple_of(start + core * rows, rows), rows), :] = block[:rows]
+    out[pl.ds(pl.multiple_of(start + (1 - core) * rows, rows), rows), :] = block[rows:]
+
+
+def split(offset, ahead, behind, sent, kept):
+    @pl.when(foreign(offset))
+    def _():
+        sent[...] = ahead[...]
+        kept[...] = behind[...]
+
+    @pl.when(jnp.logical_not(foreign(offset)))
+    def _():
+        sent[...] = behind[...]
+        kept[...] = ahead[...]
+
+
+def plain_kernel(turned, *refs):
+    refs[-1][...] = score(turned, refs[:-1])
+
+
+def second_kernel(turned, *refs):
+    *queries, sent, kept, total = refs
+    half = sent.shape[0]
+    total[...] = score(turned, queries)
+    split(2, total.at[:half], total.at[half:], sent, kept)
+
+
+def third_kernel(turned, first, *refs):
+    *queries, sent, kept, total = refs
+    half = total.shape[0] // 2
+    total[...] = score(turned, queries)
+    split(1, first.at[:half], total.at[half:], sent.at[:half], kept.at[:half])
+    split(3, total.at[:half], first.at[half:], sent.at[half:], kept.at[half:])
+
+
+def fourth_kernel(turned, own, *refs):
+    *queries, sent, kept, total = refs
+    total[...] = score(turned, queries)
+    split(4, total, own, sent, kept)
+
+
+def block_call(kernel, name, rows, total, turned, operands):
+    columns = turned.shape[2]
+    block = jax.ShapeDtypeStruct((rows, columns), jnp.float32)
+    return pl.pallas_call(
+        kernel,
+        out_shape=(block, block) if total else block,
+        in_specs=[VMEM] * (1 + len(operands)),
+        out_specs=(VMEM, VMEM) if total else VMEM,
+        scratch_shapes=[pltpu.VMEM((total, columns), jnp.float32)] if total else [],
+        compiler_params=pltpu.CompilerParams(vmem_limit_bytes=24 << 20),
+        cost_estimate=pl.CostEstimate(flops=2 << 30, bytes_accessed=9 << 20, transcendentals=0),
+        name=name,
+    )(turned, *operands)
+
+
+def gather_kernel(kept2, got2, kept13, got13, out):
+    half = kept2.shape[0]
+
+    def place(offset, kept, got):
+        block = kept[...] + got[...]
+
+        @pl.when(foreign(offset))
+        def _():
+            put(out, chip_at(offset - 4), offset - 4, block)
+
+        @pl.when(jnp.logical_not(foreign(offset)))
+        def _():
+            put(out, chip_at(offset), offset, block)
+
+    place(2, kept2, got2)
+    place(1, kept13.at[:half], got13.at[:half])
+    place(3, kept13.at[half:], got13.at[half:])
+
+
+def last_kernel(kept, got, table, out, block, sems):
+    del table
+    rows = kept.shape[0] // 2
+    block[...] = kept[...] + got[...]
+    at = jnp.where(foreign(4), chip_at(0), chip_at(4)) - 4 * lax.axis_index("layer")
+    core = lax.rem(lax.axis_index("row"), 2)
+    copies = []
+    for n, c in enumerate((core, 1 - core)):
+        start = pl.multiple_of((2 * at + c) * rows, rows)
+        copies.append(pltpu.make_async_copy(block.at[n * rows:(n + 1) * rows], out.at[pl.ds(start, rows)], sems.at[n]))
+    for copy in copies:
+        copy.start()
+    for copy in copies:
+        copy.wait()
+
+
+def finish(parts, rows, columns):
+    (kept2, got2), (kept13, got13), (kept4, got4) = parts
+    hbm = pl.BlockSpec(memory_space=pl.ANY)
+    table = jax.ShapeDtypeStruct((rows, columns), jnp.float32)
+    params = pltpu.CompilerParams(vmem_limit_bytes=8 << 20)
+    most = pl.pallas_call(
+        gather_kernel, out_shape=table, in_specs=[VMEM] * 4, out_specs=VMEM, compiler_params=params, name="gather_rows"
+    )(kept2, got2, kept13, got13)
+    return pl.pallas_call(
+        last_kernel,
+        out_shape=table,
+        in_specs=[VMEM, VMEM, hbm],
+        out_specs=hbm,
+        scratch_shapes=[pltpu.VMEM(kept4.shape, jnp.float32), pltpu.SemaphoreType.DMA((2,))],
+        input_output_aliases={2: 0},
+        compiler_params=params,
+        name="last_rows",
+    )(kept4, got4, most)
+
+
+def ring_order(chips):
+    half = chips // 2
+    return [2 * i for i in range(half)] + [2 * i + 1 for i in reversed(range(half))]
+
+
+def ring_device(query_grads, train_grads, left_inverse, right_inverse):
+    chips, groups, cores = 8, 2, 2
+    order = ring_order(chips)
+    flat = lambda layer, chip, core: (layer * chips + chip) * cores + core
+    every = [(y, h, c) for y in range(groups) for h in range(chips) for c in range(cores)]
+    step = lambda h, c: order[(order.index(h) + (1 - 2 * c)) % chips]
+    swap = [(flat(y, h, c), flat(y, h, 1 - c)) for y, h, c in every]
+    across = [(flat(y, h, c), flat(1 - y, h, c)) for y, h, c in every]
+    around = [(flat(y, h, c), flat(y, step(h, c), c)) for y, h, c in every]
+    send = lambda v, pairs: lax.ppermute(v, AXES, pairs)
+
+    mine = precondition(query_grads, left_inverse, right_inverse)
+    theirs = send(mine, swap)
+    held = [mine, theirs]
+    turned, theirs_after = transpose(train_grads, theirs)
+    held = [mine, theirs_after]
+    rows = 2 * mine.shape[1]
+    zeroth = block_call(plain_kernel, "scores_0", rows, 0, turned, held)
+    pairs = []
+    for k in range(1, 4):
+        held = [send(h, around) for h in held]
+        queries = held + [send(h, swap) for h in held]
+        if k == 1:
+            first = block_call(plain_kernel, "scores_1", 2 * rows, 0, turned, queries)
+            continue
+        if k == 2:
+            sent, kept = block_call(second_kernel, "scores_2", rows, 2 * rows, turned, queries)
+        else:
+            sent, kept = block_call(third_kernel, "scores_3", 2 * rows, 2 * rows, turned, [first] + queries)
+        pairs.append((kept, send(sent, across)))
+    end = send(held[0], around)
+    sent, kept = block_call(fourth_kernel, "scores_4", rows, rows, turned, [zeroth, end, send(end, swap)])
+    pairs.append((kept, send(sent, across)))
+    return finish(pairs, chips // groups * rows, turned.shape[2])
 
 
 def on_device(query_grads, train_grads, left_inverse, right_inverse):
@@ -28,6 +310,7 @@
         P("layer", None, None),
         P("layer", None, None),
     )
+    ring = mesh.shape["layer"] == 2 and mesh.shape["row"] == 16
     return jax.shard_map(
-        on_device, mesh=mesh, in_specs=placed, out_specs=P("layer", "row"), check_vma=False
+        ring_device if ring else on_device, mesh=mesh, in_specs=placed, out_specs=P("layer", "row"), check_vma=False
     )

time: 129 us -> 71.7 us (0.56)
  waiting for transfers between devices: 96.5 us -> 30.5 us
  starting transfers between devices: 0.04 us -> 19.1 us
  Pallas kernels: 0 us -> 15.6 us
  matrix products: 15 us -> 0 us
  between operations: 13.4 us -> 0.09 us
  local copies, waits for them, and re-layouts: 3.7 us -> 6.1 us
    all_gather x1 -> x0, waiting for transfers between devices: 77.7 us -> none  [on_device(): lax.all_gather(rotated, 'row', axis=1, tiled=True)]
    ppermute x0 -> x18, waiting for transfers between devices: none -> 30.5 us  [ring_device(): send = lambda v, pairs: lax.ppermute(v, AXES, pairs)]
    ppermute x0 -> x18, starting transfers between devices: none -> 19.1 us  [ring_device(): send = lambda v, pairs: lax.ppermute(v, AXES, pairs)]
    reduce_scatter x1 -> x0, waiting for transfers between devices: 18.7 us -> none  [on_device(): lax.psum_scatter(partial_value, 'layer', scatter_dimension=0, tiled=True)]
    pallas_call x0 -> x9, Pallas kernels: none -> 15.6 us  [the longest x5 6.94 us: block_call(): pl.pallas_call(kernel, out_shape=(block, block) if total else block, in_s...]
    dot_general x3 -> x0, matrix products: 15 us -> none  [the longest x1 11.3 us: on_device(): jnp.einsum('lqf,ltf->qt', lax.all_gather(rotated, 'row', axis=1, tiled=Tr...]
    unnamed x2 -> x8, local copies, waits for them, and re-layouts: 0.01 us -> 6.1 us
    reshape x1 -> x0, local copies, waits for them, and re-layouts: 2.08 us -> none  [on_device(): square = query_grads.astype(jnp.float32).reshape(layers, rows, proj, proj)]
  transfers between devices with their start and end apart: 2 -> 18, of which waited for: 2 -> 8; matrix products, arithmetic and copies ran while one was open for 0% -> 0% of each run, Pallas kernels for 0% -> 17%
where the time goes in v1:
time: 71.7 us; the launch traced here: 71.4 us
  waiting for transfers between devices  30.5 us (43%)
  starting transfers between devices  19.1 us (27%)
  Pallas kernels  15.6 us (22%)
  local copies, waits for them, and re-layouts  6.1 us (9%)
    ppermute x18, waiting for transfers between devices, ring_device(): send = lambda v, pairs: lax.ppermute(v, AXES, pairs)  30.5 us
    ppermute x18, starting transfers between devices, ring_device(): send = lambda v, pairs: lax.ppermute(v, AXES, pairs)  19.1 us
    pallas_call x5, Pallas kernels, block_call(): pl.pallas_call(kernel, out_shape=(block, block) if total else block, in_s...  6.94 us
    unnamed x8, local copies, waits for them, and re-layouts  6.1 us
    pallas_call x1, Pallas kernels, transpose(): pl.pallas_call(transpose_kernel, out_shape=(jax.ShapeDtypeStruct((layers,...  4.38 us
    pallas_call x1, Pallas kernels, precondition(): pl.pallas_call(precondition_kernel, out_shape=jax.ShapeDtypeStruct(query....  2.72 us
  transfers between devices with their start and end apart: 18, of which 8 were waited for; matrix products, arithmetic and copies ran while one was open for 0% of the time, Pallas kernels for 17%

profile of v1, /device:TPU:0, one launch (start us, length us, event | category | flops | bytes accessed | tf_op | source)
XLA Modules:
  0.0 71.4 jit_solution(563389429878829394)
XLA Ops:
  2.7 2.7 %precondition.1.refs_0_ = bf16[2,32,4096]{2,1,0:T(8,128)(2,1)S(1)} custom-call(bf16[2,32,4096]{2,1,0:T(8,128)(2,1)S(1)} %copy-done.1, f32[2,64,64]{2,1,0:T(8,128)S(1)} %copy-done.2, f32[2,64,64]{2,1,0:T(8,128)S(1)} %copy-done.3), custom_call_target="tpu_custom_call" | custom-call | flops 2147483648 | bytes 4194304 | tf_op jit(solution)/shard_map/precondition/pallas_call | solution.py:60
  6.0 2.6 %collective-permute-start.1 = (bf16[2,32,4096]{2,1,0:T(8,128)(2,1)S(1)}, bf16[2,32,4096]{2,1,0:T(8,128)(2,1)S(1)}, u32[]{:S(2)}, u32[]{:S(2)}) collective-permute-start(bf16[2,32,4096]{2,1,0:T(8,128)(2,1)S(1)} %precondition.1.refs_0_), channel_id=1, source_target_pairs={{0,4},{1,3},{2,0},{3,7},{4,8},{5,1},{6,2},{7,11},{8,12},{9,5},{10,... | collective-permute-start | bytes 1572872 | tf_op jit(solution)/shard_map/ppermute | solution.py:262
  8.6 3.4 %copy-done = bf16[2,512,4096]{2,1,0:T(8,128)(2,1)S(1)} copy-done((bf16[2,512,4096]{2,1,0:T(8,128)(2,1)S(1)}, bf16[2,512,4096]{2,1,0:T(8,128)(2,1)}, u32[]{:S(2)}) %copy-start) | copy-done | bytes 8388632
  12.0 4.4 %transpose.1 = (bf16[2,4096,512]{2,1,0:T(8,128)(2,1)S(1)}, bf16[2,32,4096]{2,1,0:T(8,128)(2,1)S(1)}) custom-call(bf16[2,512,4096]{2,1,0:T(8,128)(2,1)S(1)} %copy-done, bf16[2,32,4096]{2,1,0:T(8,128)(2,1)S(1)} %collective-permute-done.pass_in), custom_call_target="tpu_custom_call", output_to_operand_aliasing={{1}: (1, {})} | custom-call | flops 4294967296 | bytes 16777216 | tf_op jit(solution)/shard_map/transpose/pallas_call | solution.py:96
  16.4 1.9 %collective-permute-start.7 = (bf16[2,32,4096]{2,1,0:T(8,128)(2,1)S(1)}, bf16[2,32,4096]{2,1,0:T(8,128)(2,1)S(1)}, u32[]{:S(2)}, u32[]{:S(2)}) collective-permute-start(bf16[2,32,4096]{2,1,0:T(8,128)(2,1)S(1)} %get-tuple-element.14.refs_1_), channel_id=1, source_target_pairs={{0,4},{1,3},{2,0},{3,7},{4,8},{5,1},{6,2},{7,11},{8,12},{9,5},{10,... | collective-permute-start | bytes 1572872 | tf_op jit(solution)/shard_map/ppermute | solution.py:262
  18.3 1.6 %collective-permute-start.2 = (bf16[2,32,4096]{2,1,0:T(8,128)(2,1)S(1)}, bf16[2,32,4096]{2,1,0:T(8,128)(2,1)S(1)}, u32[]{:S(2)}, u32[]{:S(2)}) collective-permute-start(bf16[2,32,4096]{2,1,0:T(8,128)(2,1)S(1)} %collective-permute-done.1.refs_0_), channel_id=1, source_target_pairs={{0,4},{1,3},{2,0},{3,7},{4,8},{5,1},{6,2},{7,11},{8,12},{9,5},{10,... | collective-permute-start | bytes 1572872 | tf_op jit(solution)/shard_map/ppermute | solution.py:262
  19.9 5.8 %collective-permute-done.7.refs_1_ = bf16[2,32,4096]{2,1,0:T(8,128)(2,1)S(1)} collective-permute-done((bf16[2,32,4096]{2,1,0:T(8,128)(2,1)S(1)}, bf16[2,32,4096]{2,1,0:T(8,128)(2,1)S(1)}, u32[]{:S(2)}, u32[]{:S(2)}) %collective-permute-start.7) | collective-permute-done | bytes 524320 | tf_op jit(solution)/shard_map/ppermute | solution.py:262
  25.6 1.8 %collective-permute-start.8 = (bf16[2,32,4096]{2,1,0:T(8,128)(2,1)S(1)}, bf16[2,32,4096]{2,1,0:T(8,128)(2,1)S(1)}, u32[]{:S(2)}, u32[]{:S(2)}) collective-permute-start(bf16[2,32,4096]{2,1,0:T(8,128)(2,1)S(1)} %collective-permute-done.7.refs_1_), channel_id=1, source_target_pairs={{0,4},{1,3},{2,0},{3,7},{4,8},{5,1},{6,2},{7,11},{8,12},{9,5},{10,... | collective-permute-start | bytes 1572872 | tf_op jit(solution)/shard_map/ppermute | solution.py:262
  27.5 3.8 %collective-permute-done.2.refs_0_ = bf16[2,32,4096]{2,1,0:T(8,128)(2,1)S(1)} collective-permute-done((bf16[2,32,4096]{2,1,0:T(8,128)(2,1)S(1)}, bf16[2,32,4096]{2,1,0:T(8,128)(2,1)S(1)}, u32[]{:S(2)}, u32[]{:S(2)}) %collective-permute-start.2) | collective-permute-done | bytes 524320 | tf_op jit(solution)/shard_map/ppermute | solution.py:262
  31.2 1.8 %collective-permute-start.3 = (bf16[2,32,4096]{2,1,0:T(8,128)(2,1)S(1)}, bf16[2,32,4096]{2,1,0:T(8,128)(2,1)S(1)}, u32[]{:S(2)}, u32[]{:S(2)}) collective-permute-start(bf16[2,32,4096]{2,1,0:T(8,128)(2,1)S(1)} %collective-permute-done.2.refs_0_), channel_id=1, source_target_pairs={{0,4},{1,3},{2,0},{3,7},{4,8},{5,1},{6,2},{7,11},{8,12},{9,5},{10,... | collective-permute-start | bytes 1572872 | tf_op jit(solution)/shard_map/ppermute | solution.py:262
  33.6 3.3 %collective-permute-done.8.refs_1_ = bf16[2,32,4096]{2,1,0:T(8,128)(2,1)S(1)} collective-permute-done((bf16[2,32,4096]{2,1,0:T(8,128)(2,1)S(1)}, bf16[2,32,4096]{2,1,0:T(8,128)(2,1)S(1)}, u32[]{:S(2)}, u32[]{:S(2)}) %collective-permute-start.8) | collective-permute-done | bytes 524320 | tf_op jit(solution)/shard_map/ppermute | solution.py:262
  36.8 1.8 %collective-permute-start.14 = (bf16[2,32,4096]{2,1,0:T(8,128)(2,1)S(1)}, bf16[2,32,4096]{2,1,0:T(8,128)(2,1)S(1)}, u32[]{:S(2)}, u32[]{:S(2)}) collective-permute-start(bf16[2,32,4096]{2,1,0:T(8,128)(2,1)S(1)} %collective-permute-done.8.refs_1_), channel_id=1, source_target_pairs={{0,4},{1,3},{2,0},{3,7},{4,8},{5,1},{6,2},{7,11},{8,12},{9,5},{10,... | collective-permute-start | bytes 1572872 | tf_op jit(solution)/shard_map/ppermute | solution.py:262
  38.7 3.8 %collective-permute-done.3.refs_0_ = bf16[2,32,4096]{2,1,0:T(8,128)(2,1)S(1)} collective-permute-done((bf16[2,32,4096]{2,1,0:T(8,128)(2,1)S(1)}, bf16[2,32,4096]{2,1,0:T(8,128)(2,1)S(1)}, u32[]{:S(2)}, u32[]{:S(2)}) %collective-permute-start.3) | collective-permute-done | bytes 524320 | tf_op jit(solution)/shard_map/ppermute | solution.py:262
  42.5 1.8 %collective-permute-start.4 = (bf16[2,32,4096]{2,1,0:T(8,128)(2,1)S(1)}, bf16[2,32,4096]{2,1,0:T(8,128)(2,1)S(1)}, u32[]{:S(2)}, u32[]{:S(2)}) collective-permute-start(bf16[2,32,4096]{2,1,0:T(8,128)(2,1)S(1)} %collective-permute-done.3.refs_0_), channel_id=1, source_target_pairs={{0,4},{1,3},{2,0},{3,7},{4,8},{5,1},{6,2},{7,11},{8,12},{9,5},{10,... | collective-permute-start | bytes 1572872 | tf_op jit(solution)/shard_map/ppermute | solution.py:262
  44.9 3.2 %collective-permute-done.14.refs_1_ = bf16[2,32,4096]{2,1,0:T(8,128)(2,1)S(1)} collective-permute-done((bf16[2,32,4096]{2,1,0:T(8,128)(2,1)S(1)}, bf16[2,32,4096]{2,1,0:T(8,128)(2,1)S(1)}, u32[]{:S(2)}, u32[]{:S(2)}) %collective-permute-start.14) | collective-permute-done | bytes 524320 | tf_op jit(solution)/shard_map/ppermute | solution.py:262
  48.1 1.5 %scores_0.1.own = f32[64,512]{1,0:T(8,128)S(1)} custom-call(bf16[2,4096,512]{2,1,0:T(8,128)(2,1)S(1)} %get-tuple-element.13.turned, bf16[2,32,4096]{2,1,0:T(8,128)(2,1)S(1)} %precondition.1.refs_0_, bf16[2,32,4096]{2,1,0:T(8,128)(2,1)S(1)} %get-tuple-element.14.refs_1_), custom_call_target="tpu_custom_call" | custom-call | flops 2147483648 | bytes 9437184 | tf_op jit(solution)/shard_map/scores_0/pallas_call | solution.py:181
  49.6 4.1 %collective-permute-done.4.refs_0_ = bf16[2,32,4096]{2,1,0:T(8,128)(2,1)S(1)} collective-permute-done((bf16[2,32,4096]{2,1,0:T(8,128)(2,1)S(1)}, bf16[2,32,4096]{2,1,0:T(8,128)(2,1)S(1)}, u32[]{:S(2)}, u32[]{:S(2)}) %collective-permute-start.4) | collective-permute-done | bytes 524320 | tf_op jit(solution)/shard_map/ppermute | solution.py:262
  53.7 1.3 %scores_1.1.first = f32[128,512]{1,0:T(8,128)S(1)} custom-call(bf16[2,4096,512]{2,1,0:T(8,128)(2,1)S(1)} %get-tuple-element.13.turned, bf16[2,32,4096]{2,1,0:T(8,128)(2,1)S(1)} %collective-permute-done.1.refs_0_, bf16[2,32,4096]{2,1,0:T(8,128)(2,1)S(1)} %collective-permute-done.7.refs_1_, bf16[2,32,4096]{2,1,0:T(8,128)(2,1)S(1)} %collective-permute-done.12.refs_2_, ...), custom_call_target="tpu_custom_call" | custom-call | flops 2147483648 | bytes 9437184 | tf_op jit(solution)/shard_map/scores_1/pallas_call | solution.py:181
  55.0 1.3 %scores_2.1 = (f32[64,512]{1,0:T(8,128)S(1)}, f32[64,512]{1,0:T(8,128)S(1)}) custom-call(bf16[2,4096,512]{2,1,0:T(8,128)(2,1)S(1)} %get-tuple-element.13.turned, bf16[2,32,4096]{2,1,0:T(8,128)(2,1)S(1)} %collective-permute-done.2.refs_0_, bf16[2,32,4096]{2,1,0:T(8,128)(2,1)S(1)} %collective-permute-done.8.refs_1_, ...), custom_call_target="tpu_custom_call" | custom-call | flops 2147483648 | bytes 9437184 | tf_op jit(solution)/shard_map/scores_2/pallas_call | solution.py:181
  56.3 1.9 %collective-permute-start.11 = (f32[64,512]{1,0:T(8,128)S(1)}, f32[64,512]{1,0:T(8,128)S(1)}, u32[]{:S(2)}, u32[]{:S(2)}) collective-permute-start(f32[64,512]{1,0:T(8,128)S(1)} %get-tuple-element.18), channel_id=1, source_target_pairs={{0,16},{1,17},{2,18},{3,19},{4,20},{5,21},{6,22},{7,23},{8,24},{9,... | collective-permute-start | bytes 393224 | tf_op jit(solution)/shard_map/ppermute | solution.py:262
  58.1 1.3 %scores_3.1 = (f32[128,512]{1,0:T(8,128)S(1)}, f32[128,512]{1,0:T(8,128)S(1)}) custom-call(bf16[2,4096,512]{2,1,0:T(8,128)(2,1)S(1)} %get-tuple-element.13.turned, f32[128,512]{1,0:T(8,128)S(1)} %scores_1.1.first, bf16[2,32,4096]{2,1,0:T(8,128)(2,1)S(1)} %collective-permute-done.3.refs_0_, bf16[2,32,4096]{2,1,0:T(8,128)(2,1)S(1)} %collective-permute-done.14.refs_1_, ...), custom_call_target="tpu_custom_call" | custom-call | flops 2147483648 | bytes 9437184 | tf_op jit(solution)/shard_map/scores_3/pallas_call | solution.py:181
  59.7 1.6 %scores_4.1 = (f32[64,512]{1,0:T(8,128)S(1)}, f32[64,512]{1,0:T(8,128)S(1)}) custom-call(bf16[2,4096,512]{2,1,0:T(8,128)(2,1)S(1)} %get-tuple-element.13.turned, f32[64,512]{1,0:T(8,128)S(1)} %scores_0.1.own, bf16[2,32,4096]{2,1,0:T(8,128)(2,1)S(1)} %collective-permute-done.4.refs_0_, bf16[2,32,4096]{2,1,0:T(8,128)(2,1)S(1)} %collective-permute-done.5.refs_1_), custom_call_target="tpu_custom_call" | custom-call | flops 2147483648 | bytes 9437184 | tf_op jit(solution)/shard_map/scores_4/pallas_call | solution.py:181
  61.3 1.9 %collective-permute-start.6 = (f32[64,512]{1,0:T(8,128)S(1)}, f32[64,512]{1,0:T(8,128)S(1)}, u32[]{:S(2)}, u32[]{:S(2)}) collective-permute-start(f32[64,512]{1,0:T(8,128)S(1)} %get-tuple-element.16), channel_id=1, source_target_pairs={{0,16},{1,17},{2,18},{3,19},{4,20},{5,21},{6,22},{7,23},{8,24},{9,... | collective-permute-start | bytes 393224 | tf_op jit(solution)/shard_map/ppermute | solution.py:262
  63.2 5.5 %collective-permute-done.17.got13 = f32[128,512]{1,0:T(8,128)S(1)} collective-permute-done((f32[128,512]{1,0:T(8,128)S(1)}, f32[128,512]{1,0:T(8,128)S(1)}, u32[]{:S(2)}, u32[]{:S(2)}) %collective-permute-start.17) | collective-permute-done | bytes 262176 | tf_op jit(solution)/shard_map/ppermute | solution.py:262
  (29 shorter events, 7.5 us)
Async XLA Ops:
  0.0 1.0 %copy-start.1 = (bf16[2,32,4096]{2,1,0:T(8,128)(2,1)S(1)}, bf16[2,32,4096]{2,1,0:T(8,128)(2,1)}, u32[]{:S(2)}) copy-start(bf16[2,32,4096]{2,1,0:T(8,128)(2,1)} %query.1) | copy-start | bytes 1572868
  1.0 0.8 %copy-start.2 = (f32[2,64,64]{2,1,0:T(8,128)S(1)}, f32[2,64,64]{2,1,0:T(8,128)}, u32[]{:S(2)}) copy-start(f32[2,64,64]{2,1,0:T(8,128)} %left.1) | copy-start | bytes 98308
  1.9 0.8 %copy-start.3 = (f32[2,64,64]{2,1,0:T(8,128)S(1)}, f32[2,64,64]{2,1,0:T(8,128)}, u32[]{:S(2)}) copy-start(f32[2,64,64]{2,1,0:T(8,128)} %right.1) | copy-start | bytes 98308
  5.4 3.2 %collective-permute-start = (bf16[2,32,4096]{2,1,0:T(8,128)(2,1)S(1)}, bf16[2,32,4096]{2,1,0:T(8,128)(2,1)S(1)}, u32[]{:S(2)}, u32[]{:S(2)}) collective-permute-start(bf16[2,32,4096]{2,1,0:T(8,128)(2,1)S(1)} %precondition.1.refs_0_), channel_id=1, source_target_pairs={{0,1},{1,0},{2,3},{3,2},{4,5},{5,4},{6,7},{7,6},{8,9},{9,8},{10,11... | collective-permute-start | bytes 1572872 | tf_op jit(solution)/shard_map/ppermute | solution.py:262
  6.0 12.3 %collective-permute-start.1 = (bf16[2,32,4096]{2,1,0:T(8,128)(2,1)S(1)}, bf16[2,32,4096]{2,1,0:T(8,128)(2,1)S(1)}, u32[]{:S(2)}, u32[]{:S(2)}) collective-permute-start(bf16[2,32,4096]{2,1,0:T(8,128)(2,1)S(1)} %precondition.1.refs_0_), channel_id=1, source_target_pairs={{0,4},{1,3},{2,0},{3,7},{4,8},{5,1},{6,2},{7,11},{8,12},{9,5},{10,... | collective-permute-start | bytes 1572872 | tf_op jit(solution)/shard_map/ppermute | solution.py:262
  8.6 3.4 %copy-start = (bf16[2,512,4096]{2,1,0:T(8,128)(2,1)S(1)}, bf16[2,512,4096]{2,1,0:T(8,128)(2,1)}, u32[]{:S(2)}) copy-start(bf16[2,512,4096]{2,1,0:T(8,128)(2,1)} %train.1) | copy-start | bytes 25165828
  16.4 9.2 %collective-permute-start.7 = (bf16[2,32,4096]{2,1,0:T(8,128)(2,1)S(1)}, bf16[2,32,4096]{2,1,0:T(8,128)(2,1)S(1)}, u32[]{:S(2)}, u32[]{:S(2)}) collective-permute-start(bf16[2,32,4096]{2,1,0:T(8,128)(2,1)S(1)} %get-tuple-element.14.refs_1_), channel_id=1, source_target_pairs={{0,4},{1,3},{2,0},{3,7},{4,8},{5,1},{6,2},{7,11},{8,12},{9,5},{10,... | collective-permute-start | bytes 1572872 | tf_op jit(solution)/shard_map/ppermute | solution.py:262
  18.3 13.0 %collective-permute-start.2 = (bf16[2,32,4096]{2,1,0:T(8,128)(2,1)S(1)}, bf16[2,32,4096]{2,1,0:T(8,128)(2,1)S(1)}, u32[]{:S(2)}, u32[]{:S(2)}) collective-permute-start(bf16[2,32,4096]{2,1,0:T(8,128)(2,1)S(1)} %collective-permute-done.1.refs_0_), channel_id=1, source_target_pairs={{0,4},{1,3},{2,0},{3,7},{4,8},{5,1},{6,2},{7,11},{8,12},{9,5},{10,... | collective-permute-start | bytes 1572872 | tf_op jit(solution)/shard_map/ppermute | solution.py:262
  25.6 11.2 %collective-permute-start.8 = (bf16[2,32,4096]{2,1,0:T(8,128)(2,1)S(1)}, bf16[2,32,4096]{2,1,0:T(8,128)(2,1)S(1)}, u32[]{:S(2)}, u32[]{:S(2)}) collective-permute-start(bf16[2,32,4096]{2,1,0:T(8,128)(2,1)S(1)} %collective-permute-done.7.refs_1_), channel_id=1, source_target_pairs={{0,4},{1,3},{2,0},{3,7},{4,8},{5,1},{6,2},{7,11},{8,12},{9,5},{10,... | collective-permute-start | bytes 1572872 | tf_op jit(solution)/shard_map/ppermute | solution.py:262
  31.2 11.2 %collective-permute-start.3 = (bf16[2,32,4096]{2,1,0:T(8,128)(2,1)S(1)}, bf16[2,32,4096]{2,1,0:T(8,128)(2,1)S(1)}, u32[]{:S(2)}, u32[]{:S(2)}) collective-permute-start(bf16[2,32,4096]{2,1,0:T(8,128)(2,1)S(1)} %collective-permute-done.2.refs_0_), channel_id=1, source_target_pairs={{0,4},{1,3},{2,0},{3,7},{4,8},{5,1},{6,2},{7,11},{8,12},{9,5},{10,... | collective-permute-start | bytes 1572872 | tf_op jit(solution)/shard_map/ppermute | solution.py:262
  33.1 11.2 %collective-permute-start.12 = (bf16[2,32,4096]{2,1,0:T(8,128)(2,1)S(1)}, bf16[2,32,4096]{2,1,0:T(8,128)(2,1)S(1)}, u32[]{:S(2)}, u32[]{:S(2)}) collective-permute-start(bf16[2,32,4096]{2,1,0:T(8,128)(2,1)S(1)} %collective-permute-done.1.refs_0_), channel_id=1, source_target_pairs={{0,1},{1,0},{2,3},{3,2},{4,5},{5,4},{6,7},{7,6},{8,9},{9,8},{10,11... | collective-permute-start | bytes 1572872 | tf_op jit(solution)/shard_map/ppermute | solution.py:262
  33.1 11.7 %collective-permute-start.13 = (bf16[2,32,4096]{2,1,0:T(8,128)(2,1)S(1)}, bf16[2,32,4096]{2,1,0:T(8,128)(2,1)S(1)}, u32[]{:S(2)}, u32[]{:S(2)}) collective-permute-start(bf16[2,32,4096]{2,1,0:T(8,128)(2,1)S(1)} %collective-permute-done.7.refs_1_), channel_id=1, source_target_pairs={{0,1},{1,0},{2,3},{3,2},{4,5},{5,4},{6,7},{7,6},{8,9},{9,8},{10,11... | collective-permute-start | bytes 1572872 | tf_op jit(solution)/shard_map/ppermute | solution.py:262
  36.8 11.2 %collective-permute-start.14 = (bf16[2,32,4096]{2,1,0:T(8,128)(2,1)S(1)}, bf16[2,32,4096]{2,1,0:T(8,128)(2,1)S(1)}, u32[]{:S(2)}, u32[]{:S(2)}) collective-permute-start(bf16[2,32,4096]{2,1,0:T(8,128)(2,1)S(1)} %collective-permute-done.8.refs_1_), channel_id=1, source_target_pairs={{0,4},{1,3},{2,0},{3,7},{4,8},{5,1},{6,2},{7,11},{8,12},{9,5},{10,... | collective-permute-start | bytes 1572872 | tf_op jit(solution)/shard_map/ppermute | solution.py:262
  42.5 11.2 %collective-permute-start.4 = (bf16[2,32,4096]{2,1,0:T(8,128)(2,1)S(1)}, bf16[2,32,4096]{2,1,0:T(8,128)(2,1)S(1)}, u32[]{:S(2)}, u32[]{:S(2)}) collective-permute-start(bf16[2,32,4096]{2,1,0:T(8,128)(2,1)S(1)} %collective-permute-done.3.refs_0_), channel_id=1, source_target_pairs={{0,4},{1,3},{2,0},{3,7},{4,8},{5,1},{6,2},{7,11},{8,12},{9,5},{10,... | collective-permute-start | bytes 1572872 | tf_op jit(solution)/shard_map/ppermute | solution.py:262
  44.3 10.7 %collective-permute-start.9 = (bf16[2,32,4096]{2,1,0:T(8,128)(2,1)S(1)}, bf16[2,32,4096]{2,1,0:T(8,128)(2,1)S(1)}, u32[]{:S(2)}, u32[]{:S(2)}) collective-permute-start(bf16[2,32,4096]{2,1,0:T(8,128)(2,1)S(1)} %collective-permute-done.2.refs_0_), channel_id=1, source_target_pairs={{0,1},{1,0},{2,3},{3,2},{4,5},{5,4},{6,7},{7,6},{8,9},{9,8},{10,11... | collective-permute-start | bytes 1572872 | tf_op jit(solution)/shard_map/ppermute | solution.py:262
  44.3 10.7 %collective-permute-start.10 = (bf16[2,32,4096]{2,1,0:T(8,128)(2,1)S(1)}, bf16[2,32,4096]{2,1,0:T(8,128)(2,1)S(1)}, u32[]{:S(2)}, u32[]{:S(2)}) collective-permute-start(bf16[2,32,4096]{2,1,0:T(8,128)(2,1)S(1)} %collective-permute-done.8.refs_1_), channel_id=1, source_target_pairs={{0,1},{1,0},{2,3},{3,2},{4,5},{5,4},{6,7},{7,6},{8,9},{9,8},{10,11... | collective-permute-start | bytes 1572872 | tf_op jit(solution)/shard_map/ppermute | solution.py:262
  44.8 13.3 %collective-permute-start.15 = (bf16[2,32,4096]{2,1,0:T(8,128)(2,1)S(1)}, bf16[2,32,4096]{2,1,0:T(8,128)(2,1)S(1)}, u32[]{:S(2)}, u32[]{:S(2)}) collective-permute-start(bf16[2,32,4096]{2,1,0:T(8,128)(2,1)S(1)} %collective-permute-done.3.refs_0_), channel_id=1, source_target_pairs={{0,1},{1,0},{2,3},{3,2},{4,5},{5,4},{6,7},{7,6},{8,9},{9,8},{10,11... | collective-permute-start | bytes 1572872 | tf_op jit(solution)/shard_map/ppermute | solution.py:262
  48.1 10.0 %collective-permute-start.16 = (bf16[2,32,4096]{2,1,0:T(8,128)(2,1)S(1)}, bf16[2,32,4096]{2,1,0:T(8,128)(2,1)S(1)}, u32[]{:S(2)}, u32[]{:S(2)}) collective-permute-start(bf16[2,32,4096]{2,1,0:T(8,128)(2,1)S(1)} %collective-permute-done.14.refs_1_), channel_id=1, source_target_pairs={{0,1},{1,0},{2,3},{3,2},{4,5},{5,4},{6,7},{7,6},{8,9},{9,8},{10,11... | collective-permute-start | bytes 1572872 | tf_op jit(solution)/shard_map/ppermute | solution.py:262
  53.7 6.0 %collective-permute-start.5 = (bf16[2,32,4096]{2,1,0:T(8,128)(2,1)S(1)}, bf16[2,32,4096]{2,1,0:T(8,128)(2,1)S(1)}, u32[]{:S(2)}, u32[]{:S(2)}) collective-permute-start(bf16[2,32,4096]{2,1,0:T(8,128)(2,1)S(1)} %collective-permute-done.4.refs_0_), channel_id=1, source_target_pairs={{0,1},{1,0},{2,3},{3,2},{4,5},{5,4},{6,7},{7,6},{8,9},{9,8},{10,11... | collective-permute-start | bytes 1572872 | tf_op jit(solution)/shard_map/ppermute | solution.py:262
  56.3 6.9 %collective-permute-start.11 = (f32[64,512]{1,0:T(8,128)S(1)}, f32[64,512]{1,0:T(8,128)S(1)}, u32[]{:S(2)}, u32[]{:S(2)}) collective-permute-start(f32[64,512]{1,0:T(8,128)S(1)} %get-tuple-element.18), channel_id=1, source_target_pairs={{0,16},{1,17},{2,18},{3,19},{4,20},{5,21},{6,22},{7,23},{8,24},{9,... | collective-permute-start | bytes 393224 | tf_op jit(solution)/shard_map/ppermute | solution.py:262
  59.4 9.2 %collective-permute-start.17 = (f32[128,512]{1,0:T(8,128)S(1)}, f32[128,512]{1,0:T(8,128)S(1)}, u32[]{:S(2)}, u32[]{:S(2)}) collective-permute-start(f32[128,512]{1,0:T(8,128)S(1)} %get-tuple-element.20), channel_id=1, source_target_pairs={{0,16},{1,17},{2,18},{3,19},{4,20},{5,21},{6,22},{7,23},{8,24},{9,... | collective-permute-start | bytes 786440 | tf_op jit(solution)/shard_map/ppermute | solution.py:262
  61.3 9.4 %collective-permute-start.6 = (f32[64,512]{1,0:T(8,128)S(1)}, f32[64,512]{1,0:T(8,128)S(1)}, u32[]{:S(2)}, u32[]{:S(2)}) collective-permute-start(f32[64,512]{1,0:T(8,128)S(1)} %get-tuple-element.16), channel_id=1, source_target_pairs={{0,16},{1,17},{2,18},{3,19},{4,20},{5,21},{6,22},{7,23},{8,24},{9,... | collective-permute-start | bytes 393224 | tf_op jit(solution)/shard_map/ppermute | solution.py:262

commit v2 on v1

--- a/solution.py
+++ b/solution.py
@@ -1,3 +1,5 @@
+import functools
+
 import jax
 import jax.numpy as jnp
 from jax import lax
@@ -7,6 +9,7 @@
 
 AXES = ("layer", "row")
 VMEM = pl.BlockSpec(memory_space=pltpu.VMEM)
+HBM = pl.BlockSpec(memory_space=pl.ANY)
 
 
 def halves(v):
@@ -18,7 +21,15 @@
     return jnp.dot(a, b, preferred_element_type=jnp.float32)
 
 
-def precondition_kernel(query, left, right, out, turned, mixed):
+def precondition_kernel(query_hbm, left_hbm, right_hbm, out, query, left, right, turned, mixed, sems):
+    copies = [
+        pltpu.make_async_copy(src, dst, sems.at[n])
+        for n, (src, dst) in enumerate(((left_hbm, left), (right_hbm, right), (query_hbm, query)))
+    ]
+    for copy in copies:
+        copy.start()
+    copies[0].wait()
+    copies[1].wait()
     layers, rows, feat = query.shape
     proj = left.shape[1]
     half = proj // 2
@@ -30,6 +41,7 @@
     j = lax.broadcasted_iota(jnp.int32, (proj, proj), 1)
     pick = (j == 2 * lax.rem(i, half) + i // half).astype(jnp.bfloat16)
     pick_t = (i == 2 * lax.rem(j, half) + j // half).astype(jnp.bfloat16)
+    copies[2].wait()
     step = 8
     low = lax.rem(lax.broadcasted_iota(jnp.int32, (pairs, step * 128), 1), 128) < proj
     for l in range(layers):
@@ -60,59 +72,66 @@
     return pl.pallas_call(
         precondition_kernel,
         out_shape=jax.ShapeDtypeStruct(query.shape, jnp.bfloat16),
-        in_specs=[VMEM] * 3,
+        in_specs=[HBM] * 3,
         out_specs=VMEM,
-        scratch_shapes=[scratch, scratch],
+        scratch_shapes=[
+            pltpu.VMEM(query.shape, query.dtype),
+            pltpu.VMEM(left.shape, left.dtype),
+            pltpu.VMEM(right.shape, right.dtype),
+            scratch,
+            scratch,
+            pltpu.SemaphoreType.DMA((3,)),
+        ],
         compiler_params=pltpu.CompilerParams(vmem_limit_bytes=16 << 20),
         cost_estimate=pl.CostEstimate(flops=2 << 30, bytes_accessed=4 << 20, transcendentals=0),
         name="precondition",
-    )(query, left, right)
-
-
-def transpose_kernel(train, pass_in, out, pass_out, buffer, sems):
-    del pass_in, pass_out
+    )(*(pltpu.with_memory_space_constraint(v, pltpu.HBM) for v in (query, left, right)))
+
+
+def transpose_kernel(layer, train, out, buffer, sems):
+    feat = train.shape[2]
+    deep, rows, wide = buffer.shape
+    steps = feat // wide
+
+    def copy(n):
+        return pltpu.make_async_copy(train.at[layer, :, pl.ds(n * wide, wide)], buffer.at[n % deep], sems.at[n % deep])
+
+    for n in range(deep):
+        copy(n).start()
+    for n in range(steps):
+        copy(n).wait()
+        out[n * wide:(n + 1) * wide, :] = buffer[n % deep].T
+        if n + deep < steps:
+            copy(n + deep).start()
+
+
+def transpose(layer, train):
     layers, rows, feat = train.shape
-    wide = buffer.shape[2]
-    steps = [(l, k) for l in range(layers) for k in range(0, feat, wide)]
-    deep = buffer.shape[0]
-
-    def copy(n):
-        l, k = steps[n]
-        return pltpu.make_async_copy(train.at[l, :, pl.ds(k, wide)], buffer.at[n % deep], sems.at[n % deep])
-
-    for n in range(deep - 1):
-        copy(n).start()
-    for n, (l, k) in enumerate(steps):
-        if n + deep - 1 < len(steps):
-            copy(n + deep - 1).start()
-        copy(n).wait()
-        out[l, k:k + wide, :] = buffer[n % deep].T
-
-
-def transpose(train, passed):
-    layers, rows, feat = train.shape
-    wide, deep = 512, 4
-    hbm = pl.BlockSpec(memory_space=pl.ANY)
+    wide, deep = 512, 8
     return pl.pallas_call(
-        transpose_kernel,
-        out_shape=(jax.ShapeDtypeStruct((layers, feat, rows), train.dtype), jax.ShapeDtypeStruct(passed.shape, passed.dtype)),
-        in_specs=[hbm, hbm],
-        out_specs=(VMEM, hbm),
+        functools.partial(transpose_kernel, layer),
+        out_shape=pltpu.VMEM((feat, rows), train.dtype),
+        in_specs=[HBM],
+        out_specs=VMEM,
         scratch_shapes=[pltpu.VMEM((deep, rows, wide), train.dtype), pltpu.SemaphoreType.DMA((deep,))],
-        input_output_aliases={1: 1},
-        compiler_params=pltpu.CompilerParams(vmem_limit_bytes=24 << 20),
-        cost_estimate=pl.CostEstimate(flops=4 << 30, bytes_accessed=16 << 20, transcendentals=0),
-        name="transpose",
-    )(train, passed)
+        compiler_params=pltpu.CompilerParams(vmem_limit_bytes=16 << 20),
+        cost_estimate=pl.CostEstimate(flops=2 << 30, bytes_accessed=8 << 20, transcendentals=0),
+        name="transpose_%d" % layer,
+    )(pltpu.with_memory_space_constraint(train, pltpu.HBM))
 
 
 def score(turned, queries):
     total = None
-    for l in range(turned.shape[0]):
+    for l in range(len(turned)):
         rows = jnp.concatenate([q[l] for q in queries], axis=0)
-        term = dot(rows, turned[l])
+        term = dot(rows, turned[l][...])
         total = term if total is None else total + term
     return total
+
+
+def score_parts(turned, more, a, b, swapped, low, high):
+    second = [q.at[1:] for q in (a, b, swapped)]
+    return score((turned,), [a, b, swapped, low]) + score((more,), second + [high])
 
 
 def chip_at(offset):
@@ -150,44 +169,44 @@
         kept[...] = ahead[...]
 
 
-def plain_kernel(turned, *refs):
-    refs[-1][...] = score(turned, refs[:-1])
-
-
-def second_kernel(turned, *refs):
+def plain_kernel(turned, more, *refs):
+    refs[-1][...] = score((turned, more), refs[:-1])
+
+
+def second_kernel(turned, more, *refs):
     *queries, sent, kept, total = refs
     half = sent.shape[0]
-    total[...] = score(turned, queries)
+    total[...] = score_parts(turned, more, *queries)
     split(2, total.at[:half], total.at[half:], sent, kept)
 
 
-def third_kernel(turned, first, *refs):
+def third_kernel(turned, more, first, *refs):
     *queries, sent, kept, total = refs
     half = total.shape[0] // 2
-    total[...] = score(turned, queries)
+    total[...] = score_parts(turned, more, *queries)
     split(1, first.at[:half], total.at[half:], sent.at[:half], kept.at[:half])
     split(3, total.at[:half], first.at[half:], sent.at[half:], kept.at[half:])
 
 
-def fourth_kernel(turned, own, *refs):
-    *queries, sent, kept, total = refs
-    total[...] = score(turned, queries)
+def fourth_kernel(turned, more, own, *refs):
+    a, low0, low1, high0, high1, sent, kept, total = refs
+    total[...] = score((turned,), [a, low0, low1]) + score((more,), [a.at[1:], high0, high1])
     split(4, total, own, sent, kept)
 
 
 def block_call(kernel, name, rows, total, turned, operands):
-    columns = turned.shape[2]
+    columns = turned[0].shape[1]
     block = jax.ShapeDtypeStruct((rows, columns), jnp.float32)
     return pl.pallas_call(
         kernel,
         out_shape=(block, block) if total else block,
-        in_specs=[VMEM] * (1 + len(operands)),
+        in_specs=[VMEM] * (2 + len(operands)),
         out_specs=(VMEM, VMEM) if total else VMEM,
         scratch_shapes=[pltpu.VMEM((total, columns), jnp.float32)] if total else [],
         compiler_params=pltpu.CompilerParams(vmem_limit_bytes=24 << 20),
-        cost_estimate=pl.CostEstimate(flops=2 << 30, bytes_accessed=9 << 20, transcendentals=0),
+        cost_estimate=pl.CostEstimate(flops=1 << 10, bytes_accessed=1 << 10, transcendentals=0),
         name=name,
-    )(turned, *operands)
+    )(*turned, *operands)
 
 
 def gather_kernel(kept2, got2, kept13, got13, out):
@@ -231,7 +250,8 @@
     table = jax.ShapeDtypeStruct((rows, columns), jnp.float32)
     params = pltpu.CompilerParams(vmem_limit_bytes=8 << 20)
     most = pl.pallas_call(
-        gather_kernel, out_shape=table, in_specs=[VMEM] * 4, out_specs=VMEM, compiler_params=params, name="gather_rows"
+        gather_kernel, out_shape=table, in_specs=[VMEM] * 4, out_specs=VMEM, compiler_params=params, name="gather_rows",
+        cost_estimate=pl.CostEstimate(flops=60 << 30, bytes_accessed=1 << 20, transcendentals=0),
     )(kept2, got2, kept13, got13)
     return pl.pallas_call(
         last_kernel,
@@ -261,29 +281,34 @@
     around = [(flat(y, h, c), flat(y, step(h, c), c)) for y, h, c in every]
     send = lambda v, pairs: lax.ppermute(v, AXES, pairs)
 
+    after = lax.optimization_barrier
     mine = precondition(query_grads, left_inverse, right_inverse)
-    theirs = send(mine, swap)
-    held = [mine, theirs]
-    turned, theirs_after = transpose(train_grads, theirs)
-    held = [mine, theirs_after]
+    turned = [transpose(0, train_grads)]
+    a, b = [mine, send(mine, around)], [send(mine, swap)]
+    (b0, turned[0]) = after((b[0], turned[0]))
+    turned.append(transpose(1, train_grads))
+    b.append(send(b0, around))
     rows = 2 * mine.shape[1]
-    zeroth = block_call(plain_kernel, "scores_0", rows, 0, turned, held)
-    pairs = []
-    for k in range(1, 4):
-        held = [send(h, around) for h in held]
-        queries = held + [send(h, swap) for h in held]
-        if k == 1:
-            first = block_call(plain_kernel, "scores_1", 2 * rows, 0, turned, queries)
-            continue
-        if k == 2:
-            sent, kept = block_call(second_kernel, "scores_2", rows, 2 * rows, turned, queries)
-        else:
-            sent, kept = block_call(third_kernel, "scores_3", 2 * rows, 2 * rows, turned, [first] + queries)
-        pairs.append((kept, send(sent, across)))
-    end = send(held[0], around)
-    sent, kept = block_call(fourth_kernel, "scores_4", rows, rows, turned, [zeroth, end, send(end, swap)])
-    pairs.append((kept, send(sent, across)))
-    return finish(pairs, chips // groups * rows, turned.shape[2])
+    zeroth = block_call(plain_kernel, "scores_0", rows, 0, turned, [a[0], b0])
+    a.append(send(a[1], around))
+    b[1], zeroth = after((b[1], zeroth))
+    b.append(send(b[1], around))
+    first = block_call(plain_kernel, "scores_1", 2 * rows, 0, turned, [a[1], b[1], send(a[1], swap), send(b[1], swap)])
+    a.append(send(a[2], around))
+    b[2], first = after((b[2], first))
+    b.append(send(b[2], around))
+    sent2, kept2 = block_call(second_kernel, "scores_2", rows, 2 * rows, turned, [a[2], b[2], send(a[2], swap), *(send(b[2][l:l + 1], swap) for l in range(2))])
+    a[3], _ = after((a[3], sent2))
+    a.append(send(a[3], around))
+    got2 = send(sent2, across)
+    b[3], _ = after((b[3], got2))
+    sent3, kept3 = block_call(third_kernel, "scores_3", 2 * rows, 2 * rows, turned, [first, a[3], b[3], send(a[3], swap), *(send(b[3][l:l + 1], swap) for l in range(2))])
+    a[4], _ = after((a[4], sent3))
+    got3 = send(sent3, across)
+    ends = [a[4], *(send(a[4][l:l + 1, 16 * n:16 * n + 16], swap) for l in range(2) for n in range(2))]
+    sent4, kept4 = block_call(fourth_kernel, "scores_4", rows, rows, turned, [zeroth, *ends])
+    pairs = [(kept2, got2), (kept3, got3), (kept4, send(sent4, across))]
+    return finish(pairs, chips // groups * rows, turned[0].shape[1])
 
 
 def on_device(query_grads, train_grads, left_inverse, right_inverse):

time: 71.7 us -> 58.5 us (0.82)
  waiting for transfers between devices: 30.5 us -> 18 us
  local copies, waits for them, and re-layouts: 6.1 us -> 0.1 us
  starting transfers between devices: 19.1 us -> 22.4 us
  Pallas kernels: 15.6 us -> 17.7 us
    ppermute x18 -> x23, waiting for transfers between devices: 30.5 us -> 18 us  [ring_device(): send = lambda v, pairs: lax.ppermute(v, AXES, pairs)]
    unnamed x8 -> x0, local copies, waits for them, and re-layouts: 6.1 us -> none
    ppermute x18 -> x23, starting transfers between devices: 19.1 us -> 22.4 us  [ring_device(): send = lambda v, pairs: lax.ppermute(v, AXES, pairs)]
    pallas_call x1, Pallas kernels: 2.72 us -> 3.88 us  [precondition(): pl.pallas_call(precondition_kernel, out_shape=jax.ShapeDtypeStruct(query....]
    pallas_call x1 -> x2, Pallas kernels: 4.38 us -> 5.27 us  [transpose(): pl.pallas_call(functools.partial(transpose_kernel, layer), out_shape=pltp...]
  transfers between devices with their start and end apart: 18 -> 23, of which waited for: 8 -> 16; matrix products, arithmetic and copies ran while one was open for 0% -> 0% of each run, Pallas kernels for 17% -> 23%
where the time goes in v2:
time: 58.5 us; the launch traced here: 58.3 us
  starting transfers between devices  22.4 us (38%)
  waiting for transfers between devices  18 us (31%)
  Pallas kernels  17.7 us (30%)
    ppermute x23, starting transfers between devices, ring_device(): send = lambda v, pairs: lax.ppermute(v, AXES, pairs)  22.4 us
    ppermute x23, waiting for transfers between devices, ring_device(): send = lambda v, pairs: lax.ppermute(v, AXES, pairs)  18 us
    pallas_call x5, Pallas kernels, block_call(): pl.pallas_call(kernel, out_shape=(block, block) if total else block, in_s...  6.94 us
    pallas_call x2, Pallas kernels, transpose(): pl.pallas_call(functools.partial(transpose_kernel, layer), out_shape=pltp...  5.27 us
    pallas_call x1, Pallas kernels, precondition(): pl.pallas_call(precondition_kernel, out_shape=jax.ShapeDtypeStruct(query....  3.88 us
  transfers between devices with their start and end apart: 23, of which 16 were waited for; matrix products, arithmetic and copies ran while one was open for 0% of the time, Pallas kernels for 23%

profile of v2, /device:TPU:0, one launch (start us, length us, event | category | flops | bytes accessed | tf_op | source)
XLA Modules:
  0.0 58.3 jit_solution(3760880928749094920)
XLA Ops:
  0.0 3.9 %precondition.1.refs_0_ = bf16[2,32,4096]{2,1,0:T(8,128)(2,1)S(1)} custom-call(bf16[2,32,4096]{2,1,0:T(8,128)(2,1)} %query_hbm.1, f32[2,64,64]{2,1,0:T(8,128)} %left_hbm.1, f32[2,64,64]{2,1,0:T(8,128)} %right_hbm.1), custom_call_target="tpu_custom_call" | custom-call | flops 2147483648 | bytes 4194304 | tf_op jit(solution)/shard_map/precondition/pallas_call | solution.py:72
  4.4 2.6 %collective-permute-start.2 = (bf16[2,32,4096]{2,1,0:T(8,128)(2,1)S(1)}, bf16[2,32,4096]{2,1,0:T(8,128)(2,1)S(1)}, u32[]{:S(2)}, u32[]{:S(2)}) collective-permute-start(bf16[2,32,4096]{2,1,0:T(8,128)(2,1)S(1)} %precondition.1.refs_0_), channel_id=1, source_target_pairs={{0,4},{1,3},{2,0},{3,7},{4,8},{5,1},{6,2},{7,11},{8,12},{9,5},{10,... | collective-permute-start | bytes 1572872 | tf_op jit(solution)/shard_map/ppermute | solution.py:282
  7.0 2.6 %transpose_0.1.turned = bf16[4096,512]{1,0:T(8,128)(2,1)S(1)} custom-call(bf16[2,512,4096]{2,1,0:T(8,128)(2,1)} %train.3), custom_call_target="tpu_custom_call" | custom-call | flops 2147483648 | bytes 8388608 | tf_op jit(solution)/shard_map/transpose_0/pallas_call | solution.py:111
  9.7 1.6 %collective-permute-start.1 = (bf16[2,32,4096]{2,1,0:T(8,128)(2,1)S(1)}, bf16[2,32,4096]{2,1,0:T(8,128)(2,1)S(1)}, u32[]{:S(2)}, u32[]{:S(2)}) collective-permute-start(bf16[2,32,4096]{2,1,0:T(8,128)(2,1)S(1)} %collective-permute-done.refs_1_), channel_id=1, source_target_pairs={{0,4},{1,3},{2,0},{3,7},{4,8},{5,1},{6,2},{7,11},{8,12},{9,5},{10,... | collective-permute-start | bytes 1572872 | tf_op jit(solution)/shard_map/ppermute | solution.py:282
  11.3 2.6 %transpose_1.1.more = bf16[4096,512]{1,0:T(8,128)(2,1)S(1)} custom-call(bf16[2,512,4096]{2,1,0:T(8,128)(2,1)} %train.3), custom_call_target="tpu_custom_call" | custom-call | flops 2147483648 | bytes 8388608 | tf_op jit(solution)/shard_map/transpose_1/pallas_call | solution.py:111
  14.0 1.5 %scores_0.1.own = f32[64,512]{1,0:T(8,128)S(1)} custom-call(bf16[4096,512]{1,0:T(8,128)(2,1)S(1)} %transpose_0.1.turned, bf16[4096,512]{1,0:T(8,128)(2,1)S(1)} %transpose_1.1.more, bf16[2,32,4096]{2,1,0:T(8,128)(2,1)S(1)} %precondition.1.refs_0_, bf16[2,32,4096]{2,1,0:T(8,128)(2,1)S(1)} %collective-permute-done.refs_1_), custom_call_target="tpu_custom_call" | custom-call | flops 1024 | bytes 1024 | tf_op jit(solution)/shard_map/scores_0/pallas_call | solution.py:200
  15.6 1.6 %collective-permute-start.3 = (bf16[2,32,4096]{2,1,0:T(8,128)(2,1)S(1)}, bf16[2,32,4096]{2,1,0:T(8,128)(2,1)S(1)}, u32[]{:S(2)}, u32[]{:S(2)}) collective-permute-start(bf16[2,32,4096]{2,1,0:T(8,128)(2,1)S(1)} %collective-permute-done.2.refs_0_), channel_id=1, source_target_pairs={{0,4},{1,3},{2,0},{3,7},{4,8},{5,1},{6,2},{7,11},{8,12},{9,5},{10,... | collective-permute-start | bytes 1572872 | tf_op jit(solution)/shard_map/ppermute | solution.py:282
  17.2 2.5 %collective-permute-done.1.refs_1_ = bf16[2,32,4096]{2,1,0:T(8,128)(2,1)S(1)} collective-permute-done((bf16[2,32,4096]{2,1,0:T(8,128)(2,1)S(1)}, bf16[2,32,4096]{2,1,0:T(8,128)(2,1)S(1)}, u32[]{:S(2)}, u32[]{:S(2)}) %collective-permute-start.1) | collective-permute-done | bytes 524320 | tf_op jit(solution)/shard_map/ppermute | solution.py:282
  19.7 2.1 %collective-permute-start.5 = (bf16[2,32,4096]{2,1,0:T(8,128)(2,1)S(1)}, bf16[2,32,4096]{2,1,0:T(8,128)(2,1)S(1)}, u32[]{:S(2)}, u32[]{:S(2)}) collective-permute-start(bf16[2,32,4096]{2,1,0:T(8,128)(2,1)S(1)} %collective-permute-done.1.refs_1_), channel_id=1, source_target_pairs={{0,4},{1,3},{2,0},{3,7},{4,8},{5,1},{6,2},{7,11},{8,12},{9,5},{10,... | collective-permute-start | bytes 1572872 | tf_op jit(solution)/shard_map/ppermute | solution.py:282
  21.8 3.5 %collective-permute-done.3.refs_0_ = bf16[2,32,4096]{2,1,0:T(8,128)(2,1)S(1)} collective-permute-done((bf16[2,32,4096]{2,1,0:T(8,128)(2,1)S(1)}, bf16[2,32,4096]{2,1,0:T(8,128)(2,1)S(1)}, u32[]{:S(2)}, u32[]{:S(2)}) %collective-permute-start.3) | collective-permute-done | bytes 524320 | tf_op jit(solution)/shard_map/ppermute | solution.py:282
  25.4 2.1 %collective-permute-start.4 = (bf16[2,32,4096]{2,1,0:T(8,128)(2,1)S(1)}, bf16[2,32,4096]{2,1,0:T(8,128)(2,1)S(1)}, u32[]{:S(2)}, u32[]{:S(2)}) collective-permute-start(bf16[2,32,4096]{2,1,0:T(8,128)(2,1)S(1)} %collective-permute-done.3.refs_0_), channel_id=1, source_target_pairs={{0,4},{1,3},{2,0},{3,7},{4,8},{5,1},{6,2},{7,11},{8,12},{9,5},{10,... | collective-permute-start | bytes 1572872 | tf_op jit(solution)/shard_map/ppermute | solution.py:282
  27.5 1.2 %scores_1.1.first = f32[128,512]{1,0:T(8,128)S(1)} custom-call(bf16[4096,512]{1,0:T(8,128)(2,1)S(1)} %transpose_0.1.turned, bf16[4096,512]{1,0:T(8,128)(2,1)S(1)} %transpose_1.1.more, bf16[2,32,4096]{2,1,0:T(8,128)(2,1)S(1)} %collective-permute-done.2.refs_0_, bf16[2,32,4096]{2,1,0:T(8,128)(2,1)S(1)} %collective-permute-done.1.refs_1_, ...), custom_call_target="tpu_custom_call" | custom-call | flops 1024 | bytes 1024 | tf_op jit(solution)/shard_map/scores_1/pallas_call | solution.py:200
  28.7 2.2 %collective-permute-done.5.refs_1_ = bf16[2,32,4096]{2,1,0:T(8,128)(2,1)S(1)} collective-permute-done((bf16[2,32,4096]{2,1,0:T(8,128)(2,1)S(1)}, bf16[2,32,4096]{2,1,0:T(8,128)(2,1)S(1)}, u32[]{:S(2)}, u32[]{:S(2)}) %collective-permute-start.5) | collective-permute-done | bytes 524320 | tf_op jit(solution)/shard_map/ppermute | solution.py:282
  31.0 2.1 %collective-permute-start.12 = (bf16[2,32,4096]{2,1,0:T(8,128)(2,1)S(1)}, bf16[2,32,4096]{2,1,0:T(8,128)(2,1)S(1)}, u32[]{:S(2)}, u32[]{:S(2)}) collective-permute-start(bf16[2,32,4096]{2,1,0:T(8,128)(2,1)S(1)} %collective-permute-done.5.refs_1_), channel_id=1, source_target_pairs={{0,4},{1,3},{2,0},{3,7},{4,8},{5,1},{6,2},{7,11},{8,12},{9,5},{10,... | collective-permute-start | bytes 1572872 | tf_op jit(solution)/shard_map/ppermute | solution.py:282
  35.1 1.3 %scores_2.1 = (f32[64,512]{1,0:T(8,128)S(1)}, f32[64,512]{1,0:T(8,128)S(1)}) custom-call(bf16[4096,512]{1,0:T(8,128)(2,1)S(1)} %transpose_0.1.turned, bf16[4096,512]{1,0:T(8,128)(2,1)S(1)} %transpose_1.1.more, bf16[2,32,4096]{2,1,0:T(8,128)(2,1)S(1)} %collective-permute-done.3.refs_0_, bf16[2,32,4096]{2,1,0:T(8,128)(2,1)S(1)} %collective-permute-done.5.refs_1_, ...), custom_call_target="tpu_custom_call" | custom-call | flops 1024 | bytes 1024 | tf_op jit(solution)/shard_map/scores_2/pallas_call | solution.py:200
  36.4 1.6 %collective-permute-start.13 = (f32[64,512]{1,0:T(8,128)S(1)}, f32[64,512]{1,0:T(8,128)S(1)}, u32[]{:S(2)}, u32[]{:S(2)}) collective-permute-start(f32[64,512]{1,0:T(8,128)S(1)} %get-tuple-element.25), channel_id=1, source_target_pairs={{0,16},{1,17},{2,18},{3,19},{4,20},{5,21},{6,22},{7,23},{8,24},{9,... | collective-permute-start | bytes 393224 | tf_op jit(solution)/shard_map/ppermute | solution.py:282
  38.0 1.6 %collective-permute-start.11 = (bf16[2,32,4096]{2,1,0:T(8,128)(2,1)S(1)}, bf16[2,32,4096]{2,1,0:T(8,128)(2,1)S(1)}, u32[]{:S(2)}, u32[]{:S(2)}) collective-permute-start(bf16[2,32,4096]{2,1,0:T(8,128)(2,1)S(1)} %collective-permute-done.4.refs_0_), channel_id=1, source_target_pairs={{0,4},{1,3},{2,0},{3,7},{4,8},{5,1},{6,2},{7,11},{8,12},{9,5},{10,... | collective-permute-start | bytes 1572872 | tf_op jit(solution)/shard_map/ppermute | solution.py:282
  39.5 2.4 %collective-permute-done.13.got2 = f32[64,512]{1,0:T(8,128)S(1)} collective-permute-done((f32[64,512]{1,0:T(8,128)S(1)}, f32[64,512]{1,0:T(8,128)S(1)}, u32[]{:S(2)}, u32[]{:S(2)}) %collective-permute-start.13) | collective-permute-done | bytes 131104 | tf_op jit(solution)/shard_map/ppermute | solution.py:282
  42.8 1.0 %collective-permute-done.15.refs_3_ = bf16[1,32,4096]{2,1,0:T(8,128)(2,1)S(1)} collective-permute-done((bf16[1,32,4096]{2,1,0:T(8,128)(2,1)S(1)}, bf16[1,32,4096]{2,1,0:T(8,128)(2,1)S(1)}, u32[]{:S(2)}, u32[]{:S(2)}) %collective-permute-start.15) | collective-permute-done | bytes 262176 | tf_op jit(solution)/shard_map/ppermute | solution.py:282
  44.2 1.3 %scores_3.1 = (f32[128,512]{1,0:T(8,128)S(1)}, f32[128,512]{1,0:T(8,128)S(1)}) custom-call(bf16[4096,512]{1,0:T(8,128)(2,1)S(1)} %transpose_0.1.turned, bf16[4096,512]{1,0:T(8,128)(2,1)S(1)} %transpose_1.1.more, f32[128,512]{1,0:T(8,128)S(1)} %scores_1.1.first, bf16[2,32,4096]{2,1,0:T(8,128)(2,1)S(1)} %collective-permute-done.4.refs_0_, ...), custom_call_target="tpu_custom_call" | custom-call | flops 1024 | bytes 1024 | tf_op jit(solution)/shard_map/scores_3/pallas_call | solution.py:200
  45.5 2.1 %collective-permute-start.22 = (f32[128,512]{1,0:T(8,128)S(1)}, f32[128,512]{1,0:T(8,128)S(1)}, u32[]{:S(2)}, u32[]{:S(2)}) collective-permute-start(f32[128,512]{1,0:T(8,128)S(1)} %get-tuple-element.29), channel_id=1, source_target_pairs={{0,16},{1,17},{2,18},{3,19},{4,20},{5,21},{6,22},{7,23},{8,24},{9,... | collective-permute-start | bytes 786440 | tf_op jit(solution)/shard_map/ppermute | solution.py:282
  50.0 1.6 %scores_4.1 = (f32[64,512]{1,0:T(8,128)S(1)}, f32[64,512]{1,0:T(8,128)S(1)}) custom-call(bf16[4096,512]{1,0:T(8,128)(2,1)S(1)} %transpose_0.1.turned, bf16[4096,512]{1,0:T(8,128)(2,1)S(1)} %transpose_1.1.more, f32[64,512]{1,0:T(8,128)S(1)} %scores_0.1.own, bf16[2,32,4096]{2,1,0:T(8,128)(2,1)S(1)} %collective-permute-done.11.refs_0_, ...), custom_call_target="tpu_custom_call" | custom-call | flops 1024 | bytes 1024 | tf_op jit(solution)/shard_map/scores_4/pallas_call | solution.py:200
  51.6 2.1 %collective-permute-start.21 = (f32[64,512]{1,0:T(8,128)S(1)}, f32[64,512]{1,0:T(8,128)S(1)}, u32[]{:S(2)}, u32[]{:S(2)}) collective-permute-start(f32[64,512]{1,0:T(8,128)S(1)} %get-tuple-element.32), channel_id=1, source_target_pairs={{0,16},{1,17},{2,18},{3,19},{4,20},{5,21},{6,22},{7,23},{8,24},{9,... | collective-permute-start | bytes 393224 | tf_op jit(solution)/shard_map/ppermute | solution.py:282
  55.2 2.5 %collective-permute-done.21.got = f32[64,512]{1,0:T(8,128)S(1)} collective-permute-done((f32[64,512]{1,0:T(8,128)S(1)}, f32[64,512]{1,0:T(8,128)S(1)}, u32[]{:S(2)}, u32[]{:S(2)}) %collective-permute-start.21) | collective-permute-done | bytes 131104 | tf_op jit(solution)/shard_map/ppermute | solution.py:282
  (35 shorter events, 8.3 us)
Async XLA Ops:
  3.9 5.8 %collective-permute-start = (bf16[2,32,4096]{2,1,0:T(8,128)(2,1)S(1)}, bf16[2,32,4096]{2,1,0:T(8,128)(2,1)S(1)}, u32[]{:S(2)}, u32[]{:S(2)}) collective-permute-start(bf16[2,32,4096]{2,1,0:T(8,128)(2,1)S(1)} %precondition.1.refs_0_), channel_id=1, source_target_pairs={{0,1},{1,0},{2,3},{3,2},{4,5},{5,4},{6,7},{7,6},{8,9},{9,8},{10,11... | collective-permute-start | bytes 1572872 | tf_op jit(solution)/shard_map/ppermute | solution.py:282
  4.4 11.1 %collective-permute-start.2 = (bf16[2,32,4096]{2,1,0:T(8,128)(2,1)S(1)}, bf16[2,32,4096]{2,1,0:T(8,128)(2,1)S(1)}, u32[]{:S(2)}, u32[]{:S(2)}) collective-permute-start(bf16[2,32,4096]{2,1,0:T(8,128)(2,1)S(1)} %precondition.1.refs_0_), channel_id=1, source_target_pairs={{0,4},{1,3},{2,0},{3,7},{4,8},{5,1},{6,2},{7,11},{8,12},{9,5},{10,... | collective-permute-start | bytes 1572872 | tf_op jit(solution)/shard_map/ppermute | solution.py:282
  9.7 10.0 %collective-permute-start.1 = (bf16[2,32,4096]{2,1,0:T(8,128)(2,1)S(1)}, bf16[2,32,4096]{2,1,0:T(8,128)(2,1)S(1)}, u32[]{:S(2)}, u32[]{:S(2)}) collective-permute-start(bf16[2,32,4096]{2,1,0:T(8,128)(2,1)S(1)} %collective-permute-done.refs_1_), channel_id=1, source_target_pairs={{0,4},{1,3},{2,0},{3,7},{4,8},{5,1},{6,2},{7,11},{8,12},{9,5},{10,... | collective-permute-start | bytes 1572872 | tf_op jit(solution)/shard_map/ppermute | solution.py:282
  15.5 11.9 %collective-permute-start.6 = (bf16[2,32,4096]{2,1,0:T(8,128)(2,1)S(1)}, bf16[2,32,4096]{2,1,0:T(8,128)(2,1)S(1)}, u32[]{:S(2)}, u32[]{:S(2)}) collective-permute-start(bf16[2,32,4096]{2,1,0:T(8,128)(2,1)S(1)} %collective-permute-done.2.refs_0_), channel_id=1, source_target_pairs={{0,1},{1,0},{2,3},{3,2},{4,5},{5,4},{6,7},{7,6},{8,9},{9,8},{10,11... | collective-permute-start | bytes 1572872 | tf_op jit(solution)/shard_map/ppermute | solution.py:282
  15.6 9.7 %collective-permute-start.3 = (bf16[2,32,4096]{2,1,0:T(8,128)(2,1)S(1)}, bf16[2,32,4096]{2,1,0:T(8,128)(2,1)S(1)}, u32[]{:S(2)}, u32[]{:S(2)}) collective-permute-start(bf16[2,32,4096]{2,1,0:T(8,128)(2,1)S(1)} %collective-permute-done.2.refs_0_), channel_id=1, source_target_pairs={{0,4},{1,3},{2,0},{3,7},{4,8},{5,1},{6,2},{7,11},{8,12},{9,5},{10,... | collective-permute-start | bytes 1572872 | tf_op jit(solution)/shard_map/ppermute | solution.py:282
  19.7 7.7 %collective-permute-start.7 = (bf16[2,32,4096]{2,1,0:T(8,128)(2,1)S(1)}, bf16[2,32,4096]{2,1,0:T(8,128)(2,1)S(1)}, u32[]{:S(2)}, u32[]{:S(2)}) collective-permute-start(bf16[2,32,4096]{2,1,0:T(8,128)(2,1)S(1)} %collective-permute-done.1.refs_1_), channel_id=1, source_target_pairs={{0,1},{1,0},{2,3},{3,2},{4,5},{5,4},{6,7},{7,6},{8,9},{9,8},{10,11... | collective-permute-start | bytes 1572872 | tf_op jit(solution)/shard_map/ppermute | solution.py:282
  19.7 11.2 %collective-permute-start.5 = (bf16[2,32,4096]{2,1,0:T(8,128)(2,1)S(1)}, bf16[2,32,4096]{2,1,0:T(8,128)(2,1)S(1)}, u32[]{:S(2)}, u32[]{:S(2)}) collective-permute-start(bf16[2,32,4096]{2,1,0:T(8,128)(2,1)S(1)} %collective-permute-done.1.refs_1_), channel_id=1, source_target_pairs={{0,4},{1,3},{2,0},{3,7},{4,8},{5,1},{6,2},{7,11},{8,12},{9,5},{10,... | collective-permute-start | bytes 1572872 | tf_op jit(solution)/shard_map/ppermute | solution.py:282
  25.4 8.3 %collective-permute-start.8 = (bf16[2,32,4096]{2,1,0:T(8,128)(2,1)S(1)}, bf16[2,32,4096]{2,1,0:T(8,128)(2,1)S(1)}, u32[]{:S(2)}, u32[]{:S(2)}) collective-permute-start(bf16[2,32,4096]{2,1,0:T(8,128)(2,1)S(1)} %collective-permute-done.3.refs_0_), channel_id=1, source_target_pairs={{0,1},{1,0},{2,3},{3,2},{4,5},{5,4},{6,7},{7,6},{8,9},{9,8},{10,11... | collective-permute-start | bytes 1572872 | tf_op jit(solution)/shard_map/ppermute | solution.py:282
  25.4 12.6 %collective-permute-start.4 = (bf16[2,32,4096]{2,1,0:T(8,128)(2,1)S(1)}, bf16[2,32,4096]{2,1,0:T(8,128)(2,1)S(1)}, u32[]{:S(2)}, u32[]{:S(2)}) collective-permute-start(bf16[2,32,4096]{2,1,0:T(8,128)(2,1)S(1)} %collective-permute-done.3.refs_0_), channel_id=1, source_target_pairs={{0,4},{1,3},{2,0},{3,7},{4,8},{5,1},{6,2},{7,11},{8,12},{9,5},{10,... | collective-permute-start | bytes 1572872 | tf_op jit(solution)/shard_map/ppermute | solution.py:282
  31.0 11.2 %collective-permute-start.12 = (bf16[2,32,4096]{2,1,0:T(8,128)(2,1)S(1)}, bf16[2,32,4096]{2,1,0:T(8,128)(2,1)S(1)}, u32[]{:S(2)}, u32[]{:S(2)}) collective-permute-start(bf16[2,32,4096]{2,1,0:T(8,128)(2,1)S(1)} %collective-permute-done.5.refs_1_), channel_id=1, source_target_pairs={{0,4},{1,3},{2,0},{3,7},{4,8},{5,1},{6,2},{7,11},{8,12},{9,5},{10,... | collective-permute-start | bytes 1572872 | tf_op jit(solution)/shard_map/ppermute | solution.py:282
  33.1 1.6 %collective-permute-start.10 = (bf16[1,32,4096]{2,1,0:T(8,128)(2,1)S(1)}, bf16[1,32,4096]{2,1,0:T(8,128)(2,1)S(1)}, u32[]{:S(2)}, u32[]{:S(2)}) collective-permute-start(bf16[1,32,4096]{2,1,0:T(8,128)(2,1)S(1)} %get-tuple-element.41), channel_id=1, source_target_pairs={{0,1},{1,0},{2,3},{3,2},{4,5},{5,4},{6,7},{7,6},{8,9},{9,8},{10,11... | collective-permute-start | bytes 786440 | tf_op jit(solution)/shard_map/ppermute | solution.py:282
  33.2 1.9 %collective-permute-start.9 = (bf16[1,32,4096]{2,1,0:T(8,128)(2,1)S(1)}, bf16[1,32,4096]{2,1,0:T(8,128)(2,1)S(1)}, u32[]{:S(2)}, u32[]{:S(2)}) collective-permute-start(bf16[1,32,4096]{2,1,0:T(8,128)(2,1)S(1)} %get-tuple-element.42), channel_id=1, source_target_pairs={{0,1},{1,0},{2,3},{3,2},{4,5},{5,4},{6,7},{7,6},{8,9},{9,8},{10,11... | collective-permute-start | bytes 786440 | tf_op jit(solution)/shard_map/ppermute | solution.py:282
  36.4 5.6 %collective-permute-start.13 = (f32[64,512]{1,0:T(8,128)S(1)}, f32[64,512]{1,0:T(8,128)S(1)}, u32[]{:S(2)}, u32[]{:S(2)}) collective-permute-start(f32[64,512]{1,0:T(8,128)S(1)} %get-tuple-element.25), channel_id=1, source_target_pairs={{0,16},{1,17},{2,18},{3,19},{4,20},{5,21},{6,22},{7,23},{8,24},{9,... | collective-permute-start | bytes 393224 | tf_op jit(solution)/shard_map/ppermute | solution.py:282
  38.0 6.3 %collective-permute-start.14 = (bf16[2,32,4096]{2,1,0:T(8,128)(2,1)S(1)}, bf16[2,32,4096]{2,1,0:T(8,128)(2,1)S(1)}, u32[]{:S(2)}, u32[]{:S(2)}) collective-permute-start(bf16[2,32,4096]{2,1,0:T(8,128)(2,1)S(1)} %collective-permute-done.4.refs_0_), channel_id=1, source_target_pairs={{0,1},{1,0},{2,3},{3,2},{4,5},{5,4},{6,7},{7,6},{8,9},{9,8},{10,11... | collective-permute-start | bytes 1572872 | tf_op jit(solution)/shard_map/ppermute | solution.py:282
  38.0 9.9 %collective-permute-start.11 = (bf16[2,32,4096]{2,1,0:T(8,128)(2,1)S(1)}, bf16[2,32,4096]{2,1,0:T(8,128)(2,1)S(1)}, u32[]{:S(2)}, u32[]{:S(2)}) collective-permute-start(bf16[2,32,4096]{2,1,0:T(8,128)(2,1)S(1)} %collective-permute-done.4.refs_0_), channel_id=1, source_target_pairs={{0,4},{1,3},{2,0},{3,7},{4,8},{5,1},{6,2},{7,11},{8,12},{9,5},{10,... | collective-permute-start | bytes 1572872 | tf_op jit(solution)/shard_map/ppermute | solution.py:282
  42.2 1.6 %collective-permute-start.15 = (bf16[1,32,4096]{2,1,0:T(8,128)(2,1)S(1)}, bf16[1,32,4096]{2,1,0:T(8,128)(2,1)S(1)}, u32[]{:S(2)}, u32[]{:S(2)}) collective-permute-start(bf16[1,32,4096]{2,1,0:T(8,128)(2,1)S(1)} %get-tuple-element.40), channel_id=1, source_target_pairs={{0,1},{1,0},{2,3},{3,2},{4,5},{5,4},{6,7},{7,6},{8,9},{9,8},{10,11... | collective-permute-start | bytes 786440 | tf_op jit(solution)/shard_map/ppermute | solution.py:282
  42.3 1.9 %collective-permute-start.16 = (bf16[1,32,4096]{2,1,0:T(8,128)(2,1)S(1)}, bf16[1,32,4096]{2,1,0:T(8,128)(2,1)S(1)}, u32[]{:S(2)}, u32[]{:S(2)}) collective-permute-start(bf16[1,32,4096]{2,1,0:T(8,128)(2,1)S(1)} %get-tuple-element.39), channel_id=1, source_target_pairs={{0,1},{1,0},{2,3},{3,2},{4,5},{5,4},{6,7},{7,6},{8,9},{9,8},{10,11... | collective-permute-start | bytes 786440 | tf_op jit(solution)/shard_map/ppermute | solution.py:282
  45.5 8.7 %collective-permute-start.22 = (f32[128,512]{1,0:T(8,128)S(1)}, f32[128,512]{1,0:T(8,128)S(1)}, u32[]{:S(2)}, u32[]{:S(2)}) collective-permute-start(f32[128,512]{1,0:T(8,128)S(1)} %get-tuple-element.29), channel_id=1, source_target_pairs={{0,16},{1,17},{2,18},{3,19},{4,20},{5,21},{6,22},{7,23},{8,24},{9,... | collective-permute-start | bytes 786440 | tf_op jit(solution)/shard_map/ppermute | solution.py:282
  47.9 1.4 %collective-permute-start.17 = (bf16[1,16,4096]{2,1,0:T(8,128)(2,1)S(1)}, bf16[1,16,4096]{2,1,0:T(8,128)(2,1)S(1)}, u32[]{:S(2)}, u32[]{:S(2)}) collective-permute-start(bf16[1,16,4096]{2,1,0:T(8,128)(2,1)S(1)} %get-tuple-element.38), channel_id=1, source_target_pairs={{0,1},{1,0},{2,3},{3,2},{4,5},{5,4},{6,7},{7,6},{8,9},{9,8},{10,11... | collective-permute-start | bytes 393224 | tf_op jit(solution)/shard_map/ppermute | solution.py:282
  47.9 1.5 %collective-permute-start.18 = (bf16[1,16,4096]{2,1,0:T(8,128)(2,1)S(1)}, bf16[1,16,4096]{2,1,0:T(8,128)(2,1)S(1)}, u32[]{:S(2)}, u32[]{:S(2)}) collective-permute-start(bf16[1,16,4096]{2,1,0:T(8,128)(2,1)S(1)} %get-tuple-element.37), channel_id=1, source_target_pairs={{0,1},{1,0},{2,3},{3,2},{4,5},{5,4},{6,7},{7,6},{8,9},{9,8},{10,11... | collective-permute-start | bytes 393224 | tf_op jit(solution)/shard_map/ppermute | solution.py:282
  48.4 1.3 %collective-permute-start.19 = (bf16[1,16,4096]{2,1,0:T(8,128)(2,1)S(1)}, bf16[1,16,4096]{2,1,0:T(8,128)(2,1)S(1)}, u32[]{:S(2)}, u32[]{:S(2)}) collective-permute-start(bf16[1,16,4096]{2,1,0:T(8,128)(2,1)S(1)} %get-tuple-element.36), channel_id=1, source_target_pairs={{0,1},{1,0},{2,3},{3,2},{4,5},{5,4},{6,7},{7,6},{8,9},{9,8},{10,11... | collective-permute-start | bytes 393224 | tf_op jit(solution)/shard_map/ppermute | solution.py:282
  48.5 1.5 %collective-permute-start.20 = (bf16[1,16,4096]{2,1,0:T(8,128)(2,1)S(1)}, bf16[1,16,4096]{2,1,0:T(8,128)(2,1)S(1)}, u32[]{:S(2)}, u32[]{:S(2)}) collective-permute-start(bf16[1,16,4096]{2,1,0:T(8,128)(2,1)S(1)} %get-tuple-element.35), channel_id=1, source_target_pairs={{0,1},{1,0},{2,3},{3,2},{4,5},{5,4},{6,7},{7,6},{8,9},{9,8},{10,11... | collective-permute-start | bytes 393224 | tf_op jit(solution)/shard_map/ppermute | solution.py:282
  51.6 6.1 %collective-permute-start.21 = (f32[64,512]{1,0:T(8,128)S(1)}, f32[64,512]{1,0:T(8,128)S(1)}, u32[]{:S(2)}, u32[]{:S(2)}) collective-permute-start(f32[64,512]{1,0:T(8,128)S(1)} %get-tuple-element.32), channel_id=1, source_target_pairs={{0,16},{1,17},{2,18},{3,19},{4,20},{5,21},{6,22},{7,23},{8,24},{9,... | collective-permute-start | bytes 393224 | tf_op jit(solution)/shard_map/ppermute | solution.py:282

commit v3 on v2

--- a/solution.py
+++ b/solution.py
@@ -21,7 +21,8 @@
     return jnp.dot(a, b, preferred_element_type=jnp.float32)
 
 
-def precondition_kernel(query_hbm, left_hbm, right_hbm, out, query, left, right, turned, mixed, sems):
+def precondition_first_kernel(query_hbm, left_hbm, right_hbm, out, query, left, right, *refs):
+    *scratch, sems = refs
     copies = [
         pltpu.make_async_copy(src, dst, sems.at[n])
         for n, (src, dst) in enumerate(((left_hbm, left), (right_hbm, right), (query_hbm, query)))
@@ -30,62 +31,72 @@
         copy.start()
     copies[0].wait()
     copies[1].wait()
+    precondition_kernel(query, left, right, out, *scratch, arrived=copies[2].wait)
+
+
+def precondition_kernel(query, left, right, out, turned, mixed, arrived=lambda: None):
     layers, rows, feat = query.shape
     proj = left.shape[1]
-    half = proj // 2
-    pairs = feat // 128
-    i = lax.broadcasted_iota(jnp.int32, (2 * proj, 2 * proj), 0) // proj
-    j = lax.broadcasted_iota(jnp.int32, (2 * proj, 2 * proj), 1) // proj
-    diagonal = i == j
+    half, pairs, stride = proj // 2, feat // 128, mixed.shape[1] // (feat // 128)
+    i = lax.broadcasted_iota(jnp.int32, (2 * proj, 4 * proj), 0) // proj
+    j = lax.broadcasted_iota(jnp.int32, (2 * proj, 4 * proj), 1) // (2 * proj)
+    same = i == j
     i = lax.broadcasted_iota(jnp.int32, (proj, proj), 0)
     j = lax.broadcasted_iota(jnp.int32, (proj, proj), 1)
     pick = (j == 2 * lax.rem(i, half) + i // half).astype(jnp.bfloat16)
     pick_t = (i == 2 * lax.rem(j, half) + j // half).astype(jnp.bfloat16)
-    copies[2].wait()
-    step = 8
-    low = lax.rem(lax.broadcasted_iota(jnp.int32, (pairs, step * 128), 1), 128) < proj
+    rights, lefts = [], []
     for l in range(layers):
         wide = jnp.concatenate([right[l], right[l]], axis=1)
-        wide = jnp.where(diagonal, jnp.concatenate([wide, wide], axis=0), 0.0)
-        rr = jnp.concatenate(halves(wide), axis=0)
-        lh, ll = (dot(dot(pick, m).astype(jnp.bfloat16), pick_t).astype(jnp.bfloat16) for m in halves(left[l]))
-        lll = jnp.concatenate([lh, ll, lh], axis=1)
+        wide = jnp.concatenate([wide, wide], axis=1)
+        wide = jnp.where(same, jnp.concatenate([wide, wide], axis=0), 0.0)
+        rights.append(jnp.concatenate(halves(wide), axis=0))
+        high, low = halves(left[l])
+        both = dot(pick, jnp.concatenate([high, low], axis=1)).astype(jnp.bfloat16)
+        high, low = (dot(both[:, n:n + proj], pick_t).astype(jnp.bfloat16) for n in (0, proj))
+        lefts.append(jnp.concatenate([high, low, high], axis=1))
+    arrived()
+    for l in range(layers):
         x = jnp.concatenate([query[l, :, k * 128:(k + 1) * 128] for k in range(pairs)], axis=0)
-        turned[l] = dot(jnp.concatenate([x, x], axis=1), rr)
-        for q0 in range(0, rows, step):
-            u = jnp.concatenate([turned[l, pl.ds(q, pairs, stride=rows), :] for q in range(q0, q0 + step)], axis=1)
-            v = jnp.concatenate(
-                [pltpu.roll(turned[l, pl.ds(q, pairs, stride=rows), :], proj, 1) for q in range(q0, q0 + step)], axis=1
-            )
-            wh, wl = halves(jnp.concatenate([jnp.where(low, u, v), jnp.where(low, v, u)], axis=0))
-            z = dot(lll, jnp.concatenate([wh, wh, wl], axis=0))
-            z = jnp.where(low, z[:half], z[half:])
+        y = dot(jnp.concatenate([x, x], axis=1), rights[l])
+        for p in range(2):
+            for k in range(pairs):
+                turned[l, p, k * stride:k * stride + rows] = y[k * rows:(k + 1) * rows, p * 128:(p + 1) * 128]
+    step = 8
+    first = lax.rem(lax.broadcasted_iota(jnp.int32, (pairs, step * 128), 1), 128) < proj
+    for l in range(layers):
+        for q in range(0, rows, step):
+            y = [
+                jnp.concatenate([turned[l, p, pl.ds(q + n, pairs, stride=stride), :] for n in range(step)], axis=1)
+                for p in range(2)
+            ]
+            high, low = halves(jnp.concatenate(y, axis=0))
+            z = dot(lefts[l], jnp.concatenate([high, high, low], axis=0))
+            z = jnp.where(first, z[:half], z[half:])
             for n in range(step):
-                mixed[l, pl.ds(q0 + n, pairs, stride=rows), :] = z[:, n * 128:(n + 1) * 128]
+                mixed[l, pl.ds(q + n, pairs, stride=stride), :] = z[:, n * 128:(n + 1) * 128]
         for m in range(pairs):
-            out[l, :, m * 128:(m + 1) * 128] = mixed[l, m * rows:(m + 1) * rows].astype(jnp.bfloat16)
-
-
-def precondition(query, left, right):
+            out[l, :, m * 128:(m + 1) * 128] = mixed[l, m * stride:m * stride + rows].astype(jnp.bfloat16)
+
+
+def precondition(query, left, right, first):
     layers, rows, feat = query.shape
-    scratch = pltpu.VMEM((layers, rows * feat // 128, 128), jnp.float32)
+    spread = (rows + 8) * feat // 128
+    scratch = [pltpu.VMEM((layers, 2, spread, 128), jnp.float32), pltpu.VMEM((layers, spread, 128), jnp.float32)]
+    operands = (query, left, right)
+    if first:
+        scratch = [pltpu.VMEM(v.shape, v.dtype) for v in operands] + scratch + [pltpu.SemaphoreType.DMA((3,))]
+        operands = [pltpu.with_memory_space_constraint(v, pltpu.HBM) for v in operands]
     return pl.pallas_call(
-        precondition_kernel,
+        precondition_first_kernel if first else precondition_kernel,
         out_shape=jax.ShapeDtypeStruct(query.shape, jnp.bfloat16),
-        in_specs=[HBM] * 3,
+        in_specs=[HBM if first else VMEM] * 3,
         out_specs=VMEM,
-        scratch_shapes=[
-            pltpu.VMEM(query.shape, query.dtype),
-            pltpu.VMEM(left.shape, left.dtype),
-            pltpu.VMEM(right.shape, right.dtype),
-            scratch,
-            scratch,
-            pltpu.SemaphoreType.DMA((3,)),
-        ],
+        scratch_shapes=scratch,
         compiler_params=pltpu.CompilerParams(vmem_limit_bytes=16 << 20),
         cost_estimate=pl.CostEstimate(flops=2 << 30, bytes_accessed=4 << 20, transcendentals=0),
-        name="precondition",
-    )(*(pltpu.with_memory_space_constraint(v, pltpu.HBM) for v in (query, left, right)))
+        name="precondition_0" if first else "precondition_1",
+    )(*operands)
 
 
 def transpose_kernel(layer, train, out, buffer, sems):
@@ -160,12 +171,12 @@
 def split(offset, ahead, behind, sent, kept):
     @pl.when(foreign(offset))
     def _():
-        sent[...] = ahead[...]
+        sent[...] = ahead[...].astype(sent.dtype)
         kept[...] = behind[...]
 
     @pl.when(jnp.logical_not(foreign(offset)))
     def _():
-        sent[...] = behind[...]
+        sent[...] = behind[...].astype(sent.dtype)
         kept[...] = ahead[...]
 
 
@@ -174,18 +185,17 @@
 
 
 def second_kernel(turned, more, *refs):
-    *queries, sent, kept, total = refs
-    half = sent.shape[0]
-    total[...] = score_parts(turned, more, *queries)
-    split(2, total.at[:half], total.at[half:], sent, kept)
-
-
-def third_kernel(turned, more, first, *refs):
+    refs[-1][...] = score_parts(turned, more, *refs[:-1])
+
+
+def third_kernel(turned, more, first, second, *refs):
     *queries, sent, kept, total = refs
     half = total.shape[0] // 2
     total[...] = score_parts(turned, more, *queries)
-    split(1, first.at[:half], total.at[half:], sent.at[:half], kept.at[:half])
-    split(3, total.at[:half], first.at[half:], sent.at[half:], kept.at[half:])
+    at = [pl.ds(n * half, half) for n in range(3)]
+    split(1, first.at[at[0]], total.at[at[1]], sent.at[at[0]], kept.at[at[0]])
+    split(2, second.at[at[0]], second.at[at[1]], sent.at[at[1]], kept.at[at[1]])
+    split(3, total.at[at[0]], first.at[at[1]], sent.at[at[2]], kept.at[at[2]])
 
 
 def fourth_kernel(turned, more, own, *refs):
@@ -194,12 +204,12 @@
     split(4, total, own, sent, kept)
 
 
-def block_call(kernel, name, rows, total, turned, operands):
+def block_call(kernel, name, rows, total, turned, operands, kind=jnp.float32):
     columns = turned[0].shape[1]
     block = jax.ShapeDtypeStruct((rows, columns), jnp.float32)
     return pl.pallas_call(
         kernel,
-        out_shape=(block, block) if total else block,
+        out_shape=(jax.ShapeDtypeStruct(block.shape, kind), block) if total else block,
         in_specs=[VMEM] * (2 + len(operands)),
         out_specs=(VMEM, VMEM) if total else VMEM,
         scratch_shapes=[pltpu.VMEM((total, columns), jnp.float32)] if total else [],
@@ -209,11 +219,11 @@
     )(*turned, *operands)
 
 
-def gather_kernel(kept2, got2, kept13, got13, out):
-    half = kept2.shape[0]
-
-    def place(offset, kept, got):
-        block = kept[...] + got[...]
+def gather_kernel(kept, got, out):
+    rows = kept.shape[0] // 3
+    for n in range(3):
+        offset = n + 1
+        block = kept[n * rows:(n + 1) * rows] + got[n * rows:(n + 1) * rows].astype(kept.dtype)
 
         @pl.when(foreign(offset))
         def _():
@@ -223,15 +233,11 @@
         def _():
             put(out, chip_at(offset), offset, block)
 
-    place(2, kept2, got2)
-    place(1, kept13.at[:half], got13.at[:half])
-    place(3, kept13.at[half:], got13.at[half:])
-
 
 def last_kernel(kept, got, table, out, block, sems):
     del table
     rows = kept.shape[0] // 2
-    block[...] = kept[...] + got[...]
+    block[...] = kept[...] + got[...].astype(kept.dtype)
     at = jnp.where(foreign(4), chip_at(0), chip_at(4)) - 4 * lax.axis_index("layer")
     core = lax.rem(lax.axis_index("row"), 2)
     copies = []
@@ -244,15 +250,14 @@
         copy.wait()
 
 
-def finish(parts, rows, columns):
-    (kept2, got2), (kept13, got13), (kept4, got4) = parts
+def finish(kept, got, kept4, got4, rows, columns):
     hbm = pl.BlockSpec(memory_space=pl.ANY)
     table = jax.ShapeDtypeStruct((rows, columns), jnp.float32)
     params = pltpu.CompilerParams(vmem_limit_bytes=8 << 20)
     most = pl.pallas_call(
-        gather_kernel, out_shape=table, in_specs=[VMEM] * 4, out_specs=VMEM, compiler_params=params, name="gather_rows",
+        gather_kernel, out_shape=table, in_specs=[VMEM] * 2, out_specs=VMEM, compiler_params=params, name="gather_rows",
         cost_estimate=pl.CostEstimate(flops=60 << 30, bytes_accessed=1 << 20, transcendentals=0),
-    )(kept2, got2, kept13, got13)
+    )(kept, got)
     return pl.pallas_call(
         last_kernel,
         out_shape=table,
@@ -282,33 +287,31 @@
     send = lambda v, pairs: lax.ppermute(v, AXES, pairs)
 
     after = lax.optimization_barrier
-    mine = precondition(query_grads, left_inverse, right_inverse)
-    turned = [transpose(0, train_grads)]
-    a, b = [mine, send(mine, around)], [send(mine, swap)]
-    (b0, turned[0]) = after((b[0], turned[0]))
-    turned.append(transpose(1, train_grads))
-    b.append(send(b0, around))
+    arrived = [send(query_grads, around), send(send(query_grads, swap), around)]
+    mine = precondition(query_grads, left_inverse, right_inverse, True)
+    a, b = [mine], [send(mine, swap)]
+    turned = [transpose(l, train_grads) for l in range(2)]
+    arrived[0], *turned = after((arrived[0], *turned))
+    a.append(precondition(arrived[0], left_inverse, right_inverse, False))
+    b.append(precondition(arrived[1], left_inverse, right_inverse, False))
     rows = 2 * mine.shape[1]
-    zeroth = block_call(plain_kernel, "scores_0", rows, 0, turned, [a[0], b0])
+    zeroth = block_call(plain_kernel, "scores_0", rows, 0, turned, [a[0], b[0]])
     a.append(send(a[1], around))
-    b[1], zeroth = after((b[1], zeroth))
     b.append(send(b[1], around))
     first = block_call(plain_kernel, "scores_1", 2 * rows, 0, turned, [a[1], b[1], send(a[1], swap), send(b[1], swap)])
     a.append(send(a[2], around))
-    b[2], first = after((b[2], first))
+    b[2], first, _ = after((b[2], first, mine))
     b.append(send(b[2], around))
-    sent2, kept2 = block_call(second_kernel, "scores_2", rows, 2 * rows, turned, [a[2], b[2], send(a[2], swap), *(send(b[2][l:l + 1], swap) for l in range(2))])
-    a[3], _ = after((a[3], sent2))
+    second = block_call(second_kernel, "scores_2", 2 * rows, 0, turned, [a[2], b[2], send(a[2], swap), *(send(b[2][l:l + 1], swap) for l in range(2))])
+    a[3], second, zeroth = after((a[3], second, zeroth))
     a.append(send(a[3], around))
-    got2 = send(sent2, across)
-    b[3], _ = after((b[3], got2))
-    sent3, kept3 = block_call(third_kernel, "scores_3", 2 * rows, 2 * rows, turned, [first, a[3], b[3], send(a[3], swap), *(send(b[3][l:l + 1], swap) for l in range(2))])
-    a[4], _ = after((a[4], sent3))
-    got3 = send(sent3, across)
-    ends = [a[4], *(send(a[4][l:l + 1, 16 * n:16 * n + 16], swap) for l in range(2) for n in range(2))]
-    sent4, kept4 = block_call(fourth_kernel, "scores_4", rows, rows, turned, [zeroth, *ends])
-    pairs = [(kept2, got2), (kept3, got3), (kept4, send(sent4, across))]
-    return finish(pairs, chips // groups * rows, turned[0].shape[1])
+    queries = [a[3], b[3], send(a[3], swap), *(send(b[3][l:l + 1], swap) for l in range(2))]
+    sent, kept = block_call(third_kernel, "scores_3", 3 * rows, 2 * rows, turned, [first, second] + queries, jnp.bfloat16)
+    a[4], _ = after((a[4], sent))
+    got = send(sent, across)
+    end = [a[4], *(send(a[4][l:l + 1, 16 * n:16 * n + 16], swap) for l in range(2) for n in range(2))]
+    sent4, kept4 = block_call(fourth_kernel, "scores_4", rows, rows, turned, [zeroth, *end], jnp.bfloat16)
+    return finish(kept, got, kept4, send(sent4, across), chips // groups * rows, turned[0].shape[1])
 
 
 def on_device(query_grads, train_grads, left_inverse, right_inverse):

time: 58.5 us -> 53.3 us (0.911)
  waiting for transfers between devices: 18 us -> 10.8 us
  Pallas kernels: 17.7 us -> 19.8 us
    ppermute x23, waiting for transfers between devices: 18 us -> 10.8 us  [ring_device(): send = lambda v, pairs: lax.ppermute(v, AXES, pairs)]
    pallas_call x7 -> x9, Pallas kernels: 11.7 us -> 13.8 us  [the longest x5 6.94 us: block_call(): pl.pallas_call(kernel, out_shape=(jax.ShapeDtypeStruct(block.shape, kind)...]
  transfers between devices with their start and end apart: 23 -> 23, of which waited for: 16 -> 12; matrix products, arithmetic and copies ran while one was open for 0% -> 0% of each run, Pallas kernels for 23% -> 36%
where the time goes in v3:
time: 53.3 us; the launch traced here: 53.1 us
  starting transfers between devices  22.2 us (42%)
  Pallas kernels  19.8 us (37%)
  waiting for transfers between devices  10.8 us (20%)
    ppermute x23, starting transfers between devices, ring_device(): send = lambda v, pairs: lax.ppermute(v, AXES, pairs)  22.2 us
    ppermute x23, waiting for transfers between devices, ring_device(): send = lambda v, pairs: lax.ppermute(v, AXES, pairs)  10.8 us
    pallas_call x5, Pallas kernels, block_call(): pl.pallas_call(kernel, out_shape=(jax.ShapeDtypeStruct(block.shape, kind)...  6.94 us
    pallas_call x3, Pallas kernels, precondition(): pl.pallas_call(precondition_first_kernel if first else precondition_kerne...  5.92 us
    pallas_call x2, Pallas kernels, transpose(): pl.pallas_call(functools.partial(transpose_kernel, layer), out_shape=pltp...  5.31 us
  transfers between devices with their start and end apart: 23, of which 12 were waited for; matrix products, arithmetic and copies ran while one was open for 0% of the time, Pallas kernels for 36%

profile of v3, /device:TPU:0, one launch (start us, length us, event | category | flops | bytes accessed | tf_op | source)
XLA Modules:
  0.0 53.1 jit_solution(8787728489694328036)
XLA Ops:
  0.5 2.6 %collective-permute-start = (bf16[2,32,4096]{2,1,0:T(8,128)(2,1)}, bf16[2,32,4096]{2,1,0:T(8,128)(2,1)S(1)}, u32[]{:S(2)}, u32[]{:S(2)}) collective-permute-start(bf16[2,32,4096]{2,1,0:T(8,128)(2,1)} %query_hbm.1), channel_id=1, source_target_pairs={{0,4},{1,3},{2,0},{3,7},{4,8},{5,1},{6,2},{7,11},{8,12},{9,5},{10,... | collective-permute-start | bytes 1572872 | tf_op jit(solution)/shard_map/ppermute | solution.py:287
  3.0 2.1 %collective-permute-start.4 = (bf16[2,32,4096]{2,1,0:T(8,128)(2,1)S(1)}, bf16[2,32,4096]{2,1,0:T(8,128)(2,1)S(1)}, u32[]{:S(2)}, u32[]{:S(2)}) collective-permute-start(bf16[2,32,4096]{2,1,0:T(8,128)(2,1)S(1)} %collective-permute-done.3), channel_id=1, source_target_pairs={{0,4},{1,3},{2,0},{3,7},{4,8},{5,1},{6,2},{7,11},{8,12},{9,5},{10,... | collective-permute-start | bytes 1572872 | tf_op jit(solution)/shard_map/ppermute | solution.py:287
  5.1 2.6 %transpose_0.1.turned = bf16[4096,512]{1,0:T(8,128)(2,1)S(1)} custom-call(bf16[2,512,4096]{2,1,0:T(8,128)(2,1)} %train.3), custom_call_target="tpu_custom_call" | custom-call | flops 2147483648 | bytes 8388608 | tf_op jit(solution)/shard_map/transpose_0/pallas_call | solution.py:122
  7.8 2.7 %transpose_1.1.more = bf16[4096,512]{1,0:T(8,128)(2,1)S(1)} custom-call(bf16[2,512,4096]{2,1,0:T(8,128)(2,1)} %train.3), custom_call_target="tpu_custom_call" | custom-call | flops 2147483648 | bytes 8388608 | tf_op jit(solution)/shard_map/transpose_1/pallas_call | solution.py:122
  10.5 1.6 %precondition_1.2.refs_0_ = bf16[2,32,4096]{2,1,0:T(8,128)(2,1)S(1)} custom-call(bf16[2,32,4096]{2,1,0:T(8,128)(2,1)S(1)} %collective-permute-done.query, f32[2,64,64]{2,1,0:T(8,128)S(1)} %copy-done, f32[2,64,64]{2,1,0:T(8,128)S(1)} %copy-done.1), custom_call_target="tpu_custom_call" | custom-call | flops 2147483648 | bytes 4194304 | tf_op jit(solution)/shard_map/precondition_1/pallas_call | solution.py:90
  12.2 1.9 %collective-permute-start.1 = (bf16[2,32,4096]{2,1,0:T(8,128)(2,1)S(1)}, bf16[2,32,4096]{2,1,0:T(8,128)(2,1)S(1)}, u32[]{:S(2)}, u32[]{:S(2)}) collective-permute-start(bf16[2,32,4096]{2,1,0:T(8,128)(2,1)S(1)} %precondition_1.2.refs_0_), channel_id=1, source_target_pairs={{0,4},{1,3},{2,0},{3,7},{4,8},{5,1},{6,2},{7,11},{8,12},{9,5},{10,... | collective-permute-start | bytes 1572872 | tf_op jit(solution)/shard_map/ppermute | solution.py:287
  14.2 1.8 %collective-permute-done.4.query = bf16[2,32,4096]{2,1,0:T(8,128)(2,1)S(1)} collective-permute-done((bf16[2,32,4096]{2,1,0:T(8,128)(2,1)S(1)}, bf16[2,32,4096]{2,1,0:T(8,128)(2,1)S(1)}, u32[]{:S(2)}, u32[]{:S(2)}) %collective-permute-start.4) | collective-permute-done | bytes 524320 | tf_op jit(solution)/shard_map/ppermute | solution.py:287
  15.9 1.6 %precondition_1.3.refs_1_ = bf16[2,32,4096]{2,1,0:T(8,128)(2,1)S(1)} custom-call(bf16[2,32,4096]{2,1,0:T(8,128)(2,1)S(1)} %collective-permute-done.4.query, f32[2,64,64]{2,1,0:T(8,128)S(1)} %copy-done, f32[2,64,64]{2,1,0:T(8,128)S(1)} %copy-done.1), custom_call_target="tpu_custom_call" | custom-call | flops 2147483648 | bytes 4194304 | tf_op jit(solution)/shard_map/precondition_1/pallas_call | solution.py:90
  17.6 2.2 %collective-permute-start.5 = (bf16[2,32,4096]{2,1,0:T(8,128)(2,1)S(1)}, bf16[2,32,4096]{2,1,0:T(8,128)(2,1)S(1)}, u32[]{:S(2)}, u32[]{:S(2)}) collective-permute-start(bf16[2,32,4096]{2,1,0:T(8,128)(2,1)S(1)} %precondition_1.3.refs_1_), channel_id=1, source_target_pairs={{0,4},{1,3},{2,0},{3,7},{4,8},{5,1},{6,2},{7,11},{8,12},{9,5},{10,... | collective-permute-start | bytes 1572872 | tf_op jit(solution)/shard_map/ppermute | solution.py:287
  19.8 2.7 %precondition_0.1.refs_0_ = bf16[2,32,4096]{2,1,0:T(8,128)(2,1)S(1)} custom-call(bf16[2,32,4096]{2,1,0:T(8,128)(2,1)} %query_hbm.1, f32[2,64,64]{2,1,0:T(8,128)} %left_hbm.1, f32[2,64,64]{2,1,0:T(8,128)} %right_hbm.1), custom_call_target="tpu_custom_call" | custom-call | flops 2147483648 | bytes 4194304 | tf_op jit(solution)/shard_map/precondition_0/pallas_call | solution.py:90
  23.1 1.6 %collective-permute-start.2 = (bf16[2,32,4096]{2,1,0:T(8,128)(2,1)S(1)}, bf16[2,32,4096]{2,1,0:T(8,128)(2,1)S(1)}, u32[]{:S(2)}, u32[]{:S(2)}) collective-permute-start(bf16[2,32,4096]{2,1,0:T(8,128)(2,1)S(1)} %collective-permute-done.1.refs_0_), channel_id=1, source_target_pairs={{0,4},{1,3},{2,0},{3,7},{4,8},{5,1},{6,2},{7,11},{8,12},{9,5},{10,... | collective-permute-start | bytes 1572872 | tf_op jit(solution)/shard_map/ppermute | solution.py:287
  24.7 1.2 %scores_1.1.first = f32[128,512]{1,0:T(8,128)S(1)} custom-call(bf16[4096,512]{1,0:T(8,128)(2,1)S(1)} %transpose_0.1.turned, bf16[4096,512]{1,0:T(8,128)(2,1)S(1)} %transpose_1.1.more, bf16[2,32,4096]{2,1,0:T(8,128)(2,1)S(1)} %precondition_1.2.refs_0_, bf16[2,32,4096]{2,1,0:T(8,128)(2,1)S(1)} %precondition_1.3.refs_1_, ...), custom_call_target="tpu_custom_call" | custom-call | flops 1024 | bytes 1024 | tf_op jit(solution)/shard_map/scores_1/pallas_call | solution.py:210
  25.9 1.2 %collective-permute-done.5.refs_1_ = bf16[2,32,4096]{2,1,0:T(8,128)(2,1)S(1)} collective-permute-done((bf16[2,32,4096]{2,1,0:T(8,128)(2,1)S(1)}, bf16[2,32,4096]{2,1,0:T(8,128)(2,1)S(1)}, u32[]{:S(2)}, u32[]{:S(2)}) %collective-permute-start.5) | collective-permute-done | bytes 524320 | tf_op jit(solution)/shard_map/ppermute | solution.py:287
  27.2 2.1 %collective-permute-start.13 = (bf16[2,32,4096]{2,1,0:T(8,128)(2,1)S(1)}, bf16[2,32,4096]{2,1,0:T(8,128)(2,1)S(1)}, u32[]{:S(2)}, u32[]{:S(2)}) collective-permute-start(bf16[2,32,4096]{2,1,0:T(8,128)(2,1)S(1)} %collective-permute-done.5.refs_1_), channel_id=1, source_target_pairs={{0,4},{1,3},{2,0},{3,7},{4,8},{5,1},{6,2},{7,11},{8,12},{9,5},{10,... | collective-permute-start | bytes 1572872 | tf_op jit(solution)/shard_map/ppermute | solution.py:287
  29.9 1.5 %scores_0.1.own = f32[64,512]{1,0:T(8,128)S(1)} custom-call(bf16[4096,512]{1,0:T(8,128)(2,1)S(1)} %transpose_0.1.turned, bf16[4096,512]{1,0:T(8,128)(2,1)S(1)} %transpose_1.1.more, bf16[2,32,4096]{2,1,0:T(8,128)(2,1)S(1)} %precondition_0.1.refs_0_, bf16[2,32,4096]{2,1,0:T(8,128)(2,1)S(1)} %collective-permute-done.11.refs_1_), custom_call_target="tpu_custom_call" | custom-call | flops 1024 | bytes 1024 | tf_op jit(solution)/shard_map/scores_0/pallas_call | solution.py:210
  31.5 1.2 %scores_2.1.second = f32[128,512]{1,0:T(8,128)S(1)} custom-call(bf16[4096,512]{1,0:T(8,128)(2,1)S(1)} %transpose_0.1.turned, bf16[4096,512]{1,0:T(8,128)(2,1)S(1)} %transpose_1.1.more, bf16[2,32,4096]{2,1,0:T(8,128)(2,1)S(1)} %collective-permute-done.1.refs_0_, bf16[2,32,4096]{2,1,0:T(8,128)(2,1)S(1)} %collective-permute-done.5.refs_1_, ...), custom_call_target="tpu_custom_call" | custom-call | flops 1024 | bytes 1024 | tf_op jit(solution)/shard_map/scores_2/pallas_call | solution.py:210
  32.9 2.0 %collective-permute-start.12 = (bf16[2,32,4096]{2,1,0:T(8,128)(2,1)S(1)}, bf16[2,32,4096]{2,1,0:T(8,128)(2,1)S(1)}, u32[]{:S(2)}, u32[]{:S(2)}) collective-permute-start(bf16[2,32,4096]{2,1,0:T(8,128)(2,1)S(1)} %collective-permute-done.2.refs_0_), channel_id=1, source_target_pairs={{0,4},{1,3},{2,0},{3,7},{4,8},{5,1},{6,2},{7,11},{8,12},{9,5},{10,... | collective-permute-start | bytes 1572872 | tf_op jit(solution)/shard_map/ppermute | solution.py:287
  34.9 3.5 %collective-permute-done.13.refs_1_ = bf16[2,32,4096]{2,1,0:T(8,128)(2,1)S(1)} collective-permute-done((bf16[2,32,4096]{2,1,0:T(8,128)(2,1)S(1)}, bf16[2,32,4096]{2,1,0:T(8,128)(2,1)S(1)}, u32[]{:S(2)}, u32[]{:S(2)}) %collective-permute-start.13) | collective-permute-done | bytes 524320 | tf_op jit(solution)/shard_map/ppermute | solution.py:287
  39.0 1.0 %collective-permute-done.15.refs_3_ = bf16[1,32,4096]{2,1,0:T(8,128)(2,1)S(1)} collective-permute-done((bf16[1,32,4096]{2,1,0:T(8,128)(2,1)S(1)}, bf16[1,32,4096]{2,1,0:T(8,128)(2,1)S(1)}, u32[]{:S(2)}, u32[]{:S(2)}) %collective-permute-start.15) | collective-permute-done | bytes 262176 | tf_op jit(solution)/shard_map/ppermute | solution.py:287
  40.4 1.3 %scores_3.1 = (bf16[192,512]{1,0:T(8,128)(2,1)S(1)}, f32[192,512]{1,0:T(8,128)S(1)}) custom-call(bf16[4096,512]{1,0:T(8,128)(2,1)S(1)} %transpose_0.1.turned, bf16[4096,512]{1,0:T(8,128)(2,1)S(1)} %transpose_1.1.more, f32[128,512]{1,0:T(8,128)S(1)} %scores_1.1.first, f32[128,512]{1,0:T(8,128)S(1)} %scores_2.1.second, ...), custom_call_target="tpu_custom_call" | custom-call | flops 1024 | bytes 1024 | tf_op jit(solution)/shard_map/scores_3/pallas_call | solution.py:210
  41.8 2.1 %collective-permute-start.22 = (bf16[192,512]{1,0:T(8,128)(2,1)S(1)}, bf16[192,512]{1,0:T(8,128)(2,1)S(1)}, u32[]{:S(2)}, u32[]{:S(2)}) collective-permute-start(bf16[192,512]{1,0:T(8,128)(2,1)S(1)} %get-tuple-element.26), channel_id=1, source_target_pairs={{0,16},{1,17},{2,18},{3,19},{4,20},{5,21},{6,22},{7,23},{8,24},{9,... | collective-permute-start | bytes 589832 | tf_op jit(solution)/shard_map/ppermute | solution.py:287
  46.2 1.6 %scores_4.1 = (bf16[64,512]{1,0:T(8,128)(2,1)S(1)}, f32[64,512]{1,0:T(8,128)S(1)}) custom-call(bf16[4096,512]{1,0:T(8,128)(2,1)S(1)} %transpose_0.1.turned, bf16[4096,512]{1,0:T(8,128)(2,1)S(1)} %transpose_1.1.more, f32[64,512]{1,0:T(8,128)S(1)} %scores_0.1.own, bf16[2,32,4096]{2,1,0:T(8,128)(2,1)S(1)} %collective-permute-done.12.refs_0_, ...), custom_call_target="tpu_custom_call" | custom-call | flops 1024 | bytes 1024 | tf_op jit(solution)/shard_map/scores_4/pallas_call | solution.py:210
  47.7 2.1 %collective-permute-start.21 = (bf16[64,512]{1,0:T(8,128)(2,1)S(1)}, bf16[64,512]{1,0:T(8,128)(2,1)S(1)}, u32[]{:S(2)}, u32[]{:S(2)}) collective-permute-start(bf16[64,512]{1,0:T(8,128)(2,1)S(1)} %get-tuple-element.29), channel_id=1, source_target_pairs={{0,16},{1,17},{2,18},{3,19},{4,20},{5,21},{6,22},{7,23},{8,24},{9,... | collective-permute-start | bytes 196616 | tf_op jit(solution)/shard_map/ppermute | solution.py:287
  50.8 1.7 %collective-permute-done.21.got = bf16[64,512]{1,0:T(8,128)(2,1)S(1)} collective-permute-done((bf16[64,512]{1,0:T(8,128)(2,1)S(1)}, bf16[64,512]{1,0:T(8,128)(2,1)S(1)}, u32[]{:S(2)}, u32[]{:S(2)}) %collective-permute-start.21) | collective-permute-done | bytes 65568 | tf_op jit(solution)/shard_map/ppermute | solution.py:287
  (41 shorter events, 6.9 us)
Async XLA Ops:
  0.0 3.0 %collective-permute-start.3 = (bf16[2,32,4096]{2,1,0:T(8,128)(2,1)}, bf16[2,32,4096]{2,1,0:T(8,128)(2,1)S(1)}, u32[]{:S(2)}, u32[]{:S(2)}) collective-permute-start(bf16[2,32,4096]{2,1,0:T(8,128)(2,1)} %query_hbm.1), channel_id=1, source_target_pairs={{0,1},{1,0},{2,3},{3,2},{4,5},{5,4},{6,7},{7,6},{8,9},{9,8},{10,11... | collective-permute-start | bytes 1572872 | tf_op jit(solution)/shard_map/ppermute | solution.py:287
  0.5 10.0 %collective-permute-start = (bf16[2,32,4096]{2,1,0:T(8,128)(2,1)}, bf16[2,32,4096]{2,1,0:T(8,128)(2,1)S(1)}, u32[]{:S(2)}, u32[]{:S(2)}) collective-permute-start(bf16[2,32,4096]{2,1,0:T(8,128)(2,1)} %query_hbm.1), channel_id=1, source_target_pairs={{0,4},{1,3},{2,0},{3,7},{4,8},{5,1},{6,2},{7,11},{8,12},{9,5},{10,... | collective-permute-start | bytes 1572872 | tf_op jit(solution)/shard_map/ppermute | solution.py:287
  3.0 12.9 %collective-permute-start.4 = (bf16[2,32,4096]{2,1,0:T(8,128)(2,1)S(1)}, bf16[2,32,4096]{2,1,0:T(8,128)(2,1)S(1)}, u32[]{:S(2)}, u32[]{:S(2)}) collective-permute-start(bf16[2,32,4096]{2,1,0:T(8,128)(2,1)S(1)} %collective-permute-done.3), channel_id=1, source_target_pairs={{0,4},{1,3},{2,0},{3,7},{4,8},{5,1},{6,2},{7,11},{8,12},{9,5},{10,... | collective-permute-start | bytes 1572872 | tf_op jit(solution)/shard_map/ppermute | solution.py:287
  7.8 2.7 %copy-start = (f32[2,64,64]{2,1,0:T(8,128)S(1)}, f32[2,64,64]{2,1,0:T(8,128)}, u32[]{:S(2)}) copy-start(f32[2,64,64]{2,1,0:T(8,128)} %left_hbm.1) | copy-start | bytes 98308
  12.1 11.0 %collective-permute-start.6 = (bf16[2,32,4096]{2,1,0:T(8,128)(2,1)S(1)}, bf16[2,32,4096]{2,1,0:T(8,128)(2,1)S(1)}, u32[]{:S(2)}, u32[]{:S(2)}) collective-permute-start(bf16[2,32,4096]{2,1,0:T(8,128)(2,1)S(1)} %precondition_1.2.refs_0_), channel_id=1, source_target_pairs={{0,1},{1,0},{2,3},{3,2},{4,5},{5,4},{6,7},{7,6},{8,9},{9,8},{10,11... | collective-permute-start | bytes 1572872 | tf_op jit(solution)/shard_map/ppermute | solution.py:287
  12.2 10.4 %collective-permute-start.1 = (bf16[2,32,4096]{2,1,0:T(8,128)(2,1)S(1)}, bf16[2,32,4096]{2,1,0:T(8,128)(2,1)S(1)}, u32[]{:S(2)}, u32[]{:S(2)}) collective-permute-start(bf16[2,32,4096]{2,1,0:T(8,128)(2,1)S(1)} %precondition_1.2.refs_0_), channel_id=1, source_target_pairs={{0,4},{1,3},{2,0},{3,7},{4,8},{5,1},{6,2},{7,11},{8,12},{9,5},{10,... | collective-permute-start | bytes 1572872 | tf_op jit(solution)/shard_map/ppermute | solution.py:287
  17.5 7.1 %collective-permute-start.7 = (bf16[2,32,4096]{2,1,0:T(8,128)(2,1)S(1)}, bf16[2,32,4096]{2,1,0:T(8,128)(2,1)S(1)}, u32[]{:S(2)}, u32[]{:S(2)}) collective-permute-start(bf16[2,32,4096]{2,1,0:T(8,128)(2,1)S(1)} %precondition_1.3.refs_1_), channel_id=1, source_target_pairs={{0,1},{1,0},{2,3},{3,2},{4,5},{5,4},{6,7},{7,6},{8,9},{9,8},{10,11... | collective-permute-start | bytes 1572872 | tf_op jit(solution)/shard_map/ppermute | solution.py:287
  17.6 9.5 %collective-permute-start.5 = (bf16[2,32,4096]{2,1,0:T(8,128)(2,1)S(1)}, bf16[2,32,4096]{2,1,0:T(8,128)(2,1)S(1)}, u32[]{:S(2)}, u32[]{:S(2)}) collective-permute-start(bf16[2,32,4096]{2,1,0:T(8,128)(2,1)S(1)} %precondition_1.3.refs_1_), channel_id=1, source_target_pairs={{0,4},{1,3},{2,0},{3,7},{4,8},{5,1},{6,2},{7,11},{8,12},{9,5},{10,... | collective-permute-start | bytes 1572872 | tf_op jit(solution)/shard_map/ppermute | solution.py:287
  22.5 6.9 %collective-permute-start.11 = (bf16[2,32,4096]{2,1,0:T(8,128)(2,1)S(1)}, bf16[2,32,4096]{2,1,0:T(8,128)(2,1)S(1)}, u32[]{:S(2)}, u32[]{:S(2)}) collective-permute-start(bf16[2,32,4096]{2,1,0:T(8,128)(2,1)S(1)} %precondition_0.1.refs_0_), channel_id=1, source_target_pairs={{0,1},{1,0},{2,3},{3,2},{4,5},{5,4},{6,7},{7,6},{8,9},{9,8},{10,11... | collective-permute-start | bytes 1572872 | tf_op jit(solution)/shard_map/ppermute | solution.py:287
  22.7 8.8 %collective-permute-start.8 = (bf16[2,32,4096]{2,1,0:T(8,128)(2,1)S(1)}, bf16[2,32,4096]{2,1,0:T(8,128)(2,1)S(1)}, u32[]{:S(2)}, u32[]{:S(2)}) collective-permute-start(bf16[2,32,4096]{2,1,0:T(8,128)(2,1)S(1)} %collective-permute-done.1.refs_0_), channel_id=1, source_target_pairs={{0,1},{1,0},{2,3},{3,2},{4,5},{5,4},{6,7},{7,6},{8,9},{9,8},{10,11... | collective-permute-start | bytes 1572872 | tf_op jit(solution)/shard_map/ppermute | solution.py:287
  23.1 9.7 %collective-permute-start.2 = (bf16[2,32,4096]{2,1,0:T(8,128)(2,1)S(1)}, bf16[2,32,4096]{2,1,0:T(8,128)(2,1)S(1)}, u32[]{:S(2)}, u32[]{:S(2)}) collective-permute-start(bf16[2,32,4096]{2,1,0:T(8,128)(2,1)S(1)} %collective-permute-done.1.refs_0_), channel_id=1, source_target_pairs={{0,4},{1,3},{2,0},{3,7},{4,8},{5,1},{6,2},{7,11},{8,12},{9,5},{10,... | collective-permute-start | bytes 1572872 | tf_op jit(solution)/shard_map/ppermute | solution.py:287
  27.2 11.2 %collective-permute-start.13 = (bf16[2,32,4096]{2,1,0:T(8,128)(2,1)S(1)}, bf16[2,32,4096]{2,1,0:T(8,128)(2,1)S(1)}, u32[]{:S(2)}, u32[]{:S(2)}) collective-permute-start(bf16[2,32,4096]{2,1,0:T(8,128)(2,1)S(1)} %collective-permute-done.5.refs_1_), channel_id=1, source_target_pairs={{0,4},{1,3},{2,0},{3,7},{4,8},{5,1},{6,2},{7,11},{8,12},{9,5},{10,... | collective-permute-start | bytes 1572872 | tf_op jit(solution)/shard_map/ppermute | solution.py:287
  29.3 2.1 %collective-permute-start.10 = (bf16[1,32,4096]{2,1,0:T(8,128)(2,1)S(1)}, bf16[1,32,4096]{2,1,0:T(8,128)(2,1)S(1)}, u32[]{:S(2)}, u32[]{:S(2)}) collective-permute-start(bf16[1,32,4096]{2,1,0:T(8,128)(2,1)S(1)} %get-tuple-element.37), channel_id=1, source_target_pairs={{0,1},{1,0},{2,3},{3,2},{4,5},{5,4},{6,7},{7,6},{8,9},{9,8},{10,11... | collective-permute-start | bytes 786440 | tf_op jit(solution)/shard_map/ppermute | solution.py:287
  29.4 2.1 %collective-permute-start.9 = (bf16[1,32,4096]{2,1,0:T(8,128)(2,1)S(1)}, bf16[1,32,4096]{2,1,0:T(8,128)(2,1)S(1)}, u32[]{:S(2)}, u32[]{:S(2)}) collective-permute-start(bf16[1,32,4096]{2,1,0:T(8,128)(2,1)S(1)} %get-tuple-element.38), channel_id=1, source_target_pairs={{0,1},{1,0},{2,3},{3,2},{4,5},{5,4},{6,7},{7,6},{8,9},{9,8},{10,11... | collective-permute-start | bytes 786440 | tf_op jit(solution)/shard_map/ppermute | solution.py:287
  32.8 6.2 %collective-permute-start.14 = (bf16[2,32,4096]{2,1,0:T(8,128)(2,1)S(1)}, bf16[2,32,4096]{2,1,0:T(8,128)(2,1)S(1)}, u32[]{:S(2)}, u32[]{:S(2)}) collective-permute-start(bf16[2,32,4096]{2,1,0:T(8,128)(2,1)S(1)} %collective-permute-done.2.refs_0_), channel_id=1, source_target_pairs={{0,1},{1,0},{2,3},{3,2},{4,5},{5,4},{6,7},{7,6},{8,9},{9,8},{10,11... | collective-permute-start | bytes 1572872 | tf_op jit(solution)/shard_map/ppermute | solution.py:287
  32.9 11.1 %collective-permute-start.12 = (bf16[2,32,4096]{2,1,0:T(8,128)(2,1)S(1)}, bf16[2,32,4096]{2,1,0:T(8,128)(2,1)S(1)}, u32[]{:S(2)}, u32[]{:S(2)}) collective-permute-start(bf16[2,32,4096]{2,1,0:T(8,128)(2,1)S(1)} %collective-permute-done.2.refs_0_), channel_id=1, source_target_pairs={{0,4},{1,3},{2,0},{3,7},{4,8},{5,1},{6,2},{7,11},{8,12},{9,5},{10,... | collective-permute-start | bytes 1572872 | tf_op jit(solution)/shard_map/ppermute | solution.py:287
  38.4 1.6 %collective-permute-start.15 = (bf16[1,32,4096]{2,1,0:T(8,128)(2,1)S(1)}, bf16[1,32,4096]{2,1,0:T(8,128)(2,1)S(1)}, u32[]{:S(2)}, u32[]{:S(2)}) collective-permute-start(bf16[1,32,4096]{2,1,0:T(8,128)(2,1)S(1)} %get-tuple-element.36), channel_id=1, source_target_pairs={{0,1},{1,0},{2,3},{3,2},{4,5},{5,4},{6,7},{7,6},{8,9},{9,8},{10,11... | collective-permute-start | bytes 786440 | tf_op jit(solution)/shard_map/ppermute | solution.py:287
  38.5 1.9 %collective-permute-start.16 = (bf16[1,32,4096]{2,1,0:T(8,128)(2,1)S(1)}, bf16[1,32,4096]{2,1,0:T(8,128)(2,1)S(1)}, u32[]{:S(2)}, u32[]{:S(2)}) collective-permute-start(bf16[1,32,4096]{2,1,0:T(8,128)(2,1)S(1)} %get-tuple-element.35), channel_id=1, source_target_pairs={{0,1},{1,0},{2,3},{3,2},{4,5},{5,4},{6,7},{7,6},{8,9},{9,8},{10,11... | collective-permute-start | bytes 786440 | tf_op jit(solution)/shard_map/ppermute | solution.py:287
  41.8 8.1 %collective-permute-start.22 = (bf16[192,512]{1,0:T(8,128)(2,1)S(1)}, bf16[192,512]{1,0:T(8,128)(2,1)S(1)}, u32[]{:S(2)}, u32[]{:S(2)}) collective-permute-start(bf16[192,512]{1,0:T(8,128)(2,1)S(1)} %get-tuple-element.26), channel_id=1, source_target_pairs={{0,16},{1,17},{2,18},{3,19},{4,20},{5,21},{6,22},{7,23},{8,24},{9,... | collective-permute-start | bytes 589832 | tf_op jit(solution)/shard_map/ppermute | solution.py:287
  44.1 1.4 %collective-permute-start.17 = (bf16[1,16,4096]{2,1,0:T(8,128)(2,1)S(1)}, bf16[1,16,4096]{2,1,0:T(8,128)(2,1)S(1)}, u32[]{:S(2)}, u32[]{:S(2)}) collective-permute-start(bf16[1,16,4096]{2,1,0:T(8,128)(2,1)S(1)} %get-tuple-element.34), channel_id=1, source_target_pairs={{0,1},{1,0},{2,3},{3,2},{4,5},{5,4},{6,7},{7,6},{8,9},{9,8},{10,11... | collective-permute-start | bytes 393224 | tf_op jit(solution)/shard_map/ppermute | solution.py:287
  44.1 1.5 %collective-permute-start.18 = (bf16[1,16,4096]{2,1,0:T(8,128)(2,1)S(1)}, bf16[1,16,4096]{2,1,0:T(8,128)(2,1)S(1)}, u32[]{:S(2)}, u32[]{:S(2)}) collective-permute-start(bf16[1,16,4096]{2,1,0:T(8,128)(2,1)S(1)} %get-tuple-element.33), channel_id=1, source_target_pairs={{0,1},{1,0},{2,3},{3,2},{4,5},{5,4},{6,7},{7,6},{8,9},{9,8},{10,11... | collective-permute-start | bytes 393224 | tf_op jit(solution)/shard_map/ppermute | solution.py:287
  44.6 1.3 %collective-permute-start.19 = (bf16[1,16,4096]{2,1,0:T(8,128)(2,1)S(1)}, bf16[1,16,4096]{2,1,0:T(8,128)(2,1)S(1)}, u32[]{:S(2)}, u32[]{:S(2)}) collective-permute-start(bf16[1,16,4096]{2,1,0:T(8,128)(2,1)S(1)} %get-tuple-element.32), channel_id=1, source_target_pairs={{0,1},{1,0},{2,3},{3,2},{4,5},{5,4},{6,7},{7,6},{8,9},{9,8},{10,11... | collective-permute-start | bytes 393224 | tf_op jit(solution)/shard_map/ppermute | solution.py:287
  44.7 1.5 %collective-permute-start.20 = (bf16[1,16,4096]{2,1,0:T(8,128)(2,1)S(1)}, bf16[1,16,4096]{2,1,0:T(8,128)(2,1)S(1)}, u32[]{:S(2)}, u32[]{:S(2)}) collective-permute-start(bf16[1,16,4096]{2,1,0:T(8,128)(2,1)S(1)} %get-tuple-element.31), channel_id=1, source_target_pairs={{0,1},{1,0},{2,3},{3,2},{4,5},{5,4},{6,7},{7,6},{8,9},{9,8},{10,11... | collective-permute-start | bytes 393224 | tf_op jit(solution)/shard_map/ppermute | solution.py:287
  47.7 4.7 %collective-permute-start.21 = (bf16[64,512]{1,0:T(8,128)(2,1)S(1)}, bf16[64,512]{1,0:T(8,128)(2,1)S(1)}, u32[]{:S(2)}, u32[]{:S(2)}) collective-permute-start(bf16[64,512]{1,0:T(8,128)(2,1)S(1)} %get-tuple-element.29), channel_id=1, source_target_pairs={{0,16},{1,17},{2,18},{3,19},{4,20},{5,21},{6,22},{7,23},{8,24},{9,... | collective-permute-start | bytes 196616 | tf_op jit(solution)/shard_map/ppermute | solution.py:287
  (1 other events, 2.7 us)

commit v4 on v3

--- a/solution.py
+++ b/solution.py
@@ -131,18 +131,25 @@
     )(pltpu.with_memory_space_constraint(train, pltpu.HBM))
 
 
-def score(turned, queries):
-    total = None
-    for l in range(len(turned)):
-        rows = jnp.concatenate([q[l] for q in queries], axis=0)
-        term = dot(rows, turned[l][...])
-        total = term if total is None else total + term
-    return total
-
-
-def score_parts(turned, more, a, b, swapped, low, high):
-    second = [q.at[1:] for q in (a, b, swapped)]
-    return score((turned,), [a, b, swapped, low]) + score((more,), second + [high])
+def layer_score(turned, rows):
+    rows = [row[...] for row in rows]
+    count = sum(row.shape[0] for row in rows)
+    rows = rows * max(1, 128 // count)
+    return dot(jnp.concatenate(rows, axis=0), turned[...])[:count]
+
+
+def pieces(unit, layer):
+    if not isinstance(unit, (list, tuple)):
+        return [unit.at[layer]]
+    half = len(unit) // 2
+    return [piece.at[0] for piece in unit[layer * half:(layer + 1) * half]]
+
+
+def score(turned, more, units):
+    return sum(
+        layer_score(t, [piece for unit in units for piece in pieces(unit, layer)])
+        for layer, t in enumerate((turned, more))
+    )
 
 
 def chip_at(offset):
@@ -181,37 +188,63 @@
 
 
 def plain_kernel(turned, more, *refs):
-    refs[-1][...] = score((turned, more), refs[:-1])
-
-
-def second_kernel(turned, more, *refs):
-    refs[-1][...] = score_parts(turned, more, *refs[:-1])
-
-
-def third_kernel(turned, more, first, second, *refs):
+    refs[-1][...] = score(turned, more, refs[:-1])
+
+
+def second_kernel(turned, more, own, *refs):
+    *queries, sent, kept, total = refs
+    half = kept.shape[0]
+    total[...] = score(turned, more, [*queries[:3], queries[3:]])
+    split(2, total.at[:half], total.at[half:], sent.at[:half], kept)
+    sent[half:] = own[...].astype(sent.dtype)
+
+
+def third_kernel(turned, more, first, *refs):
     *queries, sent, kept, total = refs
     half = total.shape[0] // 2
-    total[...] = score_parts(turned, more, *queries)
-    at = [pl.ds(n * half, half) for n in range(3)]
-    split(1, first.at[at[0]], total.at[at[1]], sent.at[at[0]], kept.at[at[0]])
-    split(2, second.at[at[0]], second.at[at[1]], sent.at[at[1]], kept.at[at[1]])
-    split(3, total.at[at[0]], first.at[at[1]], sent.at[at[2]], kept.at[at[2]])
-
-
-def fourth_kernel(turned, more, own, *refs):
-    a, low0, low1, high0, high1, sent, kept, total = refs
-    total[...] = score((turned,), [a, low0, low1]) + score((more,), [a.at[1:], high0, high1])
-    split(4, total, own, sent, kept)
-
-
-def block_call(kernel, name, rows, total, turned, operands, kind=jnp.float32):
+    total[...] = score(turned, more, [*queries[:3], queries[3:]])
+    split(1, first.at[:half], total.at[half:], sent.at[:half], kept.at[:half])
+    split(3, total.at[:half], first.at[half:], sent.at[half:2 * half], kept.at[half:])
+
+
+def opening_kernel(turned, *refs):
+    unit, *swapped, out = refs
+    out[...] = layer_score(turned, [unit.at[0]] + [ref.at[0] for ref in swapped])
+
+
+def second_layer(turned, opening, unit, swapped):
+    return opening[...] + layer_score(turned, [unit.at[1]] + [ref.at[0] for ref in swapped])
+
+
+def fourth_kernel(turned, opening, *refs):
+    unit, *swapped, sent = refs
+
+    @pl.when(foreign(4))
+    def _():
+        sent[...] = second_layer(turned, opening, unit, swapped).astype(sent.dtype)
+
+    @pl.when(jnp.logical_not(foreign(4)))
+    def _():
+        sent[...] = jnp.zeros_like(sent)
+
+
+def fifth_kernel(turned, opening, *refs):
+    unit, *swapped, kept = refs
+
+    @pl.when(jnp.logical_not(foreign(4)))
+    def _():
+        kept[...] = second_layer(turned, opening, unit, swapped)
+
+
+def block_call(kernel, name, rows, total, turned, operands, kind=jnp.float32, sent=0):
     columns = turned[0].shape[1]
     block = jax.ShapeDtypeStruct((rows, columns), jnp.float32)
+    one = total is None
     return pl.pallas_call(
         kernel,
-        out_shape=(jax.ShapeDtypeStruct(block.shape, kind), block) if total else block,
-        in_specs=[VMEM] * (2 + len(operands)),
-        out_specs=(VMEM, VMEM) if total else VMEM,
+        out_shape=(jax.ShapeDtypeStruct((max(rows, sent), columns), kind), block) if not one else jax.ShapeDtypeStruct(block.shape, kind),
+        in_specs=[VMEM] * (len(turned) + len(operands)),
+        out_specs=VMEM if one else (VMEM, VMEM),
         scratch_shapes=[pltpu.VMEM((total, columns), jnp.float32)] if total else [],
         compiler_params=pltpu.CompilerParams(vmem_limit_bytes=24 << 20),
         cost_estimate=pl.CostEstimate(flops=1 << 10, bytes_accessed=1 << 10, transcendentals=0),
@@ -219,11 +252,15 @@
     )(*turned, *operands)
 
 
-def gather_kernel(kept, got, out):
-    rows = kept.shape[0] // 3
-    for n in range(3):
-        offset = n + 1
-        block = kept[n * rows:(n + 1) * rows] + got[n * rows:(n + 1) * rows].astype(kept.dtype)
+def gather_kernel(kept2, got2, kept13, got13, own, out):
+    rows = kept2.shape[0]
+    low, high = pl.ds(0, rows), pl.ds(rows, rows)
+    for offset, kept, got in (
+        (2, kept2, got2.at[low]),
+        (1, kept13.at[low], got13.at[low]),
+        (3, kept13.at[high], got13.at[high]),
+    ):
+        block = kept[...] + got[...].astype(kept.dtype)
 
         @pl.when(foreign(offset))
         def _():
@@ -233,41 +270,54 @@
         def _():
             put(out, chip_at(offset), offset, block)
 
+    @pl.when(foreign(4))
+    def _():
+        put(out, chip_at(0), 0, own[...] + got2[high].astype(own.dtype))
+
 
 def last_kernel(kept, got, table, out, block, sems):
     del table
-    rows = kept.shape[0] // 2
-    block[...] = kept[...] + got[...].astype(kept.dtype)
-    at = jnp.where(foreign(4), chip_at(0), chip_at(4)) - 4 * lax.axis_index("layer")
-    core = lax.rem(lax.axis_index("row"), 2)
-    copies = []
-    for n, c in enumerate((core, 1 - core)):
-        start = pl.multiple_of((2 * at + c) * rows, rows)
-        copies.append(pltpu.make_async_copy(block.at[n * rows:(n + 1) * rows], out.at[pl.ds(start, rows)], sems.at[n]))
-    for copy in copies:
-        copy.start()
-    for copy in copies:
-        copy.wait()
-
-
-def finish(kept, got, kept4, got4, rows, columns):
-    hbm = pl.BlockSpec(memory_space=pl.ANY)
+
+    @pl.when(jnp.logical_not(foreign(4)))
+    def _():
+        rows = kept.shape[0] // 2
+        block[...] = kept[...] + got[...].astype(kept.dtype)
+        at = chip_at(4) - 4 * lax.axis_index("layer")
+        core = lax.rem(lax.axis_index("row"), 2)
+        copies = []
+        for n, c in enumerate((core, 1 - core)):
+            start = pl.multiple_of((2 * at + c) * rows, rows)
+            copies.append(
+                pltpu.make_async_copy(block.at[n * rows:(n + 1) * rows], out.at[pl.ds(start, rows)], sems.at[n])
+            )
+        for copy in copies:
+            copy.start()
+        for copy in copies:
+            copy.wait()
+
+
+def finish(most, last, rows, columns):
     table = jax.ShapeDtypeStruct((rows, columns), jnp.float32)
     params = pltpu.CompilerParams(vmem_limit_bytes=8 << 20)
-    most = pl.pallas_call(
-        gather_kernel, out_shape=table, in_specs=[VMEM] * 2, out_specs=VMEM, compiler_params=params, name="gather_rows",
+    gathered = pl.pallas_call(
+        gather_kernel,
+        out_shape=table,
+        in_specs=[VMEM] * 5,
+        out_specs=VMEM,
+        compiler_params=params,
         cost_estimate=pl.CostEstimate(flops=60 << 30, bytes_accessed=1 << 20, transcendentals=0),
-    )(kept, got)
+        name="gather_rows",
+    )(*most)
     return pl.pallas_call(
         last_kernel,
         out_shape=table,
-        in_specs=[VMEM, VMEM, hbm],
-        out_specs=hbm,
-        scratch_shapes=[pltpu.VMEM(kept4.shape, jnp.float32), pltpu.SemaphoreType.DMA((2,))],
+        in_specs=[VMEM, VMEM, HBM],
+        out_specs=HBM,
+        scratch_shapes=[pltpu.VMEM(last[0].shape, jnp.float32), pltpu.SemaphoreType.DMA((2,))],
         input_output_aliases={2: 0},
         compiler_params=params,
         name="last_rows",
-    )(kept4, got4, most)
+    )(*last, gathered)
 
 
 def ring_order(chips):
@@ -287,6 +337,13 @@
     send = lambda v, pairs: lax.ppermute(v, AXES, pairs)
 
     after = lax.optimization_barrier
+    def quarters(unit):
+        layers, held, feat = unit.shape
+        half = held // 2
+        return [send(unit[l:l + 1, n:n + half], swap) for l in range(layers) for n in (0, half)]
+
+    halves_of = lambda unit: [send(unit[l:l + 1], swap) for l in range(unit.shape[0])]
+
     arrived = [send(query_grads, around), send(send(query_grads, swap), around)]
     mine = precondition(query_grads, left_inverse, right_inverse, True)
     a, b = [mine], [send(mine, swap)]
@@ -295,23 +352,29 @@
     a.append(precondition(arrived[0], left_inverse, right_inverse, False))
     b.append(precondition(arrived[1], left_inverse, right_inverse, False))
     rows = 2 * mine.shape[1]
-    zeroth = block_call(plain_kernel, "scores_0", rows, 0, turned, [a[0], b[0]])
+    zeroth = block_call(plain_kernel, "scores_0", rows, None, turned, [a[0], b[0]])
     a.append(send(a[1], around))
     b.append(send(b[1], around))
-    first = block_call(plain_kernel, "scores_1", 2 * rows, 0, turned, [a[1], b[1], send(a[1], swap), send(b[1], swap)])
+    first = block_call(plain_kernel, "scores_1", 2 * rows, None, turned, [a[1], b[1], send(a[1], swap), send(b[1], swap)])
     a.append(send(a[2], around))
     b[2], first, _ = after((b[2], first, mine))
     b.append(send(b[2], around))
-    second = block_call(second_kernel, "scores_2", 2 * rows, 0, turned, [a[2], b[2], send(a[2], swap), *(send(b[2][l:l + 1], swap) for l in range(2))])
-    a[3], second, zeroth = after((a[3], second, zeroth))
+    queries = [a[2], b[2], send(a[2], swap), *halves_of(b[2])]
+    sent2, kept2 = block_call(second_kernel, "scores_2", rows, 2 * rows, turned, [zeroth] + queries, jnp.bfloat16, 2 * rows)
+    a[3], _ = after((a[3], sent2))
     a.append(send(a[3], around))
-    queries = [a[3], b[3], send(a[3], swap), *(send(b[3][l:l + 1], swap) for l in range(2))]
-    sent, kept = block_call(third_kernel, "scores_3", 3 * rows, 2 * rows, turned, [first, second] + queries, jnp.bfloat16)
+    got2 = send(sent2, across)
+    b[3], got2 = after((b[3], got2))
+    queries = [a[3], b[3], send(a[3], swap), *halves_of(b[3])]
+    sent, kept = block_call(third_kernel, "scores_3", 2 * rows, 2 * rows, turned, [first] + queries, jnp.bfloat16, 2 * rows + 32)
+    got = send(sent, across)
     a[4], _ = after((a[4], sent))
-    got = send(sent, across)
-    end = [a[4], *(send(a[4][l:l + 1, 16 * n:16 * n + 16], swap) for l in range(2) for n in range(2))]
-    sent4, kept4 = block_call(fourth_kernel, "scores_4", rows, rows, turned, [zeroth, *end], jnp.bfloat16)
-    return finish(kept, got, kept4, send(sent4, across), chips // groups * rows, turned[0].shape[1])
+    swapped = quarters(a[4])
+    opening = block_call(opening_kernel, "scores_4", rows, None, turned[:1], [a[4], *swapped[:2]])
+    sent4 = block_call(fourth_kernel, "scores_5", rows, None, turned[1:], [opening, a[4], *swapped[2:]], jnp.bfloat16)
+    got4 = send(sent4, across)
+    kept4 = block_call(fifth_kernel, "scores_6", rows, None, turned[1:], [opening, a[4], *swapped[2:]])
+    return finish((kept2, got2, kept, got, zeroth), (kept4, got4), chips // groups * rows, turned[0].shape[1])
 
 
 def on_device(query_grads, train_grads, left_inverse, right_inverse):

time: 53.3 us -> 51.9 us (0.974)
  waiting for transfers between devices: 10.8 us -> 9.75 us
  Pallas kernels: 19.8 us -> 18.9 us
    ppermute x23 -> x24, waiting for transfers between devices: 10.8 us -> 9.75 us  [ring_device(): send = lambda v, pairs: lax.ppermute(v, AXES, pairs)]
    pallas_call x7 -> x9, Pallas kernels: 8.55 us -> 7.67 us  [the longest x7 6.71 us: block_call(): pl.pallas_call(kernel, out_shape=(jax.ShapeDtypeStruct((max(rows, sent),...]
    ppermute x23 -> x24, starting transfers between devices: 22.2 us -> 22.6 us  [ring_device(): send = lambda v, pairs: lax.ppermute(v, AXES, pairs)]
  transfers between devices with their start and end apart: 23 -> 24, of which waited for: 12 -> 10; matrix products, arithmetic and copies ran while one was open for 0% -> 0% of each run, Pallas kernels for 36% -> 37%
where the time goes in v4:
time: 51.9 us; the launch traced here: 51.7 us
  starting transfers between devices  22.6 us (44%)
  Pallas kernels  18.9 us (36%)
  waiting for transfers between devices  9.75 us (19%)
    ppermute x24, starting transfers between devices, ring_device(): send = lambda v, pairs: lax.ppermute(v, AXES, pairs)  22.6 us
    ppermute x24, waiting for transfers between devices, ring_device(): send = lambda v, pairs: lax.ppermute(v, AXES, pairs)  9.75 us
    pallas_call x7, Pallas kernels, block_call(): pl.pallas_call(kernel, out_shape=(jax.ShapeDtypeStruct((max(rows, sent),...  6.71 us
    pallas_call x3, Pallas kernels, precondition(): pl.pallas_call(precondition_first_kernel if first else precondition_kerne...  5.92 us
    pallas_call x2, Pallas kernels, transpose(): pl.pallas_call(functools.partial(transpose_kernel, layer), out_shape=pltp...  5.31 us
  transfers between devices with their start and end apart: 24, of which 10 were waited for; matrix products, arithmetic and copies ran while one was open for 0% of the time, Pallas kernels for 37%

profile of v4, /device:TPU:0, one launch (start us, length us, event | category | flops | bytes accessed | tf_op | source)
XLA Modules:
  0.0 51.7 jit_solution(14805419369870223552)
XLA Ops:
  0.5 2.6 %collective-permute-start = (bf16[2,32,4096]{2,1,0:T(8,128)(2,1)}, bf16[2,32,4096]{2,1,0:T(8,128)(2,1)S(1)}, u32[]{:S(2)}, u32[]{:S(2)}) collective-permute-start(bf16[2,32,4096]{2,1,0:T(8,128)(2,1)} %query_hbm.1), channel_id=1, source_target_pairs={{0,4},{1,3},{2,0},{3,7},{4,8},{5,1},{6,2},{7,11},{8,12},{9,5},{10,... | collective-permute-start | bytes 1572872 | tf_op jit(solution)/shard_map/ppermute | solution.py:337
  3.0 2.1 %collective-permute-start.5 = (bf16[2,32,4096]{2,1,0:T(8,128)(2,1)S(1)}, bf16[2,32,4096]{2,1,0:T(8,128)(2,1)S(1)}, u32[]{:S(2)}, u32[]{:S(2)}) collective-permute-start(bf16[2,32,4096]{2,1,0:T(8,128)(2,1)S(1)} %collective-permute-done.4), channel_id=1, source_target_pairs={{0,4},{1,3},{2,0},{3,7},{4,8},{5,1},{6,2},{7,11},{8,12},{9,5},{10,... | collective-permute-start | bytes 1572872 | tf_op jit(solution)/shard_map/ppermute | solution.py:337
  5.1 2.6 %transpose_0.1.turned = bf16[4096,512]{1,0:T(8,128)(2,1)S(1)} custom-call(bf16[2,512,4096]{2,1,0:T(8,128)(2,1)} %train.3), custom_call_target="tpu_custom_call" | custom-call | flops 2147483648 | bytes 8388608 | tf_op jit(solution)/shard_map/transpose_0/pallas_call | solution.py:122
  7.8 2.7 %transpose_1.1.more.turned = bf16[4096,512]{1,0:T(8,128)(2,1)S(1)} custom-call(bf16[2,512,4096]{2,1,0:T(8,128)(2,1)} %train.3), custom_call_target="tpu_custom_call" | custom-call | flops 2147483648 | bytes 8388608 | tf_op jit(solution)/shard_map/transpose_1/pallas_call | solution.py:122
  10.5 1.6 %precondition_1.2.refs_0_ = bf16[2,32,4096]{2,1,0:T(8,128)(2,1)S(1)} custom-call(bf16[2,32,4096]{2,1,0:T(8,128)(2,1)S(1)} %collective-permute-done.query, f32[2,64,64]{2,1,0:T(8,128)S(1)} %copy-done, f32[2,64,64]{2,1,0:T(8,128)S(1)} %copy-done.1), custom_call_target="tpu_custom_call" | custom-call | flops 2147483648 | bytes 4194304 | tf_op jit(solution)/shard_map/precondition_1/pallas_call | solution.py:90
  12.2 2.0 %collective-permute-start.1 = (bf16[2,32,4096]{2,1,0:T(8,128)(2,1)S(1)}, bf16[2,32,4096]{2,1,0:T(8,128)(2,1)S(1)}, u32[]{:S(2)}, u32[]{:S(2)}) collective-permute-start(bf16[2,32,4096]{2,1,0:T(8,128)(2,1)S(1)} %precondition_1.2.refs_0_), channel_id=1, source_target_pairs={{0,4},{1,3},{2,0},{3,7},{4,8},{5,1},{6,2},{7,11},{8,12},{9,5},{10,... | collective-permute-start | bytes 1572872 | tf_op jit(solution)/shard_map/ppermute | solution.py:337
  14.2 1.8 %collective-permute-done.5.query = bf16[2,32,4096]{2,1,0:T(8,128)(2,1)S(1)} collective-permute-done((bf16[2,32,4096]{2,1,0:T(8,128)(2,1)S(1)}, bf16[2,32,4096]{2,1,0:T(8,128)(2,1)S(1)}, u32[]{:S(2)}, u32[]{:S(2)}) %collective-permute-start.5) | collective-permute-done | bytes 524320 | tf_op jit(solution)/shard_map/ppermute | solution.py:337
  15.9 1.6 %precondition_1.3.refs_1_ = bf16[2,32,4096]{2,1,0:T(8,128)(2,1)S(1)} custom-call(bf16[2,32,4096]{2,1,0:T(8,128)(2,1)S(1)} %collective-permute-done.5.query, f32[2,64,64]{2,1,0:T(8,128)S(1)} %copy-done, f32[2,64,64]{2,1,0:T(8,128)S(1)} %copy-done.1), custom_call_target="tpu_custom_call" | custom-call | flops 2147483648 | bytes 4194304 | tf_op jit(solution)/shard_map/precondition_1/pallas_call | solution.py:90
  17.6 2.2 %collective-permute-start.6 = (bf16[2,32,4096]{2,1,0:T(8,128)(2,1)S(1)}, bf16[2,32,4096]{2,1,0:T(8,128)(2,1)S(1)}, u32[]{:S(2)}, u32[]{:S(2)}) collective-permute-start(bf16[2,32,4096]{2,1,0:T(8,128)(2,1)S(1)} %precondition_1.3.refs_1_), channel_id=1, source_target_pairs={{0,4},{1,3},{2,0},{3,7},{4,8},{5,1},{6,2},{7,11},{8,12},{9,5},{10,... | collective-permute-start | bytes 1572872 | tf_op jit(solution)/shard_map/ppermute | solution.py:337
  19.8 2.7 %precondition_0.1.refs_0_ = bf16[2,32,4096]{2,1,0:T(8,128)(2,1)S(1)} custom-call(bf16[2,32,4096]{2,1,0:T(8,128)(2,1)} %query_hbm.1, f32[2,64,64]{2,1,0:T(8,128)} %left.3, f32[2,64,64]{2,1,0:T(8,128)} %right.3), custom_call_target="tpu_custom_call" | custom-call | flops 2147483648 | bytes 4194304 | tf_op jit(solution)/shard_map/precondition_0/pallas_call | solution.py:90
  23.1 1.6 %collective-permute-start.2 = (bf16[2,32,4096]{2,1,0:T(8,128)(2,1)S(1)}, bf16[2,32,4096]{2,1,0:T(8,128)(2,1)S(1)}, u32[]{:S(2)}, u32[]{:S(2)}) collective-permute-start(bf16[2,32,4096]{2,1,0:T(8,128)(2,1)S(1)} %collective-permute-done.1.refs_0_), channel_id=1, source_target_pairs={{0,4},{1,3},{2,0},{3,7},{4,8},{5,1},{6,2},{7,11},{8,12},{9,5},{10,... | collective-permute-start | bytes 1572872 | tf_op jit(solution)/shard_map/ppermute | solution.py:337
  24.7 1.2 %scores_1.1.first = f32[128,512]{1,0:T(8,128)S(1)} custom-call(bf16[4096,512]{1,0:T(8,128)(2,1)S(1)} %transpose_0.1.turned, bf16[4096,512]{1,0:T(8,128)(2,1)S(1)} %transpose_1.1.more.turned, bf16[2,32,4096]{2,1,0:T(8,128)(2,1)S(1)} %precondition_1.2.refs_0_, bf16[2,32,4096]{2,1,0:T(8,128)(2,1)S(1)} %precondition_1.3.refs_1_, ...), custom_call_target="tpu_custom_call" | custom-call | flops 1024 | bytes 1024 | tf_op jit(solution)/shard_map/scores_1/pallas_call | solution.py:243
  25.9 1.2 %collective-permute-done.6.refs_1_ = bf16[2,32,4096]{2,1,0:T(8,128)(2,1)S(1)} collective-permute-done((bf16[2,32,4096]{2,1,0:T(8,128)(2,1)S(1)}, bf16[2,32,4096]{2,1,0:T(8,128)(2,1)S(1)}, u32[]{:S(2)}, u32[]{:S(2)}) %collective-permute-start.6) | collective-permute-done | bytes 524320 | tf_op jit(solution)/shard_map/ppermute | solution.py:337
  27.2 2.1 %collective-permute-start.13 = (bf16[2,32,4096]{2,1,0:T(8,128)(2,1)S(1)}, bf16[2,32,4096]{2,1,0:T(8,128)(2,1)S(1)}, u32[]{:S(2)}, u32[]{:S(2)}) collective-permute-start(bf16[2,32,4096]{2,1,0:T(8,128)(2,1)S(1)} %collective-permute-done.6.refs_1_), channel_id=1, source_target_pairs={{0,4},{1,3},{2,0},{3,7},{4,8},{5,1},{6,2},{7,11},{8,12},{9,5},{10,... | collective-permute-start | bytes 1572872 | tf_op jit(solution)/shard_map/ppermute | solution.py:337
  29.9 1.2 %scores_0.1.own = f32[64,512]{1,0:T(8,128)S(1)} custom-call(bf16[4096,512]{1,0:T(8,128)(2,1)S(1)} %transpose_0.1.turned, bf16[4096,512]{1,0:T(8,128)(2,1)S(1)} %transpose_1.1.more.turned, bf16[2,32,4096]{2,1,0:T(8,128)(2,1)S(1)} %precondition_0.1.refs_0_, bf16[2,32,4096]{2,1,0:T(8,128)(2,1)S(1)} %collective-permute-done.3.refs_1_), custom_call_target="tpu_custom_call" | custom-call | flops 1024 | bytes 1024 | tf_op jit(solution)/shard_map/scores_0/pallas_call | solution.py:243
  31.3 1.3 %scores_2.1 = (bf16[128,512]{1,0:T(8,128)(2,1)S(1)}, f32[64,512]{1,0:T(8,128)S(1)}) custom-call(bf16[4096,512]{1,0:T(8,128)(2,1)S(1)} %transpose_0.1.turned, bf16[4096,512]{1,0:T(8,128)(2,1)S(1)} %transpose_1.1.more.turned, f32[64,512]{1,0:T(8,128)S(1)} %scores_0.1.own, bf16[2,32,4096]{2,1,0:T(8,128)(2,1)S(1)} %collective-permute-done.1.refs_0_, ...), custom_call_target="tpu_custom_call" | custom-call | flops 1024 | bytes 1024 | tf_op jit(solution)/shard_map/scores_2/pallas_call | solution.py:243
  32.6 1.6 %collective-permute-start.14 = (bf16[128,512]{1,0:T(8,128)(2,1)S(1)}, bf16[128,512]{1,0:T(8,128)(2,1)S(1)}, u32[]{:S(2)}, u32[]{:S(2)}) collective-permute-start(bf16[128,512]{1,0:T(8,128)(2,1)S(1)} %get-tuple-element.22), channel_id=1, source_target_pairs={{0,16},{1,17},{2,18},{3,19},{4,20},{5,21},{6,22},{7,23},{8,24},{9,... | collective-permute-start | bytes 393224 | tf_op jit(solution)/shard_map/ppermute | solution.py:337
  34.2 1.6 %collective-permute-start.12 = (bf16[2,32,4096]{2,1,0:T(8,128)(2,1)S(1)}, bf16[2,32,4096]{2,1,0:T(8,128)(2,1)S(1)}, u32[]{:S(2)}, u32[]{:S(2)}) collective-permute-start(bf16[2,32,4096]{2,1,0:T(8,128)(2,1)S(1)} %collective-permute-done.2.refs_0_), channel_id=1, source_target_pairs={{0,4},{1,3},{2,0},{3,7},{4,8},{5,1},{6,2},{7,11},{8,12},{9,5},{10,... | collective-permute-start | bytes 1572872 | tf_op jit(solution)/shard_map/ppermute | solution.py:337
  35.7 2.4 %collective-permute-done.14.got2 = bf16[128,512]{1,0:T(8,128)(2,1)S(1)} collective-permute-done((bf16[128,512]{1,0:T(8,128)(2,1)S(1)}, bf16[128,512]{1,0:T(8,128)(2,1)S(1)}, u32[]{:S(2)}, u32[]{:S(2)}) %collective-permute-start.14) | collective-permute-done | bytes 131104 | tf_op jit(solution)/shard_map/ppermute | solution.py:337
  39.0 1.0 %collective-permute-done.16.refs_3_ = bf16[1,32,4096]{2,1,0:T(8,128)(2,1)S(1)} collective-permute-done((bf16[1,32,4096]{2,1,0:T(8,128)(2,1)S(1)}, bf16[1,32,4096]{2,1,0:T(8,128)(2,1)S(1)}, u32[]{:S(2)}, u32[]{:S(2)}) %collective-permute-start.16) | collective-permute-done | bytes 262176 | tf_op jit(solution)/shard_map/ppermute | solution.py:337
  40.4 1.5 %scores_3.1 = (bf16[160,512]{1,0:T(8,128)(2,1)S(1)}, f32[128,512]{1,0:T(8,128)S(1)}) custom-call(bf16[4096,512]{1,0:T(8,128)(2,1)S(1)} %transpose_0.1.turned, bf16[4096,512]{1,0:T(8,128)(2,1)S(1)} %transpose_1.1.more.turned, f32[128,512]{1,0:T(8,128)S(1)} %scores_1.1.first, bf16[2,32,4096]{2,1,0:T(8,128)(2,1)S(1)} %collective-permute-done.2.refs_0_, ...), custom_call_target="tpu_custom_call" | custom-call | flops 1024 | bytes 1024 | tf_op jit(solution)/shard_map/scores_3/pallas_call | solution.py:243
  41.9 2.1 %collective-permute-start.23 = (bf16[160,512]{1,0:T(8,128)(2,1)S(1)}, bf16[160,512]{1,0:T(8,128)(2,1)S(1)}, u32[]{:S(2)}, u32[]{:S(2)}) collective-permute-start(bf16[160,512]{1,0:T(8,128)(2,1)S(1)} %get-tuple-element.26), channel_id=1, source_target_pairs={{0,16},{1,17},{2,18},{3,19},{4,20},{5,21},{6,22},{7,23},{8,24},{9,... | collective-permute-start | bytes 491528 | tf_op jit(solution)/shard_map/ppermute | solution.py:337
  47.2 1.4 %collective-permute-start.22 = (bf16[64,512]{1,0:T(8,128)(2,1)S(1)}, bf16[64,512]{1,0:T(8,128)(2,1)S(1)}, u32[]{:S(2)}, u32[]{:S(2)}) collective-permute-start(bf16[64,512]{1,0:T(8,128)(2,1)S(1)} %scores_5.1), channel_id=1, source_target_pairs={{0,16},{1,17},{2,18},{3,19},{4,20},{5,21},{6,22},{7,23},{8,24},{9,... | collective-permute-start | bytes 196616 | tf_op jit(solution)/shard_map/ppermute | solution.py:337
  49.5 2.0 %collective-permute-done.22.got = bf16[64,512]{1,0:T(8,128)(2,1)S(1)} collective-permute-done((bf16[64,512]{1,0:T(8,128)(2,1)S(1)}, bf16[64,512]{1,0:T(8,128)(2,1)S(1)}, u32[]{:S(2)}, u32[]{:S(2)}) %collective-permute-start.22) | collective-permute-done | bytes 65568 | tf_op jit(solution)/shard_map/ppermute | solution.py:337
  (45 shorter events, 7.2 us)
Async XLA Ops:
  0.0 3.0 %collective-permute-start.4 = (bf16[2,32,4096]{2,1,0:T(8,128)(2,1)}, bf16[2,32,4096]{2,1,0:T(8,128)(2,1)S(1)}, u32[]{:S(2)}, u32[]{:S(2)}) collective-permute-start(bf16[2,32,4096]{2,1,0:T(8,128)(2,1)} %query_hbm.1), channel_id=1, source_target_pairs={{0,1},{1,0},{2,3},{3,2},{4,5},{5,4},{6,7},{7,6},{8,9},{9,8},{10,11... | collective-permute-start | bytes 1572872 | tf_op jit(solution)/shard_map/ppermute | solution.py:337
  0.5 10.0 %collective-permute-start = (bf16[2,32,4096]{2,1,0:T(8,128)(2,1)}, bf16[2,32,4096]{2,1,0:T(8,128)(2,1)S(1)}, u32[]{:S(2)}, u32[]{:S(2)}) collective-permute-start(bf16[2,32,4096]{2,1,0:T(8,128)(2,1)} %query_hbm.1), channel_id=1, source_target_pairs={{0,4},{1,3},{2,0},{3,7},{4,8},{5,1},{6,2},{7,11},{8,12},{9,5},{10,... | collective-permute-start | bytes 1572872 | tf_op jit(solution)/shard_map/ppermute | solution.py:337
  3.0 12.9 %collective-permute-start.5 = (bf16[2,32,4096]{2,1,0:T(8,128)(2,1)S(1)}, bf16[2,32,4096]{2,1,0:T(8,128)(2,1)S(1)}, u32[]{:S(2)}, u32[]{:S(2)}) collective-permute-start(bf16[2,32,4096]{2,1,0:T(8,128)(2,1)S(1)} %collective-permute-done.4), channel_id=1, source_target_pairs={{0,4},{1,3},{2,0},{3,7},{4,8},{5,1},{6,2},{7,11},{8,12},{9,5},{10,... | collective-permute-start | bytes 1572872 | tf_op jit(solution)/shard_map/ppermute | solution.py:337
  12.1 11.0 %collective-permute-start.7 = (bf16[2,32,4096]{2,1,0:T(8,128)(2,1)S(1)}, bf16[2,32,4096]{2,1,0:T(8,128)(2,1)S(1)}, u32[]{:S(2)}, u32[]{:S(2)}) collective-permute-start(bf16[2,32,4096]{2,1,0:T(8,128)(2,1)S(1)} %precondition_1.2.refs_0_), channel_id=1, source_target_pairs={{0,1},{1,0},{2,3},{3,2},{4,5},{5,4},{6,7},{7,6},{8,9},{9,8},{10,11... | collective-permute-start | bytes 1572872 | tf_op jit(solution)/shard_map/ppermute | solution.py:337
  12.2 10.4 %collective-permute-start.1 = (bf16[2,32,4096]{2,1,0:T(8,128)(2,1)S(1)}, bf16[2,32,4096]{2,1,0:T(8,128)(2,1)S(1)}, u32[]{:S(2)}, u32[]{:S(2)}) collective-permute-start(bf16[2,32,4096]{2,1,0:T(8,128)(2,1)S(1)} %precondition_1.2.refs_0_), channel_id=1, source_target_pairs={{0,4},{1,3},{2,0},{3,7},{4,8},{5,1},{6,2},{7,11},{8,12},{9,5},{10,... | collective-permute-start | bytes 1572872 | tf_op jit(solution)/shard_map/ppermute | solution.py:337
  17.5 7.1 %collective-permute-start.8 = (bf16[2,32,4096]{2,1,0:T(8,128)(2,1)S(1)}, bf16[2,32,4096]{2,1,0:T(8,128)(2,1)S(1)}, u32[]{:S(2)}, u32[]{:S(2)}) collective-permute-start(bf16[2,32,4096]{2,1,0:T(8,128)(2,1)S(1)} %precondition_1.3.refs_1_), channel_id=1, source_target_pairs={{0,1},{1,0},{2,3},{3,2},{4,5},{5,4},{6,7},{7,6},{8,9},{9,8},{10,11... | collective-permute-start | bytes 1572872 | tf_op jit(solution)/shard_map/ppermute | solution.py:337
  17.6 9.5 %collective-permute-start.6 = (bf16[2,32,4096]{2,1,0:T(8,128)(2,1)S(1)}, bf16[2,32,4096]{2,1,0:T(8,128)(2,1)S(1)}, u32[]{:S(2)}, u32[]{:S(2)}) collective-permute-start(bf16[2,32,4096]{2,1,0:T(8,128)(2,1)S(1)} %precondition_1.3.refs_1_), channel_id=1, source_target_pairs={{0,4},{1,3},{2,0},{3,7},{4,8},{5,1},{6,2},{7,11},{8,12},{9,5},{10,... | collective-permute-start | bytes 1572872 | tf_op jit(solution)/shard_map/ppermute | solution.py:337
  22.5 6.9 %collective-permute-start.3 = (bf16[2,32,4096]{2,1,0:T(8,128)(2,1)S(1)}, bf16[2,32,4096]{2,1,0:T(8,128)(2,1)S(1)}, u32[]{:S(2)}, u32[]{:S(2)}) collective-permute-start(bf16[2,32,4096]{2,1,0:T(8,128)(2,1)S(1)} %precondition_0.1.refs_0_), channel_id=1, source_target_pairs={{0,1},{1,0},{2,3},{3,2},{4,5},{5,4},{6,7},{7,6},{8,9},{9,8},{10,11... | collective-permute-start | bytes 1572872 | tf_op jit(solution)/shard_map/ppermute | solution.py:337
  22.7 8.5 %collective-permute-start.9 = (bf16[2,32,4096]{2,1,0:T(8,128)(2,1)S(1)}, bf16[2,32,4096]{2,1,0:T(8,128)(2,1)S(1)}, u32[]{:S(2)}, u32[]{:S(2)}) collective-permute-start(bf16[2,32,4096]{2,1,0:T(8,128)(2,1)S(1)} %collective-permute-done.1.refs_0_), channel_id=1, source_target_pairs={{0,1},{1,0},{2,3},{3,2},{4,5},{5,4},{6,7},{7,6},{8,9},{9,8},{10,11... | collective-permute-start | bytes 1572872 | tf_op jit(solution)/shard_map/ppermute | solution.py:337
  23.1 11.1 %collective-permute-start.2 = (bf16[2,32,4096]{2,1,0:T(8,128)(2,1)S(1)}, bf16[2,32,4096]{2,1,0:T(8,128)(2,1)S(1)}, u32[]{:S(2)}, u32[]{:S(2)}) collective-permute-start(bf16[2,32,4096]{2,1,0:T(8,128)(2,1)S(1)} %collective-permute-done.1.refs_0_), channel_id=1, source_target_pairs={{0,4},{1,3},{2,0},{3,7},{4,8},{5,1},{6,2},{7,11},{8,12},{9,5},{10,... | collective-permute-start | bytes 1572872 | tf_op jit(solution)/shard_map/ppermute | solution.py:337
  27.2 11.2 %collective-permute-start.13 = (bf16[2,32,4096]{2,1,0:T(8,128)(2,1)S(1)}, bf16[2,32,4096]{2,1,0:T(8,128)(2,1)S(1)}, u32[]{:S(2)}, u32[]{:S(2)}) collective-permute-start(bf16[2,32,4096]{2,1,0:T(8,128)(2,1)S(1)} %collective-permute-done.6.refs_1_), channel_id=1, source_target_pairs={{0,4},{1,3},{2,0},{3,7},{4,8},{5,1},{6,2},{7,11},{8,12},{9,5},{10,... | collective-permute-start | bytes 1572872 | tf_op jit(solution)/shard_map/ppermute | solution.py:337
  29.3 1.8 %collective-permute-start.10 = (bf16[1,32,4096]{2,1,0:T(8,128)(2,1)S(1)}, bf16[1,32,4096]{2,1,0:T(8,128)(2,1)S(1)}, u32[]{:S(2)}, u32[]{:S(2)}) collective-permute-start(bf16[1,32,4096]{2,1,0:T(8,128)(2,1)S(1)} %get-tuple-element.38), channel_id=1, source_target_pairs={{0,1},{1,0},{2,3},{3,2},{4,5},{5,4},{6,7},{7,6},{8,9},{9,8},{10,11... | collective-permute-start | bytes 786440 | tf_op jit(solution)/shard_map/ppermute | solution.py:337
  29.4 1.9 %collective-permute-start.11 = (bf16[1,32,4096]{2,1,0:T(8,128)(2,1)S(1)}, bf16[1,32,4096]{2,1,0:T(8,128)(2,1)S(1)}, u32[]{:S(2)}, u32[]{:S(2)}) collective-permute-start(bf16[1,32,4096]{2,1,0:T(8,128)(2,1)S(1)} %get-tuple-element.37), channel_id=1, source_target_pairs={{0,1},{1,0},{2,3},{3,2},{4,5},{5,4},{6,7},{7,6},{8,9},{9,8},{10,11... | collective-permute-start | bytes 786440 | tf_op jit(solution)/shard_map/ppermute | solution.py:337
  32.6 5.6 %collective-permute-start.14 = (bf16[128,512]{1,0:T(8,128)(2,1)S(1)}, bf16[128,512]{1,0:T(8,128)(2,1)S(1)}, u32[]{:S(2)}, u32[]{:S(2)}) collective-permute-start(bf16[128,512]{1,0:T(8,128)(2,1)S(1)} %get-tuple-element.22), channel_id=1, source_target_pairs={{0,16},{1,17},{2,18},{3,19},{4,20},{5,21},{6,22},{7,23},{8,24},{9,... | collective-permute-start | bytes 393224 | tf_op jit(solution)/shard_map/ppermute | solution.py:337
  34.2 6.3 %collective-permute-start.15 = (bf16[2,32,4096]{2,1,0:T(8,128)(2,1)S(1)}, bf16[2,32,4096]{2,1,0:T(8,128)(2,1)S(1)}, u32[]{:S(2)}, u32[]{:S(2)}) collective-permute-start(bf16[2,32,4096]{2,1,0:T(8,128)(2,1)S(1)} %collective-permute-done.2.refs_0_), channel_id=1, source_target_pairs={{0,1},{1,0},{2,3},{3,2},{4,5},{5,4},{6,7},{7,6},{8,9},{9,8},{10,11... | collective-permute-start | bytes 1572872 | tf_op jit(solution)/shard_map/ppermute | solution.py:337
  34.2 9.9 %collective-permute-start.12 = (bf16[2,32,4096]{2,1,0:T(8,128)(2,1)S(1)}, bf16[2,32,4096]{2,1,0:T(8,128)(2,1)S(1)}, u32[]{:S(2)}, u32[]{:S(2)}) collective-permute-start(bf16[2,32,4096]{2,1,0:T(8,128)(2,1)S(1)} %collective-permute-done.2.refs_0_), channel_id=1, source_target_pairs={{0,4},{1,3},{2,0},{3,7},{4,8},{5,1},{6,2},{7,11},{8,12},{9,5},{10,... | collective-permute-start | bytes 1572872 | tf_op jit(solution)/shard_map/ppermute | solution.py:337
  38.4 1.6 %collective-permute-start.16 = (bf16[1,32,4096]{2,1,0:T(8,128)(2,1)S(1)}, bf16[1,32,4096]{2,1,0:T(8,128)(2,1)S(1)}, u32[]{:S(2)}, u32[]{:S(2)}) collective-permute-start(bf16[1,32,4096]{2,1,0:T(8,128)(2,1)S(1)} %get-tuple-element.36), channel_id=1, source_target_pairs={{0,1},{1,0},{2,3},{3,2},{4,5},{5,4},{6,7},{7,6},{8,9},{9,8},{10,11... | collective-permute-start | bytes 786440 | tf_op jit(solution)/shard_map/ppermute | solution.py:337
  38.5 1.9 %collective-permute-start.17 = (bf16[1,32,4096]{2,1,0:T(8,128)(2,1)S(1)}, bf16[1,32,4096]{2,1,0:T(8,128)(2,1)S(1)}, u32[]{:S(2)}, u32[]{:S(2)}) collective-permute-start(bf16[1,32,4096]{2,1,0:T(8,128)(2,1)S(1)} %get-tuple-element.35), channel_id=1, source_target_pairs={{0,1},{1,0},{2,3},{3,2},{4,5},{5,4},{6,7},{7,6},{8,9},{9,8},{10,11... | collective-permute-start | bytes 786440 | tf_op jit(solution)/shard_map/ppermute | solution.py:337
  41.9 6.7 %collective-permute-start.23 = (bf16[160,512]{1,0:T(8,128)(2,1)S(1)}, bf16[160,512]{1,0:T(8,128)(2,1)S(1)}, u32[]{:S(2)}, u32[]{:S(2)}) collective-permute-start(bf16[160,512]{1,0:T(8,128)(2,1)S(1)} %get-tuple-element.26), channel_id=1, source_target_pairs={{0,16},{1,17},{2,18},{3,19},{4,20},{5,21},{6,22},{7,23},{8,24},{9,... | collective-permute-start | bytes 491528 | tf_op jit(solution)/shard_map/ppermute | solution.py:337
  44.1 1.4 %collective-permute-start.18 = (bf16[1,16,4096]{2,1,0:T(8,128)(2,1)S(1)}, bf16[1,16,4096]{2,1,0:T(8,128)(2,1)S(1)}, u32[]{:S(2)}, u32[]{:S(2)}) collective-permute-start(bf16[1,16,4096]{2,1,0:T(8,128)(2,1)S(1)} %get-tuple-element.34), channel_id=1, source_target_pairs={{0,1},{1,0},{2,3},{3,2},{4,5},{5,4},{6,7},{7,6},{8,9},{9,8},{10,11... | collective-permute-start | bytes 393224 | tf_op jit(solution)/shard_map/ppermute | solution.py:337
  44.1 1.5 %collective-permute-start.19 = (bf16[1,16,4096]{2,1,0:T(8,128)(2,1)S(1)}, bf16[1,16,4096]{2,1,0:T(8,128)(2,1)S(1)}, u32[]{:S(2)}, u32[]{:S(2)}) collective-permute-start(bf16[1,16,4096]{2,1,0:T(8,128)(2,1)S(1)} %get-tuple-element.33), channel_id=1, source_target_pairs={{0,1},{1,0},{2,3},{3,2},{4,5},{5,4},{6,7},{7,6},{8,9},{9,8},{10,11... | collective-permute-start | bytes 393224 | tf_op jit(solution)/shard_map/ppermute | solution.py:337
  44.6 1.7 %collective-permute-start.20 = (bf16[1,16,4096]{2,1,0:T(8,128)(2,1)S(1)}, bf16[1,16,4096]{2,1,0:T(8,128)(2,1)S(1)}, u32[]{:S(2)}, u32[]{:S(2)}) collective-permute-start(bf16[1,16,4096]{2,1,0:T(8,128)(2,1)S(1)} %get-tuple-element.32), channel_id=1, source_target_pairs={{0,1},{1,0},{2,3},{3,2},{4,5},{5,4},{6,7},{7,6},{8,9},{9,8},{10,11... | collective-permute-start | bytes 393224 | tf_op jit(solution)/shard_map/ppermute | solution.py:337
  44.7 1.7 %collective-permute-start.21 = (bf16[1,16,4096]{2,1,0:T(8,128)(2,1)S(1)}, bf16[1,16,4096]{2,1,0:T(8,128)(2,1)S(1)}, u32[]{:S(2)}, u32[]{:S(2)}) collective-permute-start(bf16[1,16,4096]{2,1,0:T(8,128)(2,1)S(1)} %get-tuple-element.31), channel_id=1, source_target_pairs={{0,1},{1,0},{2,3},{3,2},{4,5},{5,4},{6,7},{7,6},{8,9},{9,8},{10,11... | collective-permute-start | bytes 393224 | tf_op jit(solution)/shard_map/ppermute | solution.py:337
  47.2 4.4 %collective-permute-start.22 = (bf16[64,512]{1,0:T(8,128)(2,1)S(1)}, bf16[64,512]{1,0:T(8,128)(2,1)S(1)}, u32[]{:S(2)}, u32[]{:S(2)}) collective-permute-start(bf16[64,512]{1,0:T(8,128)(2,1)S(1)} %scores_5.1), channel_id=1, source_target_pairs={{0,16},{1,17},{2,18},{3,19},{4,20},{5,21},{6,22},{7,23},{8,24},{9,... | collective-permute-start | bytes 196616 | tf_op jit(solution)/shard_map/ppermute | solution.py:337
  (2 other events, 5.4 us)

commit v5 on v4

--- a/solution.py
+++ b/solution.py
@@ -321,22 +321,64 @@
 
 
 def ring_order(chips):
-    half = chips // 2
-    return [2 * i for i in range(half)] + [2 * i + 1 for i in reversed(range(half))]
-
-
-def ring_device(query_grads, train_grads, left_inverse, right_inverse):
-    chips, groups, cores = 8, 2, 2
+    wide = chips // 4
+    order = [(i, 0) for i in range(4)]
+    for turn, i in enumerate(reversed(range(4))):
+        others = range(1, wide)
+        order += [(i, j) for j in (reversed(others) if turn % 2 else others)]
+    return [i * wide + j for i, j in order]
+
+
+def ring_pairs(groups, chips, cores=2):
     order = ring_order(chips)
     flat = lambda layer, chip, core: (layer * chips + chip) * cores + core
     every = [(y, h, c) for y in range(groups) for h in range(chips) for c in range(cores)]
     step = lambda h, c: order[(order.index(h) + (1 - 2 * c)) % chips]
     swap = [(flat(y, h, c), flat(y, h, 1 - c)) for y, h, c in every]
-    across = [(flat(y, h, c), flat(1 - y, h, c)) for y, h, c in every]
     around = [(flat(y, h, c), flat(y, step(h, c), c)) for y, h, c in every]
-    send = lambda v, pairs: lax.ppermute(v, AXES, pairs)
-
+    across = [(flat(y, h, c), flat(groups - 1 - y, h, c)) for y, h, c in every]
+    return swap, around, across
+
+
+def send(value, pairs):
+    return lax.ppermute(value, AXES, pairs)
+
+
+def any_ring_device(groups, chips, query_grads, train_grads, left_inverse, right_inverse):
+    swap, around, _ = ring_pairs(groups, chips)
+    order = ring_order(chips)
+    mine = precondition(query_grads, left_inverse, right_inverse, True)
+    turned = [transpose(l, train_grads) for l in range(query_grads.shape[0])]
+    rows = mine.shape[1]
+    row = lax.axis_index("row")
+    chip, core = row // 2, lax.rem(row, 2)
+    place = jnp.argmax(jnp.array(order, jnp.int32) == chip).astype(jnp.int32)
+    table = jnp.zeros((chips * 2 * rows, train_grads.shape[1]), jnp.float32)
+
+    def fill(table, block, offset, core):
+        at = lax.rem(place + offset * (1 - 2 * lax.rem(row, 2)) + chips, chips)
+        at = lax.dynamic_index_in_dim(jnp.array(order, jnp.int32), at, 0, keepdims=False) * 2 + core
+        return lax.dynamic_update_slice_in_dim(table, block, at * rows, 0)
+
+    held = [mine, send(mine, swap)]
+    block = block_call(plain_kernel, "scores", 2 * rows, None, turned, held)
+    table = fill(table, block[:rows], 0, core)
+    table = fill(table, block[rows:], 0, 1 - core)
+    for k in range(1, chips // 2 + 1):
+        held = [send(h, around) for h in (held if k < chips // 2 else held[:1])]
+        queries = held + [send(h, swap) for h in held]
+        block = block_call(plain_kernel, "scores", len(queries) * rows, None, turned, queries)
+        cores = (core, 1 - core, 1 - core, core) if len(held) == 2 else (core, 1 - core)
+        for n, c in enumerate(cores):
+            table = fill(table, block[n * rows:(n + 1) * rows], -k if n < len(held) or k == chips // 2 else k, c)
+    return lax.psum_scatter(table, "layer", scatter_dimension=0, tiled=True)
+
+
+def ring_device(query_grads, train_grads, left_inverse, right_inverse):
+    chips, groups = 8, 2
+    swap, around, across = ring_pairs(groups, chips)
     after = lax.optimization_barrier
+
     def quarters(unit):
         layers, held, feat = unit.shape
         half = held // 2
@@ -377,23 +419,6 @@
     return finish((kept2, got2, kept, got, zeroth), (kept4, got4), chips // groups * rows, turned[0].shape[1])
 
 
-def on_device(query_grads, train_grads, left_inverse, right_inverse):
-    layers, rows, feat = query_grads.shape
-    proj = left_inverse.shape[1]
-    square = query_grads.astype(jnp.float32).reshape(layers, rows, proj, proj)
-    rotated = jnp.einsum(
-        "lab,lqbc,lcd->lqad", left_inverse, square, right_inverse, precision=lax.Precision.HIGHEST
-    )
-    rotated = rotated.reshape(layers, rows, feat).astype(jnp.bfloat16)
-    partial_value = jnp.einsum(
-        "lqf,ltf->qt",
-        lax.all_gather(rotated, "row", axis=1, tiled=True),
-        train_grads,
-        preferred_element_type=jnp.float32,
-    )
-    return lax.psum_scatter(partial_value, "layer", scatter_dimension=0, tiled=True)
-
-
 def solution(mesh):
     placed = (
         P("layer", "row", None),
@@ -401,7 +426,11 @@
         P("layer", None, None),
         P("layer", None, None),
     )
-    ring = mesh.shape["layer"] == 2 and mesh.shape["row"] == 16
+    groups, chips = mesh.shape["layer"], mesh.shape["row"] // 2
+    if (groups, chips) == (2, 8):
+        on_device = ring_device
+    else:
+        on_device = functools.partial(any_ring_device, groups, chips)
     return jax.shard_map(
-        ring_device if ring else on_device, mesh=mesh, in_specs=placed, out_specs=P("layer", "row"), check_vma=False
+        on_device, mesh=mesh, in_specs=placed, out_specs=P("layer", "row"), check_vma=False
     )

time: 51.9 us -> 51.9 us (level)
  no operation moved by 1% of the time
where the time goes in v5:
time: 51.9 us; the launch traced here: 51.7 us
  starting transfers between devices  22.6 us (44%)
  Pallas kernels  18.9 us (36%)
  waiting for transfers between devices  9.75 us (19%)
    ppermute x24, starting transfers between devices, send(): return lax.ppermute(value, AXES, pairs)  22.6 us
    ppermute x24, waiting for transfers between devices, send(): return lax.ppermute(value, AXES, pairs)  9.75 us
    pallas_call x7, Pallas kernels, block_call(): pl.pallas_call(kernel, out_shape=(jax.ShapeDtypeStruct((max(rows, sent),...  6.71 us
    pallas_call x3, Pallas kernels, precondition(): pl.pallas_call(precondition_first_kernel if first else precondition_kerne...  5.92 us
    pallas_call x2, Pallas kernels, transpose(): pl.pallas_call(functools.partial(transpose_kernel, layer), out_shape=pltp...  5.31 us
  transfers between devices with their start and end apart: 24, of which 10 were waited for; matrix products, arithmetic and copies ran while one was open for 0% of the time, Pallas kernels for 37%

profile of v5, /device:TPU:0, one launch (start us, length us, event | category | flops | bytes accessed | tf_op | source)
XLA Modules:
  0.0 51.7 jit_solution(14805419369870223552)
XLA Ops:
  0.5 2.6 %collective-permute-start = (bf16[2,32,4096]{2,1,0:T(8,128)(2,1)}, bf16[2,32,4096]{2,1,0:T(8,128)(2,1)S(1)}, u32[]{:S(2)}, u32[]{:S(2)}) collective-permute-start(bf16[2,32,4096]{2,1,0:T(8,128)(2,1)} %query_hbm.1), channel_id=1, source_target_pairs={{0,4},{1,3},{2,0},{3,7},{4,8},{5,1},{6,2},{7,11},{8,12},{9,5},{10,... | collective-permute-start | bytes 1572872 | tf_op jit(solution)/shard_map/ppermute | solution.py:344
  3.0 2.1 %collective-permute-start.5 = (bf16[2,32,4096]{2,1,0:T(8,128)(2,1)S(1)}, bf16[2,32,4096]{2,1,0:T(8,128)(2,1)S(1)}, u32[]{:S(2)}, u32[]{:S(2)}) collective-permute-start(bf16[2,32,4096]{2,1,0:T(8,128)(2,1)S(1)} %collective-permute-done.4), channel_id=1, source_target_pairs={{0,4},{1,3},{2,0},{3,7},{4,8},{5,1},{6,2},{7,11},{8,12},{9,5},{10,... | collective-permute-start | bytes 1572872 | tf_op jit(solution)/shard_map/ppermute | solution.py:344
  5.1 2.6 %transpose_0.1.turned = bf16[4096,512]{1,0:T(8,128)(2,1)S(1)} custom-call(bf16[2,512,4096]{2,1,0:T(8,128)(2,1)} %train.3), custom_call_target="tpu_custom_call" | custom-call | flops 2147483648 | bytes 8388608 | tf_op jit(solution)/shard_map/transpose_0/pallas_call | solution.py:122
  7.8 2.7 %transpose_1.1.more.turned = bf16[4096,512]{1,0:T(8,128)(2,1)S(1)} custom-call(bf16[2,512,4096]{2,1,0:T(8,128)(2,1)} %train.3), custom_call_target="tpu_custom_call" | custom-call | flops 2147483648 | bytes 8388608 | tf_op jit(solution)/shard_map/transpose_1/pallas_call | solution.py:122
  10.5 1.6 %precondition_1.2.refs_0_ = bf16[2,32,4096]{2,1,0:T(8,128)(2,1)S(1)} custom-call(bf16[2,32,4096]{2,1,0:T(8,128)(2,1)S(1)} %collective-permute-done.query, f32[2,64,64]{2,1,0:T(8,128)S(1)} %copy-done, f32[2,64,64]{2,1,0:T(8,128)S(1)} %copy-done.1), custom_call_target="tpu_custom_call" | custom-call | flops 2147483648 | bytes 4194304 | tf_op jit(solution)/shard_map/precondition_1/pallas_call | solution.py:90
  12.2 2.0 %collective-permute-start.1 = (bf16[2,32,4096]{2,1,0:T(8,128)(2,1)S(1)}, bf16[2,32,4096]{2,1,0:T(8,128)(2,1)S(1)}, u32[]{:S(2)}, u32[]{:S(2)}) collective-permute-start(bf16[2,32,4096]{2,1,0:T(8,128)(2,1)S(1)} %precondition_1.2.refs_0_), channel_id=1, source_target_pairs={{0,4},{1,3},{2,0},{3,7},{4,8},{5,1},{6,2},{7,11},{8,12},{9,5},{10,... | collective-permute-start | bytes 1572872 | tf_op jit(solution)/shard_map/ppermute | solution.py:344
  14.2 1.8 %collective-permute-done.5.query = bf16[2,32,4096]{2,1,0:T(8,128)(2,1)S(1)} collective-permute-done((bf16[2,32,4096]{2,1,0:T(8,128)(2,1)S(1)}, bf16[2,32,4096]{2,1,0:T(8,128)(2,1)S(1)}, u32[]{:S(2)}, u32[]{:S(2)}) %collective-permute-start.5) | collective-permute-done | bytes 524320 | tf_op jit(solution)/shard_map/ppermute | solution.py:344
  15.9 1.6 %precondition_1.3.refs_1_ = bf16[2,32,4096]{2,1,0:T(8,128)(2,1)S(1)} custom-call(bf16[2,32,4096]{2,1,0:T(8,128)(2,1)S(1)} %collective-permute-done.5.query, f32[2,64,64]{2,1,0:T(8,128)S(1)} %copy-done, f32[2,64,64]{2,1,0:T(8,128)S(1)} %copy-done.1), custom_call_target="tpu_custom_call" | custom-call | flops 2147483648 | bytes 4194304 | tf_op jit(solution)/shard_map/precondition_1/pallas_call | solution.py:90
  17.6 2.2 %collective-permute-start.6 = (bf16[2,32,4096]{2,1,0:T(8,128)(2,1)S(1)}, bf16[2,32,4096]{2,1,0:T(8,128)(2,1)S(1)}, u32[]{:S(2)}, u32[]{:S(2)}) collective-permute-start(bf16[2,32,4096]{2,1,0:T(8,128)(2,1)S(1)} %precondition_1.3.refs_1_), channel_id=1, source_target_pairs={{0,4},{1,3},{2,0},{3,7},{4,8},{5,1},{6,2},{7,11},{8,12},{9,5},{10,... | collective-permute-start | bytes 1572872 | tf_op jit(solution)/shard_map/ppermute | solution.py:344
  19.8 2.7 %precondition_0.1.refs_0_ = bf16[2,32,4096]{2,1,0:T(8,128)(2,1)S(1)} custom-call(bf16[2,32,4096]{2,1,0:T(8,128)(2,1)} %query_hbm.1, f32[2,64,64]{2,1,0:T(8,128)} %left.3, f32[2,64,64]{2,1,0:T(8,128)} %right.3), custom_call_target="tpu_custom_call" | custom-call | flops 2147483648 | bytes 4194304 | tf_op jit(solution)/shard_map/precondition_0/pallas_call | solution.py:90
  23.1 1.6 %collective-permute-start.2 = (bf16[2,32,4096]{2,1,0:T(8,128)(2,1)S(1)}, bf16[2,32,4096]{2,1,0:T(8,128)(2,1)S(1)}, u32[]{:S(2)}, u32[]{:S(2)}) collective-permute-start(bf16[2,32,4096]{2,1,0:T(8,128)(2,1)S(1)} %collective-permute-done.1.refs_0_), channel_id=1, source_target_pairs={{0,4},{1,3},{2,0},{3,7},{4,8},{5,1},{6,2},{7,11},{8,12},{9,5},{10,... | collective-permute-start | bytes 1572872 | tf_op jit(solution)/shard_map/ppermute | solution.py:344
  24.7 1.2 %scores_1.1.first = f32[128,512]{1,0:T(8,128)S(1)} custom-call(bf16[4096,512]{1,0:T(8,128)(2,1)S(1)} %transpose_0.1.turned, bf16[4096,512]{1,0:T(8,128)(2,1)S(1)} %transpose_1.1.more.turned, bf16[2,32,4096]{2,1,0:T(8,128)(2,1)S(1)} %precondition_1.2.refs_0_, bf16[2,32,4096]{2,1,0:T(8,128)(2,1)S(1)} %precondition_1.3.refs_1_, ...), custom_call_target="tpu_custom_call" | custom-call | flops 1024 | bytes 1024 | tf_op jit(solution)/shard_map/scores_1/pallas_call | solution.py:243
  25.9 1.2 %collective-permute-done.6.refs_1_ = bf16[2,32,4096]{2,1,0:T(8,128)(2,1)S(1)} collective-permute-done((bf16[2,32,4096]{2,1,0:T(8,128)(2,1)S(1)}, bf16[2,32,4096]{2,1,0:T(8,128)(2,1)S(1)}, u32[]{:S(2)}, u32[]{:S(2)}) %collective-permute-start.6) | collective-permute-done | bytes 524320 | tf_op jit(solution)/shard_map/ppermute | solution.py:344
  27.2 2.1 %collective-permute-start.13 = (bf16[2,32,4096]{2,1,0:T(8,128)(2,1)S(1)}, bf16[2,32,4096]{2,1,0:T(8,128)(2,1)S(1)}, u32[]{:S(2)}, u32[]{:S(2)}) collective-permute-start(bf16[2,32,4096]{2,1,0:T(8,128)(2,1)S(1)} %collective-permute-done.6.refs_1_), channel_id=1, source_target_pairs={{0,4},{1,3},{2,0},{3,7},{4,8},{5,1},{6,2},{7,11},{8,12},{9,5},{10,... | collective-permute-start | bytes 1572872 | tf_op jit(solution)/shard_map/ppermute | solution.py:344
  29.9 1.2 %scores_0.1.own = f32[64,512]{1,0:T(8,128)S(1)} custom-call(bf16[4096,512]{1,0:T(8,128)(2,1)S(1)} %transpose_0.1.turned, bf16[4096,512]{1,0:T(8,128)(2,1)S(1)} %transpose_1.1.more.turned, bf16[2,32,4096]{2,1,0:T(8,128)(2,1)S(1)} %precondition_0.1.refs_0_, bf16[2,32,4096]{2,1,0:T(8,128)(2,1)S(1)} %collective-permute-done.3.refs_1_), custom_call_target="tpu_custom_call" | custom-call | flops 1024 | bytes 1024 | tf_op jit(solution)/shard_map/scores_0/pallas_call | solution.py:243
  31.3 1.3 %scores_2.1 = (bf16[128,512]{1,0:T(8,128)(2,1)S(1)}, f32[64,512]{1,0:T(8,128)S(1)}) custom-call(bf16[4096,512]{1,0:T(8,128)(2,1)S(1)} %transpose_0.1.turned, bf16[4096,512]{1,0:T(8,128)(2,1)S(1)} %transpose_1.1.more.turned, f32[64,512]{1,0:T(8,128)S(1)} %scores_0.1.own, bf16[2,32,4096]{2,1,0:T(8,128)(2,1)S(1)} %collective-permute-done.1.refs_0_, ...), custom_call_target="tpu_custom_call" | custom-call | flops 1024 | bytes 1024 | tf_op jit(solution)/shard_map/scores_2/pallas_call | solution.py:243
  32.6 1.6 %collective-permute-start.14 = (bf16[128,512]{1,0:T(8,128)(2,1)S(1)}, bf16[128,512]{1,0:T(8,128)(2,1)S(1)}, u32[]{:S(2)}, u32[]{:S(2)}) collective-permute-start(bf16[128,512]{1,0:T(8,128)(2,1)S(1)} %get-tuple-element.22), channel_id=1, source_target_pairs={{0,16},{1,17},{2,18},{3,19},{4,20},{5,21},{6,22},{7,23},{8,24},{9,... | collective-permute-start | bytes 393224 | tf_op jit(solution)/shard_map/ppermute | solution.py:344
  34.2 1.6 %collective-permute-start.12 = (bf16[2,32,4096]{2,1,0:T(8,128)(2,1)S(1)}, bf16[2,32,4096]{2,1,0:T(8,128)(2,1)S(1)}, u32[]{:S(2)}, u32[]{:S(2)}) collective-permute-start(bf16[2,32,4096]{2,1,0:T(8,128)(2,1)S(1)} %collective-permute-done.2.refs_0_), channel_id=1, source_target_pairs={{0,4},{1,3},{2,0},{3,7},{4,8},{5,1},{6,2},{7,11},{8,12},{9,5},{10,... | collective-permute-start | bytes 1572872 | tf_op jit(solution)/shard_map/ppermute | solution.py:344
  35.7 2.4 %collective-permute-done.14.got2 = bf16[128,512]{1,0:T(8,128)(2,1)S(1)} collective-permute-done((bf16[128,512]{1,0:T(8,128)(2,1)S(1)}, bf16[128,512]{1,0:T(8,128)(2,1)S(1)}, u32[]{:S(2)}, u32[]{:S(2)}) %collective-permute-start.14) | collective-permute-done | bytes 131104 | tf_op jit(solution)/shard_map/ppermute | solution.py:344
  39.0 1.0 %collective-permute-done.16.refs_3_ = bf16[1,32,4096]{2,1,0:T(8,128)(2,1)S(1)} collective-permute-done((bf16[1,32,4096]{2,1,0:T(8,128)(2,1)S(1)}, bf16[1,32,4096]{2,1,0:T(8,128)(2,1)S(1)}, u32[]{:S(2)}, u32[]{:S(2)}) %collective-permute-start.16) | collective-permute-done | bytes 262176 | tf_op jit(solution)/shard_map/ppermute | solution.py:344
  40.4 1.5 %scores_3.1 = (bf16[160,512]{1,0:T(8,128)(2,1)S(1)}, f32[128,512]{1,0:T(8,128)S(1)}) custom-call(bf16[4096,512]{1,0:T(8,128)(2,1)S(1)} %transpose_0.1.turned, bf16[4096,512]{1,0:T(8,128)(2,1)S(1)} %transpose_1.1.more.turned, f32[128,512]{1,0:T(8,128)S(1)} %scores_1.1.first, bf16[2,32,4096]{2,1,0:T(8,128)(2,1)S(1)} %collective-permute-done.2.refs_0_, ...), custom_call_target="tpu_custom_call" | custom-call | flops 1024 | bytes 1024 | tf_op jit(solution)/shard_map/scores_3/pallas_call | solution.py:243
  41.9 2.1 %collective-permute-start.23 = (bf16[160,512]{1,0:T(8,128)(2,1)S(1)}, bf16[160,512]{1,0:T(8,128)(2,1)S(1)}, u32[]{:S(2)}, u32[]{:S(2)}) collective-permute-start(bf16[160,512]{1,0:T(8,128)(2,1)S(1)} %get-tuple-element.26), channel_id=1, source_target_pairs={{0,16},{1,17},{2,18},{3,19},{4,20},{5,21},{6,22},{7,23},{8,24},{9,... | collective-permute-start | bytes 491528 | tf_op jit(solution)/shard_map/ppermute | solution.py:344
  47.2 1.4 %collective-permute-start.22 = (bf16[64,512]{1,0:T(8,128)(2,1)S(1)}, bf16[64,512]{1,0:T(8,128)(2,1)S(1)}, u32[]{:S(2)}, u32[]{:S(2)}) collective-permute-start(bf16[64,512]{1,0:T(8,128)(2,1)S(1)} %scores_5.1), channel_id=1, source_target_pairs={{0,16},{1,17},{2,18},{3,19},{4,20},{5,21},{6,22},{7,23},{8,24},{9,... | collective-permute-start | bytes 196616 | tf_op jit(solution)/shard_map/ppermute | solution.py:344
  49.5 2.0 %collective-permute-done.22.got = bf16[64,512]{1,0:T(8,128)(2,1)S(1)} collective-permute-done((bf16[64,512]{1,0:T(8,128)(2,1)S(1)}, bf16[64,512]{1,0:T(8,128)(2,1)S(1)}, u32[]{:S(2)}, u32[]{:S(2)}) %collective-permute-start.22) | collective-permute-done | bytes 65568 | tf_op jit(solution)/shard_map/ppermute | solution.py:344
  (45 shorter events, 7.2 us)
Async XLA Ops:
  0.0 3.0 %collective-permute-start.4 = (bf16[2,32,4096]{2,1,0:T(8,128)(2,1)}, bf16[2,32,4096]{2,1,0:T(8,128)(2,1)S(1)}, u32[]{:S(2)}, u32[]{:S(2)}) collective-permute-start(bf16[2,32,4096]{2,1,0:T(8,128)(2,1)} %query_hbm.1), channel_id=1, source_target_pairs={{0,1},{1,0},{2,3},{3,2},{4,5},{5,4},{6,7},{7,6},{8,9},{9,8},{10,11... | collective-permute-start | bytes 1572872 | tf_op jit(solution)/shard_map/ppermute | solution.py:344
  0.5 10.0 %collective-permute-start = (bf16[2,32,4096]{2,1,0:T(8,128)(2,1)}, bf16[2,32,4096]{2,1,0:T(8,128)(2,1)S(1)}, u32[]{:S(2)}, u32[]{:S(2)}) collective-permute-start(bf16[2,32,4096]{2,1,0:T(8,128)(2,1)} %query_hbm.1), channel_id=1, source_target_pairs={{0,4},{1,3},{2,0},{3,7},{4,8},{5,1},{6,2},{7,11},{8,12},{9,5},{10,... | collective-permute-start | bytes 1572872 | tf_op jit(solution)/shard_map/ppermute | solution.py:344
  3.0 12.9 %collective-permute-start.5 = (bf16[2,32,4096]{2,1,0:T(8,128)(2,1)S(1)}, bf16[2,32,4096]{2,1,0:T(8,128)(2,1)S(1)}, u32[]{:S(2)}, u32[]{:S(2)}) collective-permute-start(bf16[2,32,4096]{2,1,0:T(8,128)(2,1)S(1)} %collective-permute-done.4), channel_id=1, source_target_pairs={{0,4},{1,3},{2,0},{3,7},{4,8},{5,1},{6,2},{7,11},{8,12},{9,5},{10,... | collective-permute-start | bytes 1572872 | tf_op jit(solution)/shard_map/ppermute | solution.py:344
  12.1 11.0 %collective-permute-start.7 = (bf16[2,32,4096]{2,1,0:T(8,128)(2,1)S(1)}, bf16[2,32,4096]{2,1,0:T(8,128)(2,1)S(1)}, u32[]{:S(2)}, u32[]{:S(2)}) collective-permute-start(bf16[2,32,4096]{2,1,0:T(8,128)(2,1)S(1)} %precondition_1.2.refs_0_), channel_id=1, source_target_pairs={{0,1},{1,0},{2,3},{3,2},{4,5},{5,4},{6,7},{7,6},{8,9},{9,8},{10,11... | collective-permute-start | bytes 1572872 | tf_op jit(solution)/shard_map/ppermute | solution.py:344
  12.2 10.4 %collective-permute-start.1 = (bf16[2,32,4096]{2,1,0:T(8,128)(2,1)S(1)}, bf16[2,32,4096]{2,1,0:T(8,128)(2,1)S(1)}, u32[]{:S(2)}, u32[]{:S(2)}) collective-permute-start(bf16[2,32,4096]{2,1,0:T(8,128)(2,1)S(1)} %precondition_1.2.refs_0_), channel_id=1, source_target_pairs={{0,4},{1,3},{2,0},{3,7},{4,8},{5,1},{6,2},{7,11},{8,12},{9,5},{10,... | collective-permute-start | bytes 1572872 | tf_op jit(solution)/shard_map/ppermute | solution.py:344
  17.5 7.1 %collective-permute-start.8 = (bf16[2,32,4096]{2,1,0:T(8,128)(2,1)S(1)}, bf16[2,32,4096]{2,1,0:T(8,128)(2,1)S(1)}, u32[]{:S(2)}, u32[]{:S(2)}) collective-permute-start(bf16[2,32,4096]{2,1,0:T(8,128)(2,1)S(1)} %precondition_1.3.refs_1_), channel_id=1, source_target_pairs={{0,1},{1,0},{2,3},{3,2},{4,5},{5,4},{6,7},{7,6},{8,9},{9,8},{10,11... | collective-permute-start | bytes 1572872 | tf_op jit(solution)/shard_map/ppermute | solution.py:344
  17.6 9.5 %collective-permute-start.6 = (bf16[2,32,4096]{2,1,0:T(8,128)(2,1)S(1)}, bf16[2,32,4096]{2,1,0:T(8,128)(2,1)S(1)}, u32[]{:S(2)}, u32[]{:S(2)}) collective-permute-start(bf16[2,32,4096]{2,1,0:T(8,128)(2,1)S(1)} %precondition_1.3.refs_1_), channel_id=1, source_target_pairs={{0,4},{1,3},{2,0},{3,7},{4,8},{5,1},{6,2},{7,11},{8,12},{9,5},{10,... | collective-permute-start | bytes 1572872 | tf_op jit(solution)/shard_map/ppermute | solution.py:344
  22.5 6.9 %collective-permute-start.3 = (bf16[2,32,4096]{2,1,0:T(8,128)(2,1)S(1)}, bf16[2,32,4096]{2,1,0:T(8,128)(2,1)S(1)}, u32[]{:S(2)}, u32[]{:S(2)}) collective-permute-start(bf16[2,32,4096]{2,1,0:T(8,128)(2,1)S(1)} %precondition_0.1.refs_0_), channel_id=1, source_target_pairs={{0,1},{1,0},{2,3},{3,2},{4,5},{5,4},{6,7},{7,6},{8,9},{9,8},{10,11... | collective-permute-start | bytes 1572872 | tf_op jit(solution)/shard_map/ppermute | solution.py:344
  22.7 8.5 %collective-permute-start.9 = (bf16[2,32,4096]{2,1,0:T(8,128)(2,1)S(1)}, bf16[2,32,4096]{2,1,0:T(8,128)(2,1)S(1)}, u32[]{:S(2)}, u32[]{:S(2)}) collective-permute-start(bf16[2,32,4096]{2,1,0:T(8,128)(2,1)S(1)} %collective-permute-done.1.refs_0_), channel_id=1, source_target_pairs={{0,1},{1,0},{2,3},{3,2},{4,5},{5,4},{6,7},{7,6},{8,9},{9,8},{10,11... | collective-permute-start | bytes 1572872 | tf_op jit(solution)/shard_map/ppermute | solution.py:344
  23.1 11.1 %collective-permute-start.2 = (bf16[2,32,4096]{2,1,0:T(8,128)(2,1)S(1)}, bf16[2,32,4096]{2,1,0:T(8,128)(2,1)S(1)}, u32[]{:S(2)}, u32[]{:S(2)}) collective-permute-start(bf16[2,32,4096]{2,1,0:T(8,128)(2,1)S(1)} %collective-permute-done.1.refs_0_), channel_id=1, source_target_pairs={{0,4},{1,3},{2,0},{3,7},{4,8},{5,1},{6,2},{7,11},{8,12},{9,5},{10,... | collective-permute-start | bytes 1572872 | tf_op jit(solution)/shard_map/ppermute | solution.py:344
  27.2 11.2 %collective-permute-start.13 = (bf16[2,32,4096]{2,1,0:T(8,128)(2,1)S(1)}, bf16[2,32,4096]{2,1,0:T(8,128)(2,1)S(1)}, u32[]{:S(2)}, u32[]{:S(2)}) collective-permute-start(bf16[2,32,4096]{2,1,0:T(8,128)(2,1)S(1)} %collective-permute-done.6.refs_1_), channel_id=1, source_target_pairs={{0,4},{1,3},{2,0},{3,7},{4,8},{5,1},{6,2},{7,11},{8,12},{9,5},{10,... | collective-permute-start | bytes 1572872 | tf_op jit(solution)/shard_map/ppermute | solution.py:344
  29.3 1.8 %collective-permute-start.10 = (bf16[1,32,4096]{2,1,0:T(8,128)(2,1)S(1)}, bf16[1,32,4096]{2,1,0:T(8,128)(2,1)S(1)}, u32[]{:S(2)}, u32[]{:S(2)}) collective-permute-start(bf16[1,32,4096]{2,1,0:T(8,128)(2,1)S(1)} %get-tuple-element.38), channel_id=1, source_target_pairs={{0,1},{1,0},{2,3},{3,2},{4,5},{5,4},{6,7},{7,6},{8,9},{9,8},{10,11... | collective-permute-start | bytes 786440 | tf_op jit(solution)/shard_map/ppermute | solution.py:344
  29.4 1.9 %collective-permute-start.11 = (bf16[1,32,4096]{2,1,0:T(8,128)(2,1)S(1)}, bf16[1,32,4096]{2,1,0:T(8,128)(2,1)S(1)}, u32[]{:S(2)}, u32[]{:S(2)}) collective-permute-start(bf16[1,32,4096]{2,1,0:T(8,128)(2,1)S(1)} %get-tuple-element.37), channel_id=1, source_target_pairs={{0,1},{1,0},{2,3},{3,2},{4,5},{5,4},{6,7},{7,6},{8,9},{9,8},{10,11... | collective-permute-start | bytes 786440 | tf_op jit(solution)/shard_map/ppermute | solution.py:344
  32.6 5.6 %collective-permute-start.14 = (bf16[128,512]{1,0:T(8,128)(2,1)S(1)}, bf16[128,512]{1,0:T(8,128)(2,1)S(1)}, u32[]{:S(2)}, u32[]{:S(2)}) collective-permute-start(bf16[128,512]{1,0:T(8,128)(2,1)S(1)} %get-tuple-element.22), channel_id=1, source_target_pairs={{0,16},{1,17},{2,18},{3,19},{4,20},{5,21},{6,22},{7,23},{8,24},{9,... | collective-permute-start | bytes 393224 | tf_op jit(solution)/shard_map/ppermute | solution.py:344
  34.2 6.3 %collective-permute-start.15 = (bf16[2,32,4096]{2,1,0:T(8,128)(2,1)S(1)}, bf16[2,32,4096]{2,1,0:T(8,128)(2,1)S(1)}, u32[]{:S(2)}, u32[]{:S(2)}) collective-permute-start(bf16[2,32,4096]{2,1,0:T(8,128)(2,1)S(1)} %collective-permute-done.2.refs_0_), channel_id=1, source_target_pairs={{0,1},{1,0},{2,3},{3,2},{4,5},{5,4},{6,7},{7,6},{8,9},{9,8},{10,11... | collective-permute-start | bytes 1572872 | tf_op jit(solution)/shard_map/ppermute | solution.py:344
  34.2 9.9 %collective-permute-start.12 = (bf16[2,32,4096]{2,1,0:T(8,128)(2,1)S(1)}, bf16[2,32,4096]{2,1,0:T(8,128)(2,1)S(1)}, u32[]{:S(2)}, u32[]{:S(2)}) collective-permute-start(bf16[2,32,4096]{2,1,0:T(8,128)(2,1)S(1)} %collective-permute-done.2.refs_0_), channel_id=1, source_target_pairs={{0,4},{1,3},{2,0},{3,7},{4,8},{5,1},{6,2},{7,11},{8,12},{9,5},{10,... | collective-permute-start | bytes 1572872 | tf_op jit(solution)/shard_map/ppermute | solution.py:344
  38.4 1.6 %collective-permute-start.16 = (bf16[1,32,4096]{2,1,0:T(8,128)(2,1)S(1)}, bf16[1,32,4096]{2,1,0:T(8,128)(2,1)S(1)}, u32[]{:S(2)}, u32[]{:S(2)}) collective-permute-start(bf16[1,32,4096]{2,1,0:T(8,128)(2,1)S(1)} %get-tuple-element.36), channel_id=1, source_target_pairs={{0,1},{1,0},{2,3},{3,2},{4,5},{5,4},{6,7},{7,6},{8,9},{9,8},{10,11... | collective-permute-start | bytes 786440 | tf_op jit(solution)/shard_map/ppermute | solution.py:344
  38.5 1.9 %collective-permute-start.17 = (bf16[1,32,4096]{2,1,0:T(8,128)(2,1)S(1)}, bf16[1,32,4096]{2,1,0:T(8,128)(2,1)S(1)}, u32[]{:S(2)}, u32[]{:S(2)}) collective-permute-start(bf16[1,32,4096]{2,1,0:T(8,128)(2,1)S(1)} %get-tuple-element.35), channel_id=1, source_target_pairs={{0,1},{1,0},{2,3},{3,2},{4,5},{5,4},{6,7},{7,6},{8,9},{9,8},{10,11... | collective-permute-start | bytes 786440 | tf_op jit(solution)/shard_map/ppermute | solution.py:344
  41.9 6.7 %collective-permute-start.23 = (bf16[160,512]{1,0:T(8,128)(2,1)S(1)}, bf16[160,512]{1,0:T(8,128)(2,1)S(1)}, u32[]{:S(2)}, u32[]{:S(2)}) collective-permute-start(bf16[160,512]{1,0:T(8,128)(2,1)S(1)} %get-tuple-element.26), channel_id=1, source_target_pairs={{0,16},{1,17},{2,18},{3,19},{4,20},{5,21},{6,22},{7,23},{8,24},{9,... | collective-permute-start | bytes 491528 | tf_op jit(solution)/shard_map/ppermute | solution.py:344
  44.1 1.4 %collective-permute-start.18 = (bf16[1,16,4096]{2,1,0:T(8,128)(2,1)S(1)}, bf16[1,16,4096]{2,1,0:T(8,128)(2,1)S(1)}, u32[]{:S(2)}, u32[]{:S(2)}) collective-permute-start(bf16[1,16,4096]{2,1,0:T(8,128)(2,1)S(1)} %get-tuple-element.34), channel_id=1, source_target_pairs={{0,1},{1,0},{2,3},{3,2},{4,5},{5,4},{6,7},{7,6},{8,9},{9,8},{10,11... | collective-permute-start | bytes 393224 | tf_op jit(solution)/shard_map/ppermute | solution.py:344
  44.1 1.5 %collective-permute-start.19 = (bf16[1,16,4096]{2,1,0:T(8,128)(2,1)S(1)}, bf16[1,16,4096]{2,1,0:T(8,128)(2,1)S(1)}, u32[]{:S(2)}, u32[]{:S(2)}) collective-permute-start(bf16[1,16,4096]{2,1,0:T(8,128)(2,1)S(1)} %get-tuple-element.33), channel_id=1, source_target_pairs={{0,1},{1,0},{2,3},{3,2},{4,5},{5,4},{6,7},{7,6},{8,9},{9,8},{10,11... | collective-permute-start | bytes 393224 | tf_op jit(solution)/shard_map/ppermute | solution.py:344
  44.6 1.7 %collective-permute-start.20 = (bf16[1,16,4096]{2,1,0:T(8,128)(2,1)S(1)}, bf16[1,16,4096]{2,1,0:T(8,128)(2,1)S(1)}, u32[]{:S(2)}, u32[]{:S(2)}) collective-permute-start(bf16[1,16,4096]{2,1,0:T(8,128)(2,1)S(1)} %get-tuple-element.32), channel_id=1, source_target_pairs={{0,1},{1,0},{2,3},{3,2},{4,5},{5,4},{6,7},{7,6},{8,9},{9,8},{10,11... | collective-permute-start | bytes 393224 | tf_op jit(solution)/shard_map/ppermute | solution.py:344
  44.7 1.7 %collective-permute-start.21 = (bf16[1,16,4096]{2,1,0:T(8,128)(2,1)S(1)}, bf16[1,16,4096]{2,1,0:T(8,128)(2,1)S(1)}, u32[]{:S(2)}, u32[]{:S(2)}) collective-permute-start(bf16[1,16,4096]{2,1,0:T(8,128)(2,1)S(1)} %get-tuple-element.31), channel_id=1, source_target_pairs={{0,1},{1,0},{2,3},{3,2},{4,5},{5,4},{6,7},{7,6},{8,9},{9,8},{10,11... | collective-permute-start | bytes 393224 | tf_op jit(solution)/shard_map/ppermute | solution.py:344
  47.2 4.4 %collective-permute-start.22 = (bf16[64,512]{1,0:T(8,128)(2,1)S(1)}, bf16[64,512]{1,0:T(8,128)(2,1)S(1)}, u32[]{:S(2)}, u32[]{:S(2)}) collective-permute-start(bf16[64,512]{1,0:T(8,128)(2,1)S(1)} %scores_5.1), channel_id=1, source_target_pairs={{0,16},{1,17},{2,18},{3,19},{4,20},{5,21},{6,22},{7,23},{8,24},{9,... | collective-permute-start | bytes 196616 | tf_op jit(solution)/shard_map/ppermute | solution.py:344
  (2 other events, 5.4 us)

commit v6 on v5

--- a/solution.py
+++ b/solution.py
@@ -275,25 +275,20 @@
         put(out, chip_at(0), 0, own[...] + got2[high].astype(own.dtype))
 
 
-def last_kernel(kept, got, table, out, block, sems):
+def last_kernel(kept, got, table, out, block, sem):
     del table
 
     @pl.when(jnp.logical_not(foreign(4)))
     def _():
         rows = kept.shape[0] // 2
-        block[...] = kept[...] + got[...].astype(kept.dtype)
-        at = chip_at(4) - 4 * lax.axis_index("layer")
         core = lax.rem(lax.axis_index("row"), 2)
-        copies = []
         for n, c in enumerate((core, 1 - core)):
-            start = pl.multiple_of((2 * at + c) * rows, rows)
-            copies.append(
-                pltpu.make_async_copy(block.at[n * rows:(n + 1) * rows], out.at[pl.ds(start, rows)], sems.at[n])
-            )
-        for copy in copies:
-            copy.start()
-        for copy in copies:
-            copy.wait()
+            part = pl.ds(n * rows, rows)
+            block[pl.ds(pl.multiple_of(c * rows, rows), rows), :] = kept[part, :] + got[part, :].astype(kept.dtype)
+        start = pl.multiple_of((chip_at(4) - 4 * lax.axis_index("layer")) * 2 * rows, 2 * rows)
+        copy = pltpu.make_async_copy(block, out.at[pl.ds(start, 2 * rows)], sem)
+        copy.start()
+        copy.wait()
 
 
 def finish(most, last, rows, columns):
@@ -305,7 +300,7 @@
         in_specs=[VMEM] * 5,
         out_specs=VMEM,
         compiler_params=params,
-        cost_estimate=pl.CostEstimate(flops=60 << 30, bytes_accessed=1 << 20, transcendentals=0),
+        cost_estimate=pl.CostEstimate(flops=1 << 30, bytes_accessed=1 << 20, transcendentals=0),
         name="gather_rows",
     )(*most)
     return pl.pallas_call(
@@ -313,7 +308,7 @@
         out_shape=table,
         in_specs=[VMEM, VMEM, HBM],
         out_specs=HBM,
-        scratch_shapes=[pltpu.VMEM(last[0].shape, jnp.float32), pltpu.SemaphoreType.DMA((2,))],
+        scratch_shapes=[pltpu.VMEM(last[0].shape, jnp.float32), pltpu.SemaphoreType.DMA],
         input_output_aliases={2: 0},
         compiler_params=params,
         name="last_rows",
@@ -408,7 +403,7 @@
     got2 = send(sent2, across)
     b[3], got2 = after((b[3], got2))
     queries = [a[3], b[3], send(a[3], swap), *halves_of(b[3])]
-    sent, kept = block_call(third_kernel, "scores_3", 2 * rows, 2 * rows, turned, [first] + queries, jnp.bfloat16, 2 * rows + 32)
+    sent, kept = block_call(third_kernel, "scores_3", 2 * rows, 2 * rows, turned, [first] + queries, jnp.bfloat16, 2 * rows + 16)
     got = send(sent, across)
     a[4], _ = after((a[4], sent))
     swapped = quarters(a[4])

time: 51.9 us -> 51.9 us (level)
  no operation moved by 1% of the time
where the time goes in v6:
time: 51.9 us; the launch traced here: 51.7 us
  starting transfers between devices  22.6 us (44%)
  Pallas kernels  18.9 us (36%)
  waiting for transfers between devices  9.75 us (19%)
    ppermute x24, starting transfers between devices, send(): return lax.ppermute(value, AXES, pairs)  22.6 us
    ppermute x24, waiting for transfers between devices, send(): return lax.ppermute(value, AXES, pairs)  9.75 us
    pallas_call x7, Pallas kernels, block_call(): pl.pallas_call(kernel, out_shape=(jax.ShapeDtypeStruct((max(rows, sent),...  6.71 us
    pallas_call x3, Pallas kernels, precondition(): pl.pallas_call(precondition_first_kernel if first else precondition_kerne...  5.92 us
    pallas_call x2, Pallas kernels, transpose(): pl.pallas_call(functools.partial(transpose_kernel, layer), out_shape=pltp...  5.31 us
  transfers between devices with their start and end apart: 24, of which 10 were waited for; matrix products, arithmetic and copies ran while one was open for 0% of the time, Pallas kernels for 37%

profile of v6, /device:TPU:0, one launch (start us, length us, event | category | flops | bytes accessed | tf_op | source)
XLA Modules:
  0.0 51.7 jit_solution(773063347571128807)
XLA Ops:
  0.5 2.6 %collective-permute-start = (bf16[2,32,4096]{2,1,0:T(8,128)(2,1)}, bf16[2,32,4096]{2,1,0:T(8,128)(2,1)S(1)}, u32[]{:S(2)}, u32[]{:S(2)}) collective-permute-start(bf16[2,32,4096]{2,1,0:T(8,128)(2,1)} %query_hbm.1), channel_id=1, source_target_pairs={{0,4},{1,3},{2,0},{3,7},{4,8},{5,1},{6,2},{7,11},{8,12},{9,5},{10,... | collective-permute-start | bytes 1572872 | tf_op jit(solution)/shard_map/ppermute | solution.py:339
  3.0 2.1 %collective-permute-start.5 = (bf16[2,32,4096]{2,1,0:T(8,128)(2,1)S(1)}, bf16[2,32,4096]{2,1,0:T(8,128)(2,1)S(1)}, u32[]{:S(2)}, u32[]{:S(2)}) collective-permute-start(bf16[2,32,4096]{2,1,0:T(8,128)(2,1)S(1)} %collective-permute-done.4), channel_id=1, source_target_pairs={{0,4},{1,3},{2,0},{3,7},{4,8},{5,1},{6,2},{7,11},{8,12},{9,5},{10,... | collective-permute-start | bytes 1572872 | tf_op jit(solution)/shard_map/ppermute | solution.py:339
  5.1 2.6 %transpose_0.1.turned = bf16[4096,512]{1,0:T(8,128)(2,1)S(1)} custom-call(bf16[2,512,4096]{2,1,0:T(8,128)(2,1)} %train.3), custom_call_target="tpu_custom_call" | custom-call | flops 2147483648 | bytes 8388608 | tf_op jit(solution)/shard_map/transpose_0/pallas_call | solution.py:122
  7.8 2.7 %transpose_1.1.more.turned = bf16[4096,512]{1,0:T(8,128)(2,1)S(1)} custom-call(bf16[2,512,4096]{2,1,0:T(8,128)(2,1)} %train.3), custom_call_target="tpu_custom_call" | custom-call | flops 2147483648 | bytes 8388608 | tf_op jit(solution)/shard_map/transpose_1/pallas_call | solution.py:122
  10.5 1.6 %precondition_1.2.refs_0_ = bf16[2,32,4096]{2,1,0:T(8,128)(2,1)S(1)} custom-call(bf16[2,32,4096]{2,1,0:T(8,128)(2,1)S(1)} %collective-permute-done.query, f32[2,64,64]{2,1,0:T(8,128)S(1)} %copy-done, f32[2,64,64]{2,1,0:T(8,128)S(1)} %copy-done.1), custom_call_target="tpu_custom_call" | custom-call | flops 2147483648 | bytes 4194304 | tf_op jit(solution)/shard_map/precondition_1/pallas_call | solution.py:90
  12.2 2.0 %collective-permute-start.1 = (bf16[2,32,4096]{2,1,0:T(8,128)(2,1)S(1)}, bf16[2,32,4096]{2,1,0:T(8,128)(2,1)S(1)}, u32[]{:S(2)}, u32[]{:S(2)}) collective-permute-start(bf16[2,32,4096]{2,1,0:T(8,128)(2,1)S(1)} %precondition_1.2.refs_0_), channel_id=1, source_target_pairs={{0,4},{1,3},{2,0},{3,7},{4,8},{5,1},{6,2},{7,11},{8,12},{9,5},{10,... | collective-permute-start | bytes 1572872 | tf_op jit(solution)/shard_map/ppermute | solution.py:339
  14.2 1.8 %collective-permute-done.5.query = bf16[2,32,4096]{2,1,0:T(8,128)(2,1)S(1)} collective-permute-done((bf16[2,32,4096]{2,1,0:T(8,128)(2,1)S(1)}, bf16[2,32,4096]{2,1,0:T(8,128)(2,1)S(1)}, u32[]{:S(2)}, u32[]{:S(2)}) %collective-permute-start.5) | collective-permute-done | bytes 524320 | tf_op jit(solution)/shard_map/ppermute | solution.py:339
  15.9 1.6 %precondition_1.3.refs_1_ = bf16[2,32,4096]{2,1,0:T(8,128)(2,1)S(1)} custom-call(bf16[2,32,4096]{2,1,0:T(8,128)(2,1)S(1)} %collective-permute-done.5.query, f32[2,64,64]{2,1,0:T(8,128)S(1)} %copy-done, f32[2,64,64]{2,1,0:T(8,128)S(1)} %copy-done.1), custom_call_target="tpu_custom_call" | custom-call | flops 2147483648 | bytes 4194304 | tf_op jit(solution)/shard_map/precondition_1/pallas_call | solution.py:90
  17.6 2.2 %collective-permute-start.6 = (bf16[2,32,4096]{2,1,0:T(8,128)(2,1)S(1)}, bf16[2,32,4096]{2,1,0:T(8,128)(2,1)S(1)}, u32[]{:S(2)}, u32[]{:S(2)}) collective-permute-start(bf16[2,32,4096]{2,1,0:T(8,128)(2,1)S(1)} %precondition_1.3.refs_1_), channel_id=1, source_target_pairs={{0,4},{1,3},{2,0},{3,7},{4,8},{5,1},{6,2},{7,11},{8,12},{9,5},{10,... | collective-permute-start | bytes 1572872 | tf_op jit(solution)/shard_map/ppermute | solution.py:339
  19.8 2.7 %precondition_0.1.refs_0_ = bf16[2,32,4096]{2,1,0:T(8,128)(2,1)S(1)} custom-call(bf16[2,32,4096]{2,1,0:T(8,128)(2,1)} %query_hbm.1, f32[2,64,64]{2,1,0:T(8,128)} %left.3, f32[2,64,64]{2,1,0:T(8,128)} %right.3), custom_call_target="tpu_custom_call" | custom-call | flops 2147483648 | bytes 4194304 | tf_op jit(solution)/shard_map/precondition_0/pallas_call | solution.py:90
  23.1 1.6 %collective-permute-start.2 = (bf16[2,32,4096]{2,1,0:T(8,128)(2,1)S(1)}, bf16[2,32,4096]{2,1,0:T(8,128)(2,1)S(1)}, u32[]{:S(2)}, u32[]{:S(2)}) collective-permute-start(bf16[2,32,4096]{2,1,0:T(8,128)(2,1)S(1)} %collective-permute-done.1.refs_0_), channel_id=1, source_target_pairs={{0,4},{1,3},{2,0},{3,7},{4,8},{5,1},{6,2},{7,11},{8,12},{9,5},{10,... | collective-permute-start | bytes 1572872 | tf_op jit(solution)/shard_map/ppermute | solution.py:339
  24.7 1.2 %scores_1.1.first = f32[128,512]{1,0:T(8,128)S(1)} custom-call(bf16[4096,512]{1,0:T(8,128)(2,1)S(1)} %transpose_0.1.turned, bf16[4096,512]{1,0:T(8,128)(2,1)S(1)} %transpose_1.1.more.turned, bf16[2,32,4096]{2,1,0:T(8,128)(2,1)S(1)} %precondition_1.2.refs_0_, bf16[2,32,4096]{2,1,0:T(8,128)(2,1)S(1)} %precondition_1.3.refs_1_, ...), custom_call_target="tpu_custom_call" | custom-call | flops 1024 | bytes 1024 | tf_op jit(solution)/shard_map/scores_1/pallas_call | solution.py:243
  25.9 1.2 %collective-permute-done.6.refs_1_ = bf16[2,32,4096]{2,1,0:T(8,128)(2,1)S(1)} collective-permute-done((bf16[2,32,4096]{2,1,0:T(8,128)(2,1)S(1)}, bf16[2,32,4096]{2,1,0:T(8,128)(2,1)S(1)}, u32[]{:S(2)}, u32[]{:S(2)}) %collective-permute-start.6) | collective-permute-done | bytes 524320 | tf_op jit(solution)/shard_map/ppermute | solution.py:339
  27.2 2.1 %collective-permute-start.13 = (bf16[2,32,4096]{2,1,0:T(8,128)(2,1)S(1)}, bf16[2,32,4096]{2,1,0:T(8,128)(2,1)S(1)}, u32[]{:S(2)}, u32[]{:S(2)}) collective-permute-start(bf16[2,32,4096]{2,1,0:T(8,128)(2,1)S(1)} %collective-permute-done.6.refs_1_), channel_id=1, source_target_pairs={{0,4},{1,3},{2,0},{3,7},{4,8},{5,1},{6,2},{7,11},{8,12},{9,5},{10,... | collective-permute-start | bytes 1572872 | tf_op jit(solution)/shard_map/ppermute | solution.py:339
  29.9 1.2 %scores_0.1.own = f32[64,512]{1,0:T(8,128)S(1)} custom-call(bf16[4096,512]{1,0:T(8,128)(2,1)S(1)} %transpose_0.1.turned, bf16[4096,512]{1,0:T(8,128)(2,1)S(1)} %transpose_1.1.more.turned, bf16[2,32,4096]{2,1,0:T(8,128)(2,1)S(1)} %precondition_0.1.refs_0_, bf16[2,32,4096]{2,1,0:T(8,128)(2,1)S(1)} %collective-permute-done.3.refs_1_), custom_call_target="tpu_custom_call" | custom-call | flops 1024 | bytes 1024 | tf_op jit(solution)/shard_map/scores_0/pallas_call | solution.py:243
  31.3 1.3 %scores_2.1 = (bf16[128,512]{1,0:T(8,128)(2,1)S(1)}, f32[64,512]{1,0:T(8,128)S(1)}) custom-call(bf16[4096,512]{1,0:T(8,128)(2,1)S(1)} %transpose_0.1.turned, bf16[4096,512]{1,0:T(8,128)(2,1)S(1)} %transpose_1.1.more.turned, f32[64,512]{1,0:T(8,128)S(1)} %scores_0.1.own, bf16[2,32,4096]{2,1,0:T(8,128)(2,1)S(1)} %collective-permute-done.1.refs_0_, ...), custom_call_target="tpu_custom_call" | custom-call | flops 1024 | bytes 1024 | tf_op jit(solution)/shard_map/scores_2/pallas_call | solution.py:243
  32.6 1.6 %collective-permute-start.14 = (bf16[128,512]{1,0:T(8,128)(2,1)S(1)}, bf16[128,512]{1,0:T(8,128)(2,1)S(1)}, u32[]{:S(2)}, u32[]{:S(2)}) collective-permute-start(bf16[128,512]{1,0:T(8,128)(2,1)S(1)} %get-tuple-element.22), channel_id=1, source_target_pairs={{0,16},{1,17},{2,18},{3,19},{4,20},{5,21},{6,22},{7,23},{8,24},{9,... | collective-permute-start | bytes 393224 | tf_op jit(solution)/shard_map/ppermute | solution.py:339
  34.2 1.6 %collective-permute-start.12 = (bf16[2,32,4096]{2,1,0:T(8,128)(2,1)S(1)}, bf16[2,32,4096]{2,1,0:T(8,128)(2,1)S(1)}, u32[]{:S(2)}, u32[]{:S(2)}) collective-permute-start(bf16[2,32,4096]{2,1,0:T(8,128)(2,1)S(1)} %collective-permute-done.2.refs_0_), channel_id=1, source_target_pairs={{0,4},{1,3},{2,0},{3,7},{4,8},{5,1},{6,2},{7,11},{8,12},{9,5},{10,... | collective-permute-start | bytes 1572872 | tf_op jit(solution)/shard_map/ppermute | solution.py:339
  35.7 2.4 %collective-permute-done.14.got2 = bf16[128,512]{1,0:T(8,128)(2,1)S(1)} collective-permute-done((bf16[128,512]{1,0:T(8,128)(2,1)S(1)}, bf16[128,512]{1,0:T(8,128)(2,1)S(1)}, u32[]{:S(2)}, u32[]{:S(2)}) %collective-permute-start.14) | collective-permute-done | bytes 131104 | tf_op jit(solution)/shard_map/ppermute | solution.py:339
  39.0 1.0 %collective-permute-done.16.refs_3_ = bf16[1,32,4096]{2,1,0:T(8,128)(2,1)S(1)} collective-permute-done((bf16[1,32,4096]{2,1,0:T(8,128)(2,1)S(1)}, bf16[1,32,4096]{2,1,0:T(8,128)(2,1)S(1)}, u32[]{:S(2)}, u32[]{:S(2)}) %collective-permute-start.16) | collective-permute-done | bytes 262176 | tf_op jit(solution)/shard_map/ppermute | solution.py:339
  40.4 1.5 %scores_3.1 = (bf16[144,512]{1,0:T(8,128)(2,1)S(1)}, f32[128,512]{1,0:T(8,128)S(1)}) custom-call(bf16[4096,512]{1,0:T(8,128)(2,1)S(1)} %transpose_0.1.turned, bf16[4096,512]{1,0:T(8,128)(2,1)S(1)} %transpose_1.1.more.turned, f32[128,512]{1,0:T(8,128)S(1)} %scores_1.1.first, bf16[2,32,4096]{2,1,0:T(8,128)(2,1)S(1)} %collective-permute-done.2.refs_0_, ...), custom_call_target="tpu_custom_call" | custom-call | flops 1024 | bytes 1024 | tf_op jit(solution)/shard_map/scores_3/pallas_call | solution.py:243
  41.9 2.1 %collective-permute-start.23 = (bf16[144,512]{1,0:T(8,128)(2,1)S(1)}, bf16[144,512]{1,0:T(8,128)(2,1)S(1)}, u32[]{:S(2)}, u32[]{:S(2)}) collective-permute-start(bf16[144,512]{1,0:T(8,128)(2,1)S(1)} %get-tuple-element.26), channel_id=1, source_target_pairs={{0,16},{1,17},{2,18},{3,19},{4,20},{5,21},{6,22},{7,23},{8,24},{9,... | collective-permute-start | bytes 442376 | tf_op jit(solution)/shard_map/ppermute | solution.py:339
  47.2 1.4 %collective-permute-start.22 = (bf16[64,512]{1,0:T(8,128)(2,1)S(1)}, bf16[64,512]{1,0:T(8,128)(2,1)S(1)}, u32[]{:S(2)}, u32[]{:S(2)}) collective-permute-start(bf16[64,512]{1,0:T(8,128)(2,1)S(1)} %scores_5.1), channel_id=1, source_target_pairs={{0,16},{1,17},{2,18},{3,19},{4,20},{5,21},{6,22},{7,23},{8,24},{9,... | collective-permute-start | bytes 196616 | tf_op jit(solution)/shard_map/ppermute | solution.py:339
  49.5 2.0 %collective-permute-done.22.got = bf16[64,512]{1,0:T(8,128)(2,1)S(1)} collective-permute-done((bf16[64,512]{1,0:T(8,128)(2,1)S(1)}, bf16[64,512]{1,0:T(8,128)(2,1)S(1)}, u32[]{:S(2)}, u32[]{:S(2)}) %collective-permute-start.22) | collective-permute-done | bytes 65568 | tf_op jit(solution)/shard_map/ppermute | solution.py:339
  (45 shorter events, 7.2 us)
Async XLA Ops:
  0.0 3.0 %collective-permute-start.4 = (bf16[2,32,4096]{2,1,0:T(8,128)(2,1)}, bf16[2,32,4096]{2,1,0:T(8,128)(2,1)S(1)}, u32[]{:S(2)}, u32[]{:S(2)}) collective-permute-start(bf16[2,32,4096]{2,1,0:T(8,128)(2,1)} %query_hbm.1), channel_id=1, source_target_pairs={{0,1},{1,0},{2,3},{3,2},{4,5},{5,4},{6,7},{7,6},{8,9},{9,8},{10,11... | collective-permute-start | bytes 1572872 | tf_op jit(solution)/shard_map/ppermute | solution.py:339
  0.5 10.0 %collective-permute-start = (bf16[2,32,4096]{2,1,0:T(8,128)(2,1)}, bf16[2,32,4096]{2,1,0:T(8,128)(2,1)S(1)}, u32[]{:S(2)}, u32[]{:S(2)}) collective-permute-start(bf16[2,32,4096]{2,1,0:T(8,128)(2,1)} %query_hbm.1), channel_id=1, source_target_pairs={{0,4},{1,3},{2,0},{3,7},{4,8},{5,1},{6,2},{7,11},{8,12},{9,5},{10,... | collective-permute-start | bytes 1572872 | tf_op jit(solution)/shard_map/ppermute | solution.py:339
  3.0 12.9 %collective-permute-start.5 = (bf16[2,32,4096]{2,1,0:T(8,128)(2,1)S(1)}, bf16[2,32,4096]{2,1,0:T(8,128)(2,1)S(1)}, u32[]{:S(2)}, u32[]{:S(2)}) collective-permute-start(bf16[2,32,4096]{2,1,0:T(8,128)(2,1)S(1)} %collective-permute-done.4), channel_id=1, source_target_pairs={{0,4},{1,3},{2,0},{3,7},{4,8},{5,1},{6,2},{7,11},{8,12},{9,5},{10,... | collective-permute-start | bytes 1572872 | tf_op jit(solution)/shard_map/ppermute | solution.py:339
  12.1 11.0 %collective-permute-start.7 = (bf16[2,32,4096]{2,1,0:T(8,128)(2,1)S(1)}, bf16[2,32,4096]{2,1,0:T(8,128)(2,1)S(1)}, u32[]{:S(2)}, u32[]{:S(2)}) collective-permute-start(bf16[2,32,4096]{2,1,0:T(8,128)(2,1)S(1)} %precondition_1.2.refs_0_), channel_id=1, source_target_pairs={{0,1},{1,0},{2,3},{3,2},{4,5},{5,4},{6,7},{7,6},{8,9},{9,8},{10,11... | collective-permute-start | bytes 1572872 | tf_op jit(solution)/shard_map/ppermute | solution.py:339
  12.2 10.4 %collective-permute-start.1 = (bf16[2,32,4096]{2,1,0:T(8,128)(2,1)S(1)}, bf16[2,32,4096]{2,1,0:T(8,128)(2,1)S(1)}, u32[]{:S(2)}, u32[]{:S(2)}) collective-permute-start(bf16[2,32,4096]{2,1,0:T(8,128)(2,1)S(1)} %precondition_1.2.refs_0_), channel_id=1, source_target_pairs={{0,4},{1,3},{2,0},{3,7},{4,8},{5,1},{6,2},{7,11},{8,12},{9,5},{10,... | collective-permute-start | bytes 1572872 | tf_op jit(solution)/shard_map/ppermute | solution.py:339
  17.5 7.1 %collective-permute-start.8 = (bf16[2,32,4096]{2,1,0:T(8,128)(2,1)S(1)}, bf16[2,32,4096]{2,1,0:T(8,128)(2,1)S(1)}, u32[]{:S(2)}, u32[]{:S(2)}) collective-permute-start(bf16[2,32,4096]{2,1,0:T(8,128)(2,1)S(1)} %precondition_1.3.refs_1_), channel_id=1, source_target_pairs={{0,1},{1,0},{2,3},{3,2},{4,5},{5,4},{6,7},{7,6},{8,9},{9,8},{10,11... | collective-permute-start | bytes 1572872 | tf_op jit(solution)/shard_map/ppermute | solution.py:339
  17.6 9.5 %collective-permute-start.6 = (bf16[2,32,4096]{2,1,0:T(8,128)(2,1)S(1)}, bf16[2,32,4096]{2,1,0:T(8,128)(2,1)S(1)}, u32[]{:S(2)}, u32[]{:S(2)}) collective-permute-start(bf16[2,32,4096]{2,1,0:T(8,128)(2,1)S(1)} %precondition_1.3.refs_1_), channel_id=1, source_target_pairs={{0,4},{1,3},{2,0},{3,7},{4,8},{5,1},{6,2},{7,11},{8,12},{9,5},{10,... | collective-permute-start | bytes 1572872 | tf_op jit(solution)/shard_map/ppermute | solution.py:339
  22.5 6.9 %collective-permute-start.3 = (bf16[2,32,4096]{2,1,0:T(8,128)(2,1)S(1)}, bf16[2,32,4096]{2,1,0:T(8,128)(2,1)S(1)}, u32[]{:S(2)}, u32[]{:S(2)}) collective-permute-start(bf16[2,32,4096]{2,1,0:T(8,128)(2,1)S(1)} %precondition_0.1.refs_0_), channel_id=1, source_target_pairs={{0,1},{1,0},{2,3},{3,2},{4,5},{5,4},{6,7},{7,6},{8,9},{9,8},{10,11... | collective-permute-start | bytes 1572872 | tf_op jit(solution)/shard_map/ppermute | solution.py:339
  22.7 8.5 %collective-permute-start.9 = (bf16[2,32,4096]{2,1,0:T(8,128)(2,1)S(1)}, bf16[2,32,4096]{2,1,0:T(8,128)(2,1)S(1)}, u32[]{:S(2)}, u32[]{:S(2)}) collective-permute-start(bf16[2,32,4096]{2,1,0:T(8,128)(2,1)S(1)} %collective-permute-done.1.refs_0_), channel_id=1, source_target_pairs={{0,1},{1,0},{2,3},{3,2},{4,5},{5,4},{6,7},{7,6},{8,9},{9,8},{10,11... | collective-permute-start | bytes 1572872 | tf_op jit(solution)/shard_map/ppermute | solution.py:339
  23.1 11.1 %collective-permute-start.2 = (bf16[2,32,4096]{2,1,0:T(8,128)(2,1)S(1)}, bf16[2,32,4096]{2,1,0:T(8,128)(2,1)S(1)}, u32[]{:S(2)}, u32[]{:S(2)}) collective-permute-start(bf16[2,32,4096]{2,1,0:T(8,128)(2,1)S(1)} %collective-permute-done.1.refs_0_), channel_id=1, source_target_pairs={{0,4},{1,3},{2,0},{3,7},{4,8},{5,1},{6,2},{7,11},{8,12},{9,5},{10,... | collective-permute-start | bytes 1572872 | tf_op jit(solution)/shard_map/ppermute | solution.py:339
  27.2 11.2 %collective-permute-start.13 = (bf16[2,32,4096]{2,1,0:T(8,128)(2,1)S(1)}, bf16[2,32,4096]{2,1,0:T(8,128)(2,1)S(1)}, u32[]{:S(2)}, u32[]{:S(2)}) collective-permute-start(bf16[2,32,4096]{2,1,0:T(8,128)(2,1)S(1)} %collective-permute-done.6.refs_1_), channel_id=1, source_target_pairs={{0,4},{1,3},{2,0},{3,7},{4,8},{5,1},{6,2},{7,11},{8,12},{9,5},{10,... | collective-permute-start | bytes 1572872 | tf_op jit(solution)/shard_map/ppermute | solution.py:339
  29.3 1.8 %collective-permute-start.10 = (bf16[1,32,4096]{2,1,0:T(8,128)(2,1)S(1)}, bf16[1,32,4096]{2,1,0:T(8,128)(2,1)S(1)}, u32[]{:S(2)}, u32[]{:S(2)}) collective-permute-start(bf16[1,32,4096]{2,1,0:T(8,128)(2,1)S(1)} %get-tuple-element.38), channel_id=1, source_target_pairs={{0,1},{1,0},{2,3},{3,2},{4,5},{5,4},{6,7},{7,6},{8,9},{9,8},{10,11... | collective-permute-start | bytes 786440 | tf_op jit(solution)/shard_map/ppermute | solution.py:339
  29.4 1.9 %collective-permute-start.11 = (bf16[1,32,4096]{2,1,0:T(8,128)(2,1)S(1)}, bf16[1,32,4096]{2,1,0:T(8,128)(2,1)S(1)}, u32[]{:S(2)}, u32[]{:S(2)}) collective-permute-start(bf16[1,32,4096]{2,1,0:T(8,128)(2,1)S(1)} %get-tuple-element.37), channel_id=1, source_target_pairs={{0,1},{1,0},{2,3},{3,2},{4,5},{5,4},{6,7},{7,6},{8,9},{9,8},{10,11... | collective-permute-start | bytes 786440 | tf_op jit(solution)/shard_map/ppermute | solution.py:339
  32.6 5.6 %collective-permute-start.14 = (bf16[128,512]{1,0:T(8,128)(2,1)S(1)}, bf16[128,512]{1,0:T(8,128)(2,1)S(1)}, u32[]{:S(2)}, u32[]{:S(2)}) collective-permute-start(bf16[128,512]{1,0:T(8,128)(2,1)S(1)} %get-tuple-element.22), channel_id=1, source_target_pairs={{0,16},{1,17},{2,18},{3,19},{4,20},{5,21},{6,22},{7,23},{8,24},{9,... | collective-permute-start | bytes 393224 | tf_op jit(solution)/shard_map/ppermute | solution.py:339
  34.2 6.3 %collective-permute-start.15 = (bf16[2,32,4096]{2,1,0:T(8,128)(2,1)S(1)}, bf16[2,32,4096]{2,1,0:T(8,128)(2,1)S(1)}, u32[]{:S(2)}, u32[]{:S(2)}) collective-permute-start(bf16[2,32,4096]{2,1,0:T(8,128)(2,1)S(1)} %collective-permute-done.2.refs_0_), channel_id=1, source_target_pairs={{0,1},{1,0},{2,3},{3,2},{4,5},{5,4},{6,7},{7,6},{8,9},{9,8},{10,11... | collective-permute-start | bytes 1572872 | tf_op jit(solution)/shard_map/ppermute | solution.py:339
  34.2 9.9 %collective-permute-start.12 = (bf16[2,32,4096]{2,1,0:T(8,128)(2,1)S(1)}, bf16[2,32,4096]{2,1,0:T(8,128)(2,1)S(1)}, u32[]{:S(2)}, u32[]{:S(2)}) collective-permute-start(bf16[2,32,4096]{2,1,0:T(8,128)(2,1)S(1)} %collective-permute-done.2.refs_0_), channel_id=1, source_target_pairs={{0,4},{1,3},{2,0},{3,7},{4,8},{5,1},{6,2},{7,11},{8,12},{9,5},{10,... | collective-permute-start | bytes 1572872 | tf_op jit(solution)/shard_map/ppermute | solution.py:339
  38.4 1.6 %collective-permute-start.16 = (bf16[1,32,4096]{2,1,0:T(8,128)(2,1)S(1)}, bf16[1,32,4096]{2,1,0:T(8,128)(2,1)S(1)}, u32[]{:S(2)}, u32[]{:S(2)}) collective-permute-start(bf16[1,32,4096]{2,1,0:T(8,128)(2,1)S(1)} %get-tuple-element.36), channel_id=1, source_target_pairs={{0,1},{1,0},{2,3},{3,2},{4,5},{5,4},{6,7},{7,6},{8,9},{9,8},{10,11... | collective-permute-start | bytes 786440 | tf_op jit(solution)/shard_map/ppermute | solution.py:339
  38.5 1.9 %collective-permute-start.17 = (bf16[1,32,4096]{2,1,0:T(8,128)(2,1)S(1)}, bf16[1,32,4096]{2,1,0:T(8,128)(2,1)S(1)}, u32[]{:S(2)}, u32[]{:S(2)}) collective-permute-start(bf16[1,32,4096]{2,1,0:T(8,128)(2,1)S(1)} %get-tuple-element.35), channel_id=1, source_target_pairs={{0,1},{1,0},{2,3},{3,2},{4,5},{5,4},{6,7},{7,6},{8,9},{9,8},{10,11... | collective-permute-start | bytes 786440 | tf_op jit(solution)/shard_map/ppermute | solution.py:339
  41.9 6.7 %collective-permute-start.23 = (bf16[144,512]{1,0:T(8,128)(2,1)S(1)}, bf16[144,512]{1,0:T(8,128)(2,1)S(1)}, u32[]{:S(2)}, u32[]{:S(2)}) collective-permute-start(bf16[144,512]{1,0:T(8,128)(2,1)S(1)} %get-tuple-element.26), channel_id=1, source_target_pairs={{0,16},{1,17},{2,18},{3,19},{4,20},{5,21},{6,22},{7,23},{8,24},{9,... | collective-permute-start | bytes 442376 | tf_op jit(solution)/shard_map/ppermute | solution.py:339
  44.1 1.4 %collective-permute-start.18 = (bf16[1,16,4096]{2,1,0:T(8,128)(2,1)S(1)}, bf16[1,16,4096]{2,1,0:T(8,128)(2,1)S(1)}, u32[]{:S(2)}, u32[]{:S(2)}) collective-permute-start(bf16[1,16,4096]{2,1,0:T(8,128)(2,1)S(1)} %get-tuple-element.34), channel_id=1, source_target_pairs={{0,1},{1,0},{2,3},{3,2},{4,5},{5,4},{6,7},{7,6},{8,9},{9,8},{10,11... | collective-permute-start | bytes 393224 | tf_op jit(solution)/shard_map/ppermute | solution.py:339
  44.1 1.5 %collective-permute-start.19 = (bf16[1,16,4096]{2,1,0:T(8,128)(2,1)S(1)}, bf16[1,16,4096]{2,1,0:T(8,128)(2,1)S(1)}, u32[]{:S(2)}, u32[]{:S(2)}) collective-permute-start(bf16[1,16,4096]{2,1,0:T(8,128)(2,1)S(1)} %get-tuple-element.33), channel_id=1, source_target_pairs={{0,1},{1,0},{2,3},{3,2},{4,5},{5,4},{6,7},{7,6},{8,9},{9,8},{10,11... | collective-permute-start | bytes 393224 | tf_op jit(solution)/shard_map/ppermute | solution.py:339
  44.6 1.7 %collective-permute-start.20 = (bf16[1,16,4096]{2,1,0:T(8,128)(2,1)S(1)}, bf16[1,16,4096]{2,1,0:T(8,128)(2,1)S(1)}, u32[]{:S(2)}, u32[]{:S(2)}) collective-permute-start(bf16[1,16,4096]{2,1,0:T(8,128)(2,1)S(1)} %get-tuple-element.32), channel_id=1, source_target_pairs={{0,1},{1,0},{2,3},{3,2},{4,5},{5,4},{6,7},{7,6},{8,9},{9,8},{10,11... | collective-permute-start | bytes 393224 | tf_op jit(solution)/shard_map/ppermute | solution.py:339
  44.7 1.7 %collective-permute-start.21 = (bf16[1,16,4096]{2,1,0:T(8,128)(2,1)S(1)}, bf16[1,16,4096]{2,1,0:T(8,128)(2,1)S(1)}, u32[]{:S(2)}, u32[]{:S(2)}) collective-permute-start(bf16[1,16,4096]{2,1,0:T(8,128)(2,1)S(1)} %get-tuple-element.31), channel_id=1, source_target_pairs={{0,1},{1,0},{2,3},{3,2},{4,5},{5,4},{6,7},{7,6},{8,9},{9,8},{10,11... | collective-permute-start | bytes 393224 | tf_op jit(solution)/shard_map/ppermute | solution.py:339
  47.2 4.4 %collective-permute-start.22 = (bf16[64,512]{1,0:T(8,128)(2,1)S(1)}, bf16[64,512]{1,0:T(8,128)(2,1)S(1)}, u32[]{:S(2)}, u32[]{:S(2)}) collective-permute-start(bf16[64,512]{1,0:T(8,128)(2,1)S(1)} %scores_5.1), channel_id=1, source_target_pairs={{0,16},{1,17},{2,18},{3,19},{4,20},{5,21},{6,22},{7,23},{8,24},{9,... | collective-permute-start | bytes 196616 | tf_op jit(solution)/shard_map/ppermute | solution.py:339
  (2 other events, 5.4 us)

commit v7 on v6

--- a/solution.py
+++ b/solution.py
@@ -209,7 +209,10 @@
 
 def opening_kernel(turned, *refs):
     unit, *swapped, out = refs
-    out[...] = layer_score(turned, [unit.at[0]] + [ref.at[0] for ref in swapped])
+
+    @pl.when(foreign(4))
+    def _():
+        out[...] = layer_score(turned, [unit.at[0]] + [ref.at[0] for ref in swapped])
 
 
 def second_layer(turned, opening, unit, swapped):
@@ -228,12 +231,12 @@
         sent[...] = jnp.zeros_like(sent)
 
 
-def fifth_kernel(turned, opening, *refs):
+def fifth_kernel(turned, more, *refs):
     unit, *swapped, kept = refs
 
     @pl.when(jnp.logical_not(foreign(4)))
     def _():
-        kept[...] = second_layer(turned, opening, unit, swapped)
+        kept[...] = score(turned, more, [unit, swapped])
 
 
 def block_call(kernel, name, rows, total, turned, operands, kind=jnp.float32, sent=0):
@@ -300,7 +303,7 @@
         in_specs=[VMEM] * 5,
         out_specs=VMEM,
         compiler_params=params,
-        cost_estimate=pl.CostEstimate(flops=1 << 30, bytes_accessed=1 << 20, transcendentals=0),
+        cost_estimate=pl.CostEstimate(flops=60 << 30, bytes_accessed=1 << 20, transcendentals=0),
         name="gather_rows",
     )(*most)
     return pl.pallas_call(
@@ -403,14 +406,14 @@
     got2 = send(sent2, across)
     b[3], got2 = after((b[3], got2))
     queries = [a[3], b[3], send(a[3], swap), *halves_of(b[3])]
-    sent, kept = block_call(third_kernel, "scores_3", 2 * rows, 2 * rows, turned, [first] + queries, jnp.bfloat16, 2 * rows + 16)
+    sent, kept = block_call(third_kernel, "scores_3", 2 * rows, 2 * rows, turned, [first] + queries, jnp.bfloat16, 2 * rows + 32)
     got = send(sent, across)
     a[4], _ = after((a[4], sent))
     swapped = quarters(a[4])
     opening = block_call(opening_kernel, "scores_4", rows, None, turned[:1], [a[4], *swapped[:2]])
     sent4 = block_call(fourth_kernel, "scores_5", rows, None, turned[1:], [opening, a[4], *swapped[2:]], jnp.bfloat16)
     got4 = send(sent4, across)
-    kept4 = block_call(fifth_kernel, "scores_6", rows, None, turned[1:], [opening, a[4], *swapped[2:]])
+    kept4 = block_call(fifth_kernel, "scores_6", rows, None, turned, [a[4], *swapped])
     return finish((kept2, got2, kept, got, zeroth), (kept4, got4), chips // groups * rows, turned[0].shape[1])
 
 

time: 51.9 us -> 51.9 us (level)
  transfers between devices with their start and end apart: 24 -> 24, of which waited for: 10 -> 11; matrix products, arithmetic and copies ran while one was open for 0% -> 0% of each run, Pallas kernels for 37% -> 37%
where the time goes in v7:
time: 51.9 us; the launch traced here: 51.7 us
  starting transfers between devices  22.2 us (43%)
  Pallas kernels  18.9 us (36%)
  waiting for transfers between devices  10.1 us (19%)
    ppermute x24, starting transfers between devices, send(): return lax.ppermute(value, AXES, pairs)  22.2 us
    ppermute x24, waiting for transfers between devices, send(): return lax.ppermute(value, AXES, pairs)  10.1 us
    pallas_call x7, Pallas kernels, block_call(): pl.pallas_call(kernel, out_shape=(jax.ShapeDtypeStruct((max(rows, sent),...  6.72 us
    pallas_call x3, Pallas kernels, precondition(): pl.pallas_call(precondition_first_kernel if first else precondition_kerne...  5.92 us
    pallas_call x2, Pallas kernels, transpose(): pl.pallas_call(functools.partial(transpose_kernel, layer), out_shape=pltp...  5.31 us
  transfers between devices with their start and end apart: 24, of which 11 were waited for; matrix products, arithmetic and copies ran while one was open for 0% of the time, Pallas kernels for 37%

profile of v7, /device:TPU:0, one launch (start us, length us, event | category | flops | bytes accessed | tf_op | source)
XLA Modules:
  0.0 51.7 jit_solution(14169901633631833877)
XLA Ops:
  0.5 2.6 %collective-permute-start = (bf16[2,32,4096]{2,1,0:T(8,128)(2,1)}, bf16[2,32,4096]{2,1,0:T(8,128)(2,1)S(1)}, u32[]{:S(2)}, u32[]{:S(2)}) collective-permute-start(bf16[2,32,4096]{2,1,0:T(8,128)(2,1)} %query_hbm.1), channel_id=1, source_target_pairs={{0,4},{1,3},{2,0},{3,7},{4,8},{5,1},{6,2},{7,11},{8,12},{9,5},{10,... | collective-permute-start | bytes 1572872 | tf_op jit(solution)/shard_map/ppermute | solution.py:342
  3.0 2.1 %collective-permute-start.5 = (bf16[2,32,4096]{2,1,0:T(8,128)(2,1)S(1)}, bf16[2,32,4096]{2,1,0:T(8,128)(2,1)S(1)}, u32[]{:S(2)}, u32[]{:S(2)}) collective-permute-start(bf16[2,32,4096]{2,1,0:T(8,128)(2,1)S(1)} %collective-permute-done.4), channel_id=1, source_target_pairs={{0,4},{1,3},{2,0},{3,7},{4,8},{5,1},{6,2},{7,11},{8,12},{9,5},{10,... | collective-permute-start | bytes 1572872 | tf_op jit(solution)/shard_map/ppermute | solution.py:342
  5.1 2.6 %transpose_0.1.turned = bf16[4096,512]{1,0:T(8,128)(2,1)S(1)} custom-call(bf16[2,512,4096]{2,1,0:T(8,128)(2,1)} %train.3), custom_call_target="tpu_custom_call" | custom-call | flops 2147483648 | bytes 8388608 | tf_op jit(solution)/shard_map/transpose_0/pallas_call | solution.py:122
  7.8 2.7 %transpose_1.1.more.turned = bf16[4096,512]{1,0:T(8,128)(2,1)S(1)} custom-call(bf16[2,512,4096]{2,1,0:T(8,128)(2,1)} %train.3), custom_call_target="tpu_custom_call" | custom-call | flops 2147483648 | bytes 8388608 | tf_op jit(solution)/shard_map/transpose_1/pallas_call | solution.py:122
  10.5 1.6 %precondition_1.2.refs_0_ = bf16[2,32,4096]{2,1,0:T(8,128)(2,1)S(1)} custom-call(bf16[2,32,4096]{2,1,0:T(8,128)(2,1)S(1)} %collective-permute-done.query, f32[2,64,64]{2,1,0:T(8,128)S(1)} %copy-done, f32[2,64,64]{2,1,0:T(8,128)S(1)} %copy-done.1), custom_call_target="tpu_custom_call" | custom-call | flops 2147483648 | bytes 4194304 | tf_op jit(solution)/shard_map/precondition_1/pallas_call | solution.py:90
  12.2 2.0 %collective-permute-start.1 = (bf16[2,32,4096]{2,1,0:T(8,128)(2,1)S(1)}, bf16[2,32,4096]{2,1,0:T(8,128)(2,1)S(1)}, u32[]{:S(2)}, u32[]{:S(2)}) collective-permute-start(bf16[2,32,4096]{2,1,0:T(8,128)(2,1)S(1)} %precondition_1.2.refs_0_), channel_id=1, source_target_pairs={{0,4},{1,3},{2,0},{3,7},{4,8},{5,1},{6,2},{7,11},{8,12},{9,5},{10,... | collective-permute-start | bytes 1572872 | tf_op jit(solution)/shard_map/ppermute | solution.py:342
  14.2 1.8 %collective-permute-done.5.query = bf16[2,32,4096]{2,1,0:T(8,128)(2,1)S(1)} collective-permute-done((bf16[2,32,4096]{2,1,0:T(8,128)(2,1)S(1)}, bf16[2,32,4096]{2,1,0:T(8,128)(2,1)S(1)}, u32[]{:S(2)}, u32[]{:S(2)}) %collective-permute-start.5) | collective-permute-done | bytes 524320 | tf_op jit(solution)/shard_map/ppermute | solution.py:342
  15.9 1.6 %precondition_1.3.refs_1_ = bf16[2,32,4096]{2,1,0:T(8,128)(2,1)S(1)} custom-call(bf16[2,32,4096]{2,1,0:T(8,128)(2,1)S(1)} %collective-permute-done.5.query, f32[2,64,64]{2,1,0:T(8,128)S(1)} %copy-done, f32[2,64,64]{2,1,0:T(8,128)S(1)} %copy-done.1), custom_call_target="tpu_custom_call" | custom-call | flops 2147483648 | bytes 4194304 | tf_op jit(solution)/shard_map/precondition_1/pallas_call | solution.py:90
  17.6 2.2 %collective-permute-start.6 = (bf16[2,32,4096]{2,1,0:T(8,128)(2,1)S(1)}, bf16[2,32,4096]{2,1,0:T(8,128)(2,1)S(1)}, u32[]{:S(2)}, u32[]{:S(2)}) collective-permute-start(bf16[2,32,4096]{2,1,0:T(8,128)(2,1)S(1)} %precondition_1.3.refs_1_), channel_id=1, source_target_pairs={{0,4},{1,3},{2,0},{3,7},{4,8},{5,1},{6,2},{7,11},{8,12},{9,5},{10,... | collective-permute-start | bytes 1572872 | tf_op jit(solution)/shard_map/ppermute | solution.py:342
  19.8 2.7 %precondition_0.1.refs_0_ = bf16[2,32,4096]{2,1,0:T(8,128)(2,1)S(1)} custom-call(bf16[2,32,4096]{2,1,0:T(8,128)(2,1)} %query_hbm.1, f32[2,64,64]{2,1,0:T(8,128)} %left.3, f32[2,64,64]{2,1,0:T(8,128)} %right.3), custom_call_target="tpu_custom_call" | custom-call | flops 2147483648 | bytes 4194304 | tf_op jit(solution)/shard_map/precondition_0/pallas_call | solution.py:90
  23.1 1.6 %collective-permute-start.2 = (bf16[2,32,4096]{2,1,0:T(8,128)(2,1)S(1)}, bf16[2,32,4096]{2,1,0:T(8,128)(2,1)S(1)}, u32[]{:S(2)}, u32[]{:S(2)}) collective-permute-start(bf16[2,32,4096]{2,1,0:T(8,128)(2,1)S(1)} %collective-permute-done.1.refs_0_), channel_id=1, source_target_pairs={{0,4},{1,3},{2,0},{3,7},{4,8},{5,1},{6,2},{7,11},{8,12},{9,5},{10,... | collective-permute-start | bytes 1572872 | tf_op jit(solution)/shard_map/ppermute | solution.py:342
  24.7 1.2 %scores_1.1.first = f32[128,512]{1,0:T(8,128)S(1)} custom-call(bf16[4096,512]{1,0:T(8,128)(2,1)S(1)} %transpose_0.1.turned, bf16[4096,512]{1,0:T(8,128)(2,1)S(1)} %transpose_1.1.more.turned, bf16[2,32,4096]{2,1,0:T(8,128)(2,1)S(1)} %precondition_1.2.refs_0_, bf16[2,32,4096]{2,1,0:T(8,128)(2,1)S(1)} %precondition_1.3.refs_1_, ...), custom_call_target="tpu_custom_call" | custom-call | flops 1024 | bytes 1024 | tf_op jit(solution)/shard_map/scores_1/pallas_call | solution.py:246
  25.9 1.2 %collective-permute-done.6.refs_1_ = bf16[2,32,4096]{2,1,0:T(8,128)(2,1)S(1)} collective-permute-done((bf16[2,32,4096]{2,1,0:T(8,128)(2,1)S(1)}, bf16[2,32,4096]{2,1,0:T(8,128)(2,1)S(1)}, u32[]{:S(2)}, u32[]{:S(2)}) %collective-permute-start.6) | collective-permute-done | bytes 524320 | tf_op jit(solution)/shard_map/ppermute | solution.py:342
  27.2 2.1 %collective-permute-start.13 = (bf16[2,32,4096]{2,1,0:T(8,128)(2,1)S(1)}, bf16[2,32,4096]{2,1,0:T(8,128)(2,1)S(1)}, u32[]{:S(2)}, u32[]{:S(2)}) collective-permute-start(bf16[2,32,4096]{2,1,0:T(8,128)(2,1)S(1)} %collective-permute-done.6.refs_1_), channel_id=1, source_target_pairs={{0,4},{1,3},{2,0},{3,7},{4,8},{5,1},{6,2},{7,11},{8,12},{9,5},{10,... | collective-permute-start | bytes 1572872 | tf_op jit(solution)/shard_map/ppermute | solution.py:342
  29.9 1.2 %scores_0.1.own = f32[64,512]{1,0:T(8,128)S(1)} custom-call(bf16[4096,512]{1,0:T(8,128)(2,1)S(1)} %transpose_0.1.turned, bf16[4096,512]{1,0:T(8,128)(2,1)S(1)} %transpose_1.1.more.turned, bf16[2,32,4096]{2,1,0:T(8,128)(2,1)S(1)} %precondition_0.1.refs_0_, bf16[2,32,4096]{2,1,0:T(8,128)(2,1)S(1)} %collective-permute-done.3.refs_1_), custom_call_target="tpu_custom_call" | custom-call | flops 1024 | bytes 1024 | tf_op jit(solution)/shard_map/scores_0/pallas_call | solution.py:246
  31.3 1.3 %scores_2.1 = (bf16[128,512]{1,0:T(8,128)(2,1)S(1)}, f32[64,512]{1,0:T(8,128)S(1)}) custom-call(bf16[4096,512]{1,0:T(8,128)(2,1)S(1)} %transpose_0.1.turned, bf16[4096,512]{1,0:T(8,128)(2,1)S(1)} %transpose_1.1.more.turned, f32[64,512]{1,0:T(8,128)S(1)} %scores_0.1.own, bf16[2,32,4096]{2,1,0:T(8,128)(2,1)S(1)} %collective-permute-done.1.refs_0_, ...), custom_call_target="tpu_custom_call" | custom-call | flops 1024 | bytes 1024 | tf_op jit(solution)/shard_map/scores_2/pallas_call | solution.py:246
  32.6 1.6 %collective-permute-start.14 = (bf16[128,512]{1,0:T(8,128)(2,1)S(1)}, bf16[128,512]{1,0:T(8,128)(2,1)S(1)}, u32[]{:S(2)}, u32[]{:S(2)}) collective-permute-start(bf16[128,512]{1,0:T(8,128)(2,1)S(1)} %get-tuple-element.22), channel_id=1, source_target_pairs={{0,16},{1,17},{2,18},{3,19},{4,20},{5,21},{6,22},{7,23},{8,24},{9,... | collective-permute-start | bytes 393224 | tf_op jit(solution)/shard_map/ppermute | solution.py:342
  34.2 1.6 %collective-permute-start.12 = (bf16[2,32,4096]{2,1,0:T(8,128)(2,1)S(1)}, bf16[2,32,4096]{2,1,0:T(8,128)(2,1)S(1)}, u32[]{:S(2)}, u32[]{:S(2)}) collective-permute-start(bf16[2,32,4096]{2,1,0:T(8,128)(2,1)S(1)} %collective-permute-done.2.refs_0_), channel_id=1, source_target_pairs={{0,4},{1,3},{2,0},{3,7},{4,8},{5,1},{6,2},{7,11},{8,12},{9,5},{10,... | collective-permute-start | bytes 1572872 | tf_op jit(solution)/shard_map/ppermute | solution.py:342
  35.7 2.4 %collective-permute-done.14.got2 = bf16[128,512]{1,0:T(8,128)(2,1)S(1)} collective-permute-done((bf16[128,512]{1,0:T(8,128)(2,1)S(1)}, bf16[128,512]{1,0:T(8,128)(2,1)S(1)}, u32[]{:S(2)}, u32[]{:S(2)}) %collective-permute-start.14) | collective-permute-done | bytes 131104 | tf_op jit(solution)/shard_map/ppermute | solution.py:342
  39.0 1.0 %collective-permute-done.16.refs_3_ = bf16[1,32,4096]{2,1,0:T(8,128)(2,1)S(1)} collective-permute-done((bf16[1,32,4096]{2,1,0:T(8,128)(2,1)S(1)}, bf16[1,32,4096]{2,1,0:T(8,128)(2,1)S(1)}, u32[]{:S(2)}, u32[]{:S(2)}) %collective-permute-start.16) | collective-permute-done | bytes 262176 | tf_op jit(solution)/shard_map/ppermute | solution.py:342
  40.4 1.5 %scores_3.1 = (bf16[160,512]{1,0:T(8,128)(2,1)S(1)}, f32[128,512]{1,0:T(8,128)S(1)}) custom-call(bf16[4096,512]{1,0:T(8,128)(2,1)S(1)} %transpose_0.1.turned, bf16[4096,512]{1,0:T(8,128)(2,1)S(1)} %transpose_1.1.more.turned, f32[128,512]{1,0:T(8,128)S(1)} %scores_1.1.first, bf16[2,32,4096]{2,1,0:T(8,128)(2,1)S(1)} %collective-permute-done.2.refs_0_, ...), custom_call_target="tpu_custom_call" | custom-call | flops 1024 | bytes 1024 | tf_op jit(solution)/shard_map/scores_3/pallas_call | solution.py:246
  41.9 2.1 %collective-permute-start.23 = (bf16[160,512]{1,0:T(8,128)(2,1)S(1)}, bf16[160,512]{1,0:T(8,128)(2,1)S(1)}, u32[]{:S(2)}, u32[]{:S(2)}) collective-permute-start(bf16[160,512]{1,0:T(8,128)(2,1)S(1)} %get-tuple-element.26), channel_id=1, source_target_pairs={{0,16},{1,17},{2,18},{3,19},{4,20},{5,21},{6,22},{7,23},{8,24},{9,... | collective-permute-start | bytes 491528 | tf_op jit(solution)/shard_map/ppermute | solution.py:342
  47.2 1.1 %collective-permute-start.22 = (bf16[64,512]{1,0:T(8,128)(2,1)S(1)}, bf16[64,512]{1,0:T(8,128)(2,1)S(1)}, u32[]{:S(2)}, u32[]{:S(2)}) collective-permute-start(bf16[64,512]{1,0:T(8,128)(2,1)S(1)} %scores_5.1), channel_id=1, source_target_pairs={{0,16},{1,17},{2,18},{3,19},{4,20},{5,21},{6,22},{7,23},{8,24},{9,... | collective-permute-start | bytes 196616 | tf_op jit(solution)/shard_map/ppermute | solution.py:342
  49.5 2.1 %collective-permute-done.22.got = bf16[64,512]{1,0:T(8,128)(2,1)S(1)} collective-permute-done((bf16[64,512]{1,0:T(8,128)(2,1)S(1)}, bf16[64,512]{1,0:T(8,128)(2,1)S(1)}, u32[]{:S(2)}, u32[]{:S(2)}) %collective-permute-start.22) | collective-permute-done | bytes 65568 | tf_op jit(solution)/shard_map/ppermute | solution.py:342
  (45 shorter events, 7.5 us)
Async XLA Ops:
  0.0 3.0 %collective-permute-start.4 = (bf16[2,32,4096]{2,1,0:T(8,128)(2,1)}, bf16[2,32,4096]{2,1,0:T(8,128)(2,1)S(1)}, u32[]{:S(2)}, u32[]{:S(2)}) collective-permute-start(bf16[2,32,4096]{2,1,0:T(8,128)(2,1)} %query_hbm.1), channel_id=1, source_target_pairs={{0,1},{1,0},{2,3},{3,2},{4,5},{5,4},{6,7},{7,6},{8,9},{9,8},{10,11... | collective-permute-start | bytes 1572872 | tf_op jit(solution)/shard_map/ppermute | solution.py:342
  0.5 10.0 %collective-permute-start = (bf16[2,32,4096]{2,1,0:T(8,128)(2,1)}, bf16[2,32,4096]{2,1,0:T(8,128)(2,1)S(1)}, u32[]{:S(2)}, u32[]{:S(2)}) collective-permute-start(bf16[2,32,4096]{2,1,0:T(8,128)(2,1)} %query_hbm.1), channel_id=1, source_target_pairs={{0,4},{1,3},{2,0},{3,7},{4,8},{5,1},{6,2},{7,11},{8,12},{9,5},{10,... | collective-permute-start | bytes 1572872 | tf_op jit(solution)/shard_map/ppermute | solution.py:342
  3.0 12.9 %collective-permute-start.5 = (bf16[2,32,4096]{2,1,0:T(8,128)(2,1)S(1)}, bf16[2,32,4096]{2,1,0:T(8,128)(2,1)S(1)}, u32[]{:S(2)}, u32[]{:S(2)}) collective-permute-start(bf16[2,32,4096]{2,1,0:T(8,128)(2,1)S(1)} %collective-permute-done.4), channel_id=1, source_target_pairs={{0,4},{1,3},{2,0},{3,7},{4,8},{5,1},{6,2},{7,11},{8,12},{9,5},{10,... | collective-permute-start | bytes 1572872 | tf_op jit(solution)/shard_map/ppermute | solution.py:342
  12.1 11.0 %collective-permute-start.7 = (bf16[2,32,4096]{2,1,0:T(8,128)(2,1)S(1)}, bf16[2,32,4096]{2,1,0:T(8,128)(2,1)S(1)}, u32[]{:S(2)}, u32[]{:S(2)}) collective-permute-start(bf16[2,32,4096]{2,1,0:T(8,128)(2,1)S(1)} %precondition_1.2.refs_0_), channel_id=1, source_target_pairs={{0,1},{1,0},{2,3},{3,2},{4,5},{5,4},{6,7},{7,6},{8,9},{9,8},{10,11... | collective-permute-start | bytes 1572872 | tf_op jit(solution)/shard_map/ppermute | solution.py:342
  12.2 10.4 %collective-permute-start.1 = (bf16[2,32,4096]{2,1,0:T(8,128)(2,1)S(1)}, bf16[2,32,4096]{2,1,0:T(8,128)(2,1)S(1)}, u32[]{:S(2)}, u32[]{:S(2)}) collective-permute-start(bf16[2,32,4096]{2,1,0:T(8,128)(2,1)S(1)} %precondition_1.2.refs_0_), channel_id=1, source_target_pairs={{0,4},{1,3},{2,0},{3,7},{4,8},{5,1},{6,2},{7,11},{8,12},{9,5},{10,... | collective-permute-start | bytes 1572872 | tf_op jit(solution)/shard_map/ppermute | solution.py:342
  17.5 7.1 %collective-permute-start.8 = (bf16[2,32,4096]{2,1,0:T(8,128)(2,1)S(1)}, bf16[2,32,4096]{2,1,0:T(8,128)(2,1)S(1)}, u32[]{:S(2)}, u32[]{:S(2)}) collective-permute-start(bf16[2,32,4096]{2,1,0:T(8,128)(2,1)S(1)} %precondition_1.3.refs_1_), channel_id=1, source_target_pairs={{0,1},{1,0},{2,3},{3,2},{4,5},{5,4},{6,7},{7,6},{8,9},{9,8},{10,11... | collective-permute-start | bytes 1572872 | tf_op jit(solution)/shard_map/ppermute | solution.py:342
  17.6 9.5 %collective-permute-start.6 = (bf16[2,32,4096]{2,1,0:T(8,128)(2,1)S(1)}, bf16[2,32,4096]{2,1,0:T(8,128)(2,1)S(1)}, u32[]{:S(2)}, u32[]{:S(2)}) collective-permute-start(bf16[2,32,4096]{2,1,0:T(8,128)(2,1)S(1)} %precondition_1.3.refs_1_), channel_id=1, source_target_pairs={{0,4},{1,3},{2,0},{3,7},{4,8},{5,1},{6,2},{7,11},{8,12},{9,5},{10,... | collective-permute-start | bytes 1572872 | tf_op jit(solution)/shard_map/ppermute | solution.py:342
  22.5 6.9 %collective-permute-start.3 = (bf16[2,32,4096]{2,1,0:T(8,128)(2,1)S(1)}, bf16[2,32,4096]{2,1,0:T(8,128)(2,1)S(1)}, u32[]{:S(2)}, u32[]{:S(2)}) collective-permute-start(bf16[2,32,4096]{2,1,0:T(8,128)(2,1)S(1)} %precondition_0.1.refs_0_), channel_id=1, source_target_pairs={{0,1},{1,0},{2,3},{3,2},{4,5},{5,4},{6,7},{7,6},{8,9},{9,8},{10,11... | collective-permute-start | bytes 1572872 | tf_op jit(solution)/shard_map/ppermute | solution.py:342
  22.7 8.5 %collective-permute-start.9 = (bf16[2,32,4096]{2,1,0:T(8,128)(2,1)S(1)}, bf16[2,32,4096]{2,1,0:T(8,128)(2,1)S(1)}, u32[]{:S(2)}, u32[]{:S(2)}) collective-permute-start(bf16[2,32,4096]{2,1,0:T(8,128)(2,1)S(1)} %collective-permute-done.1.refs_0_), channel_id=1, source_target_pairs={{0,1},{1,0},{2,3},{3,2},{4,5},{5,4},{6,7},{7,6},{8,9},{9,8},{10,11... | collective-permute-start | bytes 1572872 | tf_op jit(solution)/shard_map/ppermute | solution.py:342
  23.1 11.1 %collective-permute-start.2 = (bf16[2,32,4096]{2,1,0:T(8,128)(2,1)S(1)}, bf16[2,32,4096]{2,1,0:T(8,128)(2,1)S(1)}, u32[]{:S(2)}, u32[]{:S(2)}) collective-permute-start(bf16[2,32,4096]{2,1,0:T(8,128)(2,1)S(1)} %collective-permute-done.1.refs_0_), channel_id=1, source_target_pairs={{0,4},{1,3},{2,0},{3,7},{4,8},{5,1},{6,2},{7,11},{8,12},{9,5},{10,... | collective-permute-start | bytes 1572872 | tf_op jit(solution)/shard_map/ppermute | solution.py:342
  27.2 11.2 %collective-permute-start.13 = (bf16[2,32,4096]{2,1,0:T(8,128)(2,1)S(1)}, bf16[2,32,4096]{2,1,0:T(8,128)(2,1)S(1)}, u32[]{:S(2)}, u32[]{:S(2)}) collective-permute-start(bf16[2,32,4096]{2,1,0:T(8,128)(2,1)S(1)} %collective-permute-done.6.refs_1_), channel_id=1, source_target_pairs={{0,4},{1,3},{2,0},{3,7},{4,8},{5,1},{6,2},{7,11},{8,12},{9,5},{10,... | collective-permute-start | bytes 1572872 | tf_op jit(solution)/shard_map/ppermute | solution.py:342
  29.3 1.8 %collective-permute-start.10 = (bf16[1,32,4096]{2,1,0:T(8,128)(2,1)S(1)}, bf16[1,32,4096]{2,1,0:T(8,128)(2,1)S(1)}, u32[]{:S(2)}, u32[]{:S(2)}) collective-permute-start(bf16[1,32,4096]{2,1,0:T(8,128)(2,1)S(1)} %get-tuple-element.38), channel_id=1, source_target_pairs={{0,1},{1,0},{2,3},{3,2},{4,5},{5,4},{6,7},{7,6},{8,9},{9,8},{10,11... | collective-permute-start | bytes 786440 | tf_op jit(solution)/shard_map/ppermute | solution.py:342
  29.4 1.9 %collective-permute-start.11 = (bf16[1,32,4096]{2,1,0:T(8,128)(2,1)S(1)}, bf16[1,32,4096]{2,1,0:T(8,128)(2,1)S(1)}, u32[]{:S(2)}, u32[]{:S(2)}) collective-permute-start(bf16[1,32,4096]{2,1,0:T(8,128)(2,1)S(1)} %get-tuple-element.37), channel_id=1, source_target_pairs={{0,1},{1,0},{2,3},{3,2},{4,5},{5,4},{6,7},{7,6},{8,9},{9,8},{10,11... | collective-permute-start | bytes 786440 | tf_op jit(solution)/shard_map/ppermute | solution.py:342
  32.6 5.6 %collective-permute-start.14 = (bf16[128,512]{1,0:T(8,128)(2,1)S(1)}, bf16[128,512]{1,0:T(8,128)(2,1)S(1)}, u32[]{:S(2)}, u32[]{:S(2)}) collective-permute-start(bf16[128,512]{1,0:T(8,128)(2,1)S(1)} %get-tuple-element.22), channel_id=1, source_target_pairs={{0,16},{1,17},{2,18},{3,19},{4,20},{5,21},{6,22},{7,23},{8,24},{9,... | collective-permute-start | bytes 393224 | tf_op jit(solution)/shard_map/ppermute | solution.py:342
  34.2 6.3 %collective-permute-start.15 = (bf16[2,32,4096]{2,1,0:T(8,128)(2,1)S(1)}, bf16[2,32,4096]{2,1,0:T(8,128)(2,1)S(1)}, u32[]{:S(2)}, u32[]{:S(2)}) collective-permute-start(bf16[2,32,4096]{2,1,0:T(8,128)(2,1)S(1)} %collective-permute-done.2.refs_0_), channel_id=1, source_target_pairs={{0,1},{1,0},{2,3},{3,2},{4,5},{5,4},{6,7},{7,6},{8,9},{9,8},{10,11... | collective-permute-start | bytes 1572872 | tf_op jit(solution)/shard_map/ppermute | solution.py:342
  34.2 9.9 %collective-permute-start.12 = (bf16[2,32,4096]{2,1,0:T(8,128)(2,1)S(1)}, bf16[2,32,4096]{2,1,0:T(8,128)(2,1)S(1)}, u32[]{:S(2)}, u32[]{:S(2)}) collective-permute-start(bf16[2,32,4096]{2,1,0:T(8,128)(2,1)S(1)} %collective-permute-done.2.refs_0_), channel_id=1, source_target_pairs={{0,4},{1,3},{2,0},{3,7},{4,8},{5,1},{6,2},{7,11},{8,12},{9,5},{10,... | collective-permute-start | bytes 1572872 | tf_op jit(solution)/shard_map/ppermute | solution.py:342
  38.4 1.6 %collective-permute-start.16 = (bf16[1,32,4096]{2,1,0:T(8,128)(2,1)S(1)}, bf16[1,32,4096]{2,1,0:T(8,128)(2,1)S(1)}, u32[]{:S(2)}, u32[]{:S(2)}) collective-permute-start(bf16[1,32,4096]{2,1,0:T(8,128)(2,1)S(1)} %get-tuple-element.36), channel_id=1, source_target_pairs={{0,1},{1,0},{2,3},{3,2},{4,5},{5,4},{6,7},{7,6},{8,9},{9,8},{10,11... | collective-permute-start | bytes 786440 | tf_op jit(solution)/shard_map/ppermute | solution.py:342
  38.5 1.9 %collective-permute-start.17 = (bf16[1,32,4096]{2,1,0:T(8,128)(2,1)S(1)}, bf16[1,32,4096]{2,1,0:T(8,128)(2,1)S(1)}, u32[]{:S(2)}, u32[]{:S(2)}) collective-permute-start(bf16[1,32,4096]{2,1,0:T(8,128)(2,1)S(1)} %get-tuple-element.35), channel_id=1, source_target_pairs={{0,1},{1,0},{2,3},{3,2},{4,5},{5,4},{6,7},{7,6},{8,9},{9,8},{10,11... | collective-permute-start | bytes 786440 | tf_op jit(solution)/shard_map/ppermute | solution.py:342
  41.9 6.6 %collective-permute-start.23 = (bf16[160,512]{1,0:T(8,128)(2,1)S(1)}, bf16[160,512]{1,0:T(8,128)(2,1)S(1)}, u32[]{:S(2)}, u32[]{:S(2)}) collective-permute-start(bf16[160,512]{1,0:T(8,128)(2,1)S(1)} %get-tuple-element.26), channel_id=1, source_target_pairs={{0,16},{1,17},{2,18},{3,19},{4,20},{5,21},{6,22},{7,23},{8,24},{9,... | collective-permute-start | bytes 491528 | tf_op jit(solution)/shard_map/ppermute | solution.py:342
  44.1 1.4 %collective-permute-start.18 = (bf16[1,16,4096]{2,1,0:T(8,128)(2,1)S(1)}, bf16[1,16,4096]{2,1,0:T(8,128)(2,1)S(1)}, u32[]{:S(2)}, u32[]{:S(2)}) collective-permute-start(bf16[1,16,4096]{2,1,0:T(8,128)(2,1)S(1)} %get-tuple-element.34), channel_id=1, source_target_pairs={{0,1},{1,0},{2,3},{3,2},{4,5},{5,4},{6,7},{7,6},{8,9},{9,8},{10,11... | collective-permute-start | bytes 393224 | tf_op jit(solution)/shard_map/ppermute | solution.py:342
  44.1 1.5 %collective-permute-start.19 = (bf16[1,16,4096]{2,1,0:T(8,128)(2,1)S(1)}, bf16[1,16,4096]{2,1,0:T(8,128)(2,1)S(1)}, u32[]{:S(2)}, u32[]{:S(2)}) collective-permute-start(bf16[1,16,4096]{2,1,0:T(8,128)(2,1)S(1)} %get-tuple-element.33), channel_id=1, source_target_pairs={{0,1},{1,0},{2,3},{3,2},{4,5},{5,4},{6,7},{7,6},{8,9},{9,8},{10,11... | collective-permute-start | bytes 393224 | tf_op jit(solution)/shard_map/ppermute | solution.py:342
  44.6 1.7 %collective-permute-start.20 = (bf16[1,16,4096]{2,1,0:T(8,128)(2,1)S(1)}, bf16[1,16,4096]{2,1,0:T(8,128)(2,1)S(1)}, u32[]{:S(2)}, u32[]{:S(2)}) collective-permute-start(bf16[1,16,4096]{2,1,0:T(8,128)(2,1)S(1)} %get-tuple-element.32), channel_id=1, source_target_pairs={{0,1},{1,0},{2,3},{3,2},{4,5},{5,4},{6,7},{7,6},{8,9},{9,8},{10,11... | collective-permute-start | bytes 393224 | tf_op jit(solution)/shard_map/ppermute | solution.py:342
  44.7 1.7 %collective-permute-start.21 = (bf16[1,16,4096]{2,1,0:T(8,128)(2,1)S(1)}, bf16[1,16,4096]{2,1,0:T(8,128)(2,1)S(1)}, u32[]{:S(2)}, u32[]{:S(2)}) collective-permute-start(bf16[1,16,4096]{2,1,0:T(8,128)(2,1)S(1)} %get-tuple-element.31), channel_id=1, source_target_pairs={{0,1},{1,0},{2,3},{3,2},{4,5},{5,4},{6,7},{7,6},{8,9},{9,8},{10,11... | collective-permute-start | bytes 393224 | tf_op jit(solution)/shard_map/ppermute | solution.py:342
  47.2 4.4 %collective-permute-start.22 = (bf16[64,512]{1,0:T(8,128)(2,1)S(1)}, bf16[64,512]{1,0:T(8,128)(2,1)S(1)}, u32[]{:S(2)}, u32[]{:S(2)}) collective-permute-start(bf16[64,512]{1,0:T(8,128)(2,1)S(1)} %scores_5.1), channel_id=1, source_target_pairs={{0,16},{1,17},{2,18},{3,19},{4,20},{5,21},{6,22},{7,23},{8,24},{9,... | collective-permute-start | bytes 196616 | tf_op jit(solution)/shard_map/ppermute | solution.py:342
  (2 other events, 5.4 us)

commit v8 on v6

--- a/solution.py
+++ b/solution.py
@@ -300,7 +300,7 @@
         in_specs=[VMEM] * 5,
         out_specs=VMEM,
         compiler_params=params,
-        cost_estimate=pl.CostEstimate(flops=1 << 30, bytes_accessed=1 << 20, transcendentals=0),
+        cost_estimate=pl.CostEstimate(flops=60 << 30, bytes_accessed=1 << 20, transcendentals=0),
         name="gather_rows",
     )(*most)
     return pl.pallas_call(
@@ -403,7 +403,7 @@
     got2 = send(sent2, across)
     b[3], got2 = after((b[3], got2))
     queries = [a[3], b[3], send(a[3], swap), *halves_of(b[3])]
-    sent, kept = block_call(third_kernel, "scores_3", 2 * rows, 2 * rows, turned, [first] + queries, jnp.bfloat16, 2 * rows + 16)
+    sent, kept = block_call(third_kernel, "scores_3", 2 * rows, 2 * rows, turned, [first] + queries, jnp.bfloat16, 2 * rows + 32)
     got = send(sent, across)
     a[4], _ = after((a[4], sent))
     swapped = quarters(a[4])

time: 51.9 us -> 51.9 us (level)
  no operation moved by 1% of the time
where the time goes in v8:
time: 51.9 us; the launch traced here: 51.7 us
  starting transfers between devices  22.6 us (44%)
  Pallas kernels  18.9 us (36%)
  waiting for transfers between devices  9.75 us (19%)
    ppermute x24, starting transfers between devices, send(): return lax.ppermute(value, AXES, pairs)  22.6 us
    ppermute x24, waiting for transfers between devices, send(): return lax.ppermute(value, AXES, pairs)  9.75 us
    pallas_call x7, Pallas kernels, block_call(): pl.pallas_call(kernel, out_shape=(jax.ShapeDtypeStruct((max(rows, sent),...  6.71 us
    pallas_call x3, Pallas kernels, precondition(): pl.pallas_call(precondition_first_kernel if first else precondition_kerne...  5.92 us
    pallas_call x2, Pallas kernels, transpose(): pl.pallas_call(functools.partial(transpose_kernel, layer), out_shape=pltp...  5.31 us
  transfers between devices with their start and end apart: 24, of which 10 were waited for; matrix products, arithmetic and copies ran while one was open for 0% of the time, Pallas kernels for 37%

profile of v8, /device:TPU:0, one launch (start us, length us, event | category | flops | bytes accessed | tf_op | source)
XLA Modules:
  0.0 51.7 jit_solution(3045504587814243522)
XLA Ops:
  0.5 2.6 %collective-permute-start = (bf16[2,32,4096]{2,1,0:T(8,128)(2,1)}, bf16[2,32,4096]{2,1,0:T(8,128)(2,1)S(1)}, u32[]{:S(2)}, u32[]{:S(2)}) collective-permute-start(bf16[2,32,4096]{2,1,0:T(8,128)(2,1)} %query_hbm.1), channel_id=1, source_target_pairs={{0,4},{1,3},{2,0},{3,7},{4,8},{5,1},{6,2},{7,11},{8,12},{9,5},{10,... | collective-permute-start | bytes 1572872 | tf_op jit(solution)/shard_map/ppermute | solution.py:339
  3.0 2.1 %collective-permute-start.5 = (bf16[2,32,4096]{2,1,0:T(8,128)(2,1)S(1)}, bf16[2,32,4096]{2,1,0:T(8,128)(2,1)S(1)}, u32[]{:S(2)}, u32[]{:S(2)}) collective-permute-start(bf16[2,32,4096]{2,1,0:T(8,128)(2,1)S(1)} %collective-permute-done.4), channel_id=1, source_target_pairs={{0,4},{1,3},{2,0},{3,7},{4,8},{5,1},{6,2},{7,11},{8,12},{9,5},{10,... | collective-permute-start | bytes 1572872 | tf_op jit(solution)/shard_map/ppermute | solution.py:339
  5.1 2.6 %transpose_0.1.turned = bf16[4096,512]{1,0:T(8,128)(2,1)S(1)} custom-call(bf16[2,512,4096]{2,1,0:T(8,128)(2,1)} %train.3), custom_call_target="tpu_custom_call" | custom-call | flops 2147483648 | bytes 8388608 | tf_op jit(solution)/shard_map/transpose_0/pallas_call | solution.py:122
  7.8 2.7 %transpose_1.1.more.turned = bf16[4096,512]{1,0:T(8,128)(2,1)S(1)} custom-call(bf16[2,512,4096]{2,1,0:T(8,128)(2,1)} %train.3), custom_call_target="tpu_custom_call" | custom-call | flops 2147483648 | bytes 8388608 | tf_op jit(solution)/shard_map/transpose_1/pallas_call | solution.py:122
  10.5 1.6 %precondition_1.2.refs_0_ = bf16[2,32,4096]{2,1,0:T(8,128)(2,1)S(1)} custom-call(bf16[2,32,4096]{2,1,0:T(8,128)(2,1)S(1)} %collective-permute-done.query, f32[2,64,64]{2,1,0:T(8,128)S(1)} %copy-done, f32[2,64,64]{2,1,0:T(8,128)S(1)} %copy-done.1), custom_call_target="tpu_custom_call" | custom-call | flops 2147483648 | bytes 4194304 | tf_op jit(solution)/shard_map/precondition_1/pallas_call | solution.py:90
  12.2 2.0 %collective-permute-start.1 = (bf16[2,32,4096]{2,1,0:T(8,128)(2,1)S(1)}, bf16[2,32,4096]{2,1,0:T(8,128)(2,1)S(1)}, u32[]{:S(2)}, u32[]{:S(2)}) collective-permute-start(bf16[2,32,4096]{2,1,0:T(8,128)(2,1)S(1)} %precondition_1.2.refs_0_), channel_id=1, source_target_pairs={{0,4},{1,3},{2,0},{3,7},{4,8},{5,1},{6,2},{7,11},{8,12},{9,5},{10,... | collective-permute-start | bytes 1572872 | tf_op jit(solution)/shard_map/ppermute | solution.py:339
  14.2 1.8 %collective-permute-done.5.query = bf16[2,32,4096]{2,1,0:T(8,128)(2,1)S(1)} collective-permute-done((bf16[2,32,4096]{2,1,0:T(8,128)(2,1)S(1)}, bf16[2,32,4096]{2,1,0:T(8,128)(2,1)S(1)}, u32[]{:S(2)}, u32[]{:S(2)}) %collective-permute-start.5) | collective-permute-done | bytes 524320 | tf_op jit(solution)/shard_map/ppermute | solution.py:339
  15.9 1.6 %precondition_1.3.refs_1_ = bf16[2,32,4096]{2,1,0:T(8,128)(2,1)S(1)} custom-call(bf16[2,32,4096]{2,1,0:T(8,128)(2,1)S(1)} %collective-permute-done.5.query, f32[2,64,64]{2,1,0:T(8,128)S(1)} %copy-done, f32[2,64,64]{2,1,0:T(8,128)S(1)} %copy-done.1), custom_call_target="tpu_custom_call" | custom-call | flops 2147483648 | bytes 4194304 | tf_op jit(solution)/shard_map/precondition_1/pallas_call | solution.py:90
  17.6 2.2 %collective-permute-start.6 = (bf16[2,32,4096]{2,1,0:T(8,128)(2,1)S(1)}, bf16[2,32,4096]{2,1,0:T(8,128)(2,1)S(1)}, u32[]{:S(2)}, u32[]{:S(2)}) collective-permute-start(bf16[2,32,4096]{2,1,0:T(8,128)(2,1)S(1)} %precondition_1.3.refs_1_), channel_id=1, source_target_pairs={{0,4},{1,3},{2,0},{3,7},{4,8},{5,1},{6,2},{7,11},{8,12},{9,5},{10,... | collective-permute-start | bytes 1572872 | tf_op jit(solution)/shard_map/ppermute | solution.py:339
  19.8 2.7 %precondition_0.1.refs_0_ = bf16[2,32,4096]{2,1,0:T(8,128)(2,1)S(1)} custom-call(bf16[2,32,4096]{2,1,0:T(8,128)(2,1)} %query_hbm.1, f32[2,64,64]{2,1,0:T(8,128)} %left.3, f32[2,64,64]{2,1,0:T(8,128)} %right.3), custom_call_target="tpu_custom_call" | custom-call | flops 2147483648 | bytes 4194304 | tf_op jit(solution)/shard_map/precondition_0/pallas_call | solution.py:90
  23.1 1.6 %collective-permute-start.2 = (bf16[2,32,4096]{2,1,0:T(8,128)(2,1)S(1)}, bf16[2,32,4096]{2,1,0:T(8,128)(2,1)S(1)}, u32[]{:S(2)}, u32[]{:S(2)}) collective-permute-start(bf16[2,32,4096]{2,1,0:T(8,128)(2,1)S(1)} %collective-permute-done.1.refs_0_), channel_id=1, source_target_pairs={{0,4},{1,3},{2,0},{3,7},{4,8},{5,1},{6,2},{7,11},{8,12},{9,5},{10,... | collective-permute-start | bytes 1572872 | tf_op jit(solution)/shard_map/ppermute | solution.py:339
  24.7 1.2 %scores_1.1.first = f32[128,512]{1,0:T(8,128)S(1)} custom-call(bf16[4096,512]{1,0:T(8,128)(2,1)S(1)} %transpose_0.1.turned, bf16[4096,512]{1,0:T(8,128)(2,1)S(1)} %transpose_1.1.more.turned, bf16[2,32,4096]{2,1,0:T(8,128)(2,1)S(1)} %precondition_1.2.refs_0_, bf16[2,32,4096]{2,1,0:T(8,128)(2,1)S(1)} %precondition_1.3.refs_1_, ...), custom_call_target="tpu_custom_call" | custom-call | flops 1024 | bytes 1024 | tf_op jit(solution)/shard_map/scores_1/pallas_call | solution.py:243
  25.9 1.2 %collective-permute-done.6.refs_1_ = bf16[2,32,4096]{2,1,0:T(8,128)(2,1)S(1)} collective-permute-done((bf16[2,32,4096]{2,1,0:T(8,128)(2,1)S(1)}, bf16[2,32,4096]{2,1,0:T(8,128)(2,1)S(1)}, u32[]{:S(2)}, u32[]{:S(2)}) %collective-permute-start.6) | collective-permute-done | bytes 524320 | tf_op jit(solution)/shard_map/ppermute | solution.py:339
  27.2 2.1 %collective-permute-start.13 = (bf16[2,32,4096]{2,1,0:T(8,128)(2,1)S(1)}, bf16[2,32,4096]{2,1,0:T(8,128)(2,1)S(1)}, u32[]{:S(2)}, u32[]{:S(2)}) collective-permute-start(bf16[2,32,4096]{2,1,0:T(8,128)(2,1)S(1)} %collective-permute-done.6.refs_1_), channel_id=1, source_target_pairs={{0,4},{1,3},{2,0},{3,7},{4,8},{5,1},{6,2},{7,11},{8,12},{9,5},{10,... | collective-permute-start | bytes 1572872 | tf_op jit(solution)/shard_map/ppermute | solution.py:339
  29.9 1.2 %scores_0.1.own = f32[64,512]{1,0:T(8,128)S(1)} custom-call(bf16[4096,512]{1,0:T(8,128)(2,1)S(1)} %transpose_0.1.turned, bf16[4096,512]{1,0:T(8,128)(2,1)S(1)} %transpose_1.1.more.turned, bf16[2,32,4096]{2,1,0:T(8,128)(2,1)S(1)} %precondition_0.1.refs_0_, bf16[2,32,4096]{2,1,0:T(8,128)(2,1)S(1)} %collective-permute-done.3.refs_1_), custom_call_target="tpu_custom_call" | custom-call | flops 1024 | bytes 1024 | tf_op jit(solution)/shard_map/scores_0/pallas_call | solution.py:243
  31.3 1.3 %scores_2.1 = (bf16[128,512]{1,0:T(8,128)(2,1)S(1)}, f32[64,512]{1,0:T(8,128)S(1)}) custom-call(bf16[4096,512]{1,0:T(8,128)(2,1)S(1)} %transpose_0.1.turned, bf16[4096,512]{1,0:T(8,128)(2,1)S(1)} %transpose_1.1.more.turned, f32[64,512]{1,0:T(8,128)S(1)} %scores_0.1.own, bf16[2,32,4096]{2,1,0:T(8,128)(2,1)S(1)} %collective-permute-done.1.refs_0_, ...), custom_call_target="tpu_custom_call" | custom-call | flops 1024 | bytes 1024 | tf_op jit(solution)/shard_map/scores_2/pallas_call | solution.py:243
  32.6 1.6 %collective-permute-start.14 = (bf16[128,512]{1,0:T(8,128)(2,1)S(1)}, bf16[128,512]{1,0:T(8,128)(2,1)S(1)}, u32[]{:S(2)}, u32[]{:S(2)}) collective-permute-start(bf16[128,512]{1,0:T(8,128)(2,1)S(1)} %get-tuple-element.22), channel_id=1, source_target_pairs={{0,16},{1,17},{2,18},{3,19},{4,20},{5,21},{6,22},{7,23},{8,24},{9,... | collective-permute-start | bytes 393224 | tf_op jit(solution)/shard_map/ppermute | solution.py:339
  34.2 1.6 %collective-permute-start.12 = (bf16[2,32,4096]{2,1,0:T(8,128)(2,1)S(1)}, bf16[2,32,4096]{2,1,0:T(8,128)(2,1)S(1)}, u32[]{:S(2)}, u32[]{:S(2)}) collective-permute-start(bf16[2,32,4096]{2,1,0:T(8,128)(2,1)S(1)} %collective-permute-done.2.refs_0_), channel_id=1, source_target_pairs={{0,4},{1,3},{2,0},{3,7},{4,8},{5,1},{6,2},{7,11},{8,12},{9,5},{10,... | collective-permute-start | bytes 1572872 | tf_op jit(solution)/shard_map/ppermute | solution.py:339
  35.7 2.4 %collective-permute-done.14.got2 = bf16[128,512]{1,0:T(8,128)(2,1)S(1)} collective-permute-done((bf16[128,512]{1,0:T(8,128)(2,1)S(1)}, bf16[128,512]{1,0:T(8,128)(2,1)S(1)}, u32[]{:S(2)}, u32[]{:S(2)}) %collective-permute-start.14) | collective-permute-done | bytes 131104 | tf_op jit(solution)/shard_map/ppermute | solution.py:339
  39.0 1.0 %collective-permute-done.16.refs_3_ = bf16[1,32,4096]{2,1,0:T(8,128)(2,1)S(1)} collective-permute-done((bf16[1,32,4096]{2,1,0:T(8,128)(2,1)S(1)}, bf16[1,32,4096]{2,1,0:T(8,128)(2,1)S(1)}, u32[]{:S(2)}, u32[]{:S(2)}) %collective-permute-start.16) | collective-permute-done | bytes 262176 | tf_op jit(solution)/shard_map/ppermute | solution.py:339
  40.4 1.5 %scores_3.1 = (bf16[160,512]{1,0:T(8,128)(2,1)S(1)}, f32[128,512]{1,0:T(8,128)S(1)}) custom-call(bf16[4096,512]{1,0:T(8,128)(2,1)S(1)} %transpose_0.1.turned, bf16[4096,512]{1,0:T(8,128)(2,1)S(1)} %transpose_1.1.more.turned, f32[128,512]{1,0:T(8,128)S(1)} %scores_1.1.first, bf16[2,32,4096]{2,1,0:T(8,128)(2,1)S(1)} %collective-permute-done.2.refs_0_, ...), custom_call_target="tpu_custom_call" | custom-call | flops 1024 | bytes 1024 | tf_op jit(solution)/shard_map/scores_3/pallas_call | solution.py:243
  41.9 2.1 %collective-permute-start.23 = (bf16[160,512]{1,0:T(8,128)(2,1)S(1)}, bf16[160,512]{1,0:T(8,128)(2,1)S(1)}, u32[]{:S(2)}, u32[]{:S(2)}) collective-permute-start(bf16[160,512]{1,0:T(8,128)(2,1)S(1)} %get-tuple-element.26), channel_id=1, source_target_pairs={{0,16},{1,17},{2,18},{3,19},{4,20},{5,21},{6,22},{7,23},{8,24},{9,... | collective-permute-start | bytes 491528 | tf_op jit(solution)/shard_map/ppermute | solution.py:339
  47.2 1.4 %collective-permute-start.22 = (bf16[64,512]{1,0:T(8,128)(2,1)S(1)}, bf16[64,512]{1,0:T(8,128)(2,1)S(1)}, u32[]{:S(2)}, u32[]{:S(2)}) collective-permute-start(bf16[64,512]{1,0:T(8,128)(2,1)S(1)} %scores_5.1), channel_id=1, source_target_pairs={{0,16},{1,17},{2,18},{3,19},{4,20},{5,21},{6,22},{7,23},{8,24},{9,... | collective-permute-start | bytes 196616 | tf_op jit(solution)/shard_map/ppermute | solution.py:339
  49.5 2.0 %collective-permute-done.22.got = bf16[64,512]{1,0:T(8,128)(2,1)S(1)} collective-permute-done((bf16[64,512]{1,0:T(8,128)(2,1)S(1)}, bf16[64,512]{1,0:T(8,128)(2,1)S(1)}, u32[]{:S(2)}, u32[]{:S(2)}) %collective-permute-start.22) | collective-permute-done | bytes 65568 | tf_op jit(solution)/shard_map/ppermute | solution.py:339
  (45 shorter events, 7.2 us)
Async XLA Ops:
  0.0 3.0 %collective-permute-start.4 = (bf16[2,32,4096]{2,1,0:T(8,128)(2,1)}, bf16[2,32,4096]{2,1,0:T(8,128)(2,1)S(1)}, u32[]{:S(2)}, u32[]{:S(2)}) collective-permute-start(bf16[2,32,4096]{2,1,0:T(8,128)(2,1)} %query_hbm.1), channel_id=1, source_target_pairs={{0,1},{1,0},{2,3},{3,2},{4,5},{5,4},{6,7},{7,6},{8,9},{9,8},{10,11... | collective-permute-start | bytes 1572872 | tf_op jit(solution)/shard_map/ppermute | solution.py:339
  0.5 10.0 %collective-permute-start = (bf16[2,32,4096]{2,1,0:T(8,128)(2,1)}, bf16[2,32,4096]{2,1,0:T(8,128)(2,1)S(1)}, u32[]{:S(2)}, u32[]{:S(2)}) collective-permute-start(bf16[2,32,4096]{2,1,0:T(8,128)(2,1)} %query_hbm.1), channel_id=1, source_target_pairs={{0,4},{1,3},{2,0},{3,7},{4,8},{5,1},{6,2},{7,11},{8,12},{9,5},{10,... | collective-permute-start | bytes 1572872 | tf_op jit(solution)/shard_map/ppermute | solution.py:339
  3.0 12.9 %collective-permute-start.5 = (bf16[2,32,4096]{2,1,0:T(8,128)(2,1)S(1)}, bf16[2,32,4096]{2,1,0:T(8,128)(2,1)S(1)}, u32[]{:S(2)}, u32[]{:S(2)}) collective-permute-start(bf16[2,32,4096]{2,1,0:T(8,128)(2,1)S(1)} %collective-permute-done.4), channel_id=1, source_target_pairs={{0,4},{1,3},{2,0},{3,7},{4,8},{5,1},{6,2},{7,11},{8,12},{9,5},{10,... | collective-permute-start | bytes 1572872 | tf_op jit(solution)/shard_map/ppermute | solution.py:339
  12.1 11.0 %collective-permute-start.7 = (bf16[2,32,4096]{2,1,0:T(8,128)(2,1)S(1)}, bf16[2,32,4096]{2,1,0:T(8,128)(2,1)S(1)}, u32[]{:S(2)}, u32[]{:S(2)}) collective-permute-start(bf16[2,32,4096]{2,1,0:T(8,128)(2,1)S(1)} %precondition_1.2.refs_0_), channel_id=1, source_target_pairs={{0,1},{1,0},{2,3},{3,2},{4,5},{5,4},{6,7},{7,6},{8,9},{9,8},{10,11... | collective-permute-start | bytes 1572872 | tf_op jit(solution)/shard_map/ppermute | solution.py:339
  12.2 10.4 %collective-permute-start.1 = (bf16[2,32,4096]{2,1,0:T(8,128)(2,1)S(1)}, bf16[2,32,4096]{2,1,0:T(8,128)(2,1)S(1)}, u32[]{:S(2)}, u32[]{:S(2)}) collective-permute-start(bf16[2,32,4096]{2,1,0:T(8,128)(2,1)S(1)} %precondition_1.2.refs_0_), channel_id=1, source_target_pairs={{0,4},{1,3},{2,0},{3,7},{4,8},{5,1},{6,2},{7,11},{8,12},{9,5},{10,... | collective-permute-start | bytes 1572872 | tf_op jit(solution)/shard_map/ppermute | solution.py:339
  17.5 7.1 %collective-permute-start.8 = (bf16[2,32,4096]{2,1,0:T(8,128)(2,1)S(1)}, bf16[2,32,4096]{2,1,0:T(8,128)(2,1)S(1)}, u32[]{:S(2)}, u32[]{:S(2)}) collective-permute-start(bf16[2,32,4096]{2,1,0:T(8,128)(2,1)S(1)} %precondition_1.3.refs_1_), channel_id=1, source_target_pairs={{0,1},{1,0},{2,3},{3,2},{4,5},{5,4},{6,7},{7,6},{8,9},{9,8},{10,11... | collective-permute-start | bytes 1572872 | tf_op jit(solution)/shard_map/ppermute | solution.py:339
  17.6 9.5 %collective-permute-start.6 = (bf16[2,32,4096]{2,1,0:T(8,128)(2,1)S(1)}, bf16[2,32,4096]{2,1,0:T(8,128)(2,1)S(1)}, u32[]{:S(2)}, u32[]{:S(2)}) collective-permute-start(bf16[2,32,4096]{2,1,0:T(8,128)(2,1)S(1)} %precondition_1.3.refs_1_), channel_id=1, source_target_pairs={{0,4},{1,3},{2,0},{3,7},{4,8},{5,1},{6,2},{7,11},{8,12},{9,5},{10,... | collective-permute-start | bytes 1572872 | tf_op jit(solution)/shard_map/ppermute | solution.py:339
  22.5 6.9 %collective-permute-start.3 = (bf16[2,32,4096]{2,1,0:T(8,128)(2,1)S(1)}, bf16[2,32,4096]{2,1,0:T(8,128)(2,1)S(1)}, u32[]{:S(2)}, u32[]{:S(2)}) collective-permute-start(bf16[2,32,4096]{2,1,0:T(8,128)(2,1)S(1)} %precondition_0.1.refs_0_), channel_id=1, source_target_pairs={{0,1},{1,0},{2,3},{3,2},{4,5},{5,4},{6,7},{7,6},{8,9},{9,8},{10,11... | collective-permute-start | bytes 1572872 | tf_op jit(solution)/shard_map/ppermute | solution.py:339
  22.7 8.5 %collective-permute-start.9 = (bf16[2,32,4096]{2,1,0:T(8,128)(2,1)S(1)}, bf16[2,32,4096]{2,1,0:T(8,128)(2,1)S(1)}, u32[]{:S(2)}, u32[]{:S(2)}) collective-permute-start(bf16[2,32,4096]{2,1,0:T(8,128)(2,1)S(1)} %collective-permute-done.1.refs_0_), channel_id=1, source_target_pairs={{0,1},{1,0},{2,3},{3,2},{4,5},{5,4},{6,7},{7,6},{8,9},{9,8},{10,11... | collective-permute-start | bytes 1572872 | tf_op jit(solution)/shard_map/ppermute | solution.py:339
  23.1 11.1 %collective-permute-start.2 = (bf16[2,32,4096]{2,1,0:T(8,128)(2,1)S(1)}, bf16[2,32,4096]{2,1,0:T(8,128)(2,1)S(1)}, u32[]{:S(2)}, u32[]{:S(2)}) collective-permute-start(bf16[2,32,4096]{2,1,0:T(8,128)(2,1)S(1)} %collective-permute-done.1.refs_0_), channel_id=1, source_target_pairs={{0,4},{1,3},{2,0},{3,7},{4,8},{5,1},{6,2},{7,11},{8,12},{9,5},{10,... | collective-permute-start | bytes 1572872 | tf_op jit(solution)/shard_map/ppermute | solution.py:339
  27.2 11.2 %collective-permute-start.13 = (bf16[2,32,4096]{2,1,0:T(8,128)(2,1)S(1)}, bf16[2,32,4096]{2,1,0:T(8,128)(2,1)S(1)}, u32[]{:S(2)}, u32[]{:S(2)}) collective-permute-start(bf16[2,32,4096]{2,1,0:T(8,128)(2,1)S(1)} %collective-permute-done.6.refs_1_), channel_id=1, source_target_pairs={{0,4},{1,3},{2,0},{3,7},{4,8},{5,1},{6,2},{7,11},{8,12},{9,5},{10,... | collective-permute-start | bytes 1572872 | tf_op jit(solution)/shard_map/ppermute | solution.py:339
  29.3 1.8 %collective-permute-start.10 = (bf16[1,32,4096]{2,1,0:T(8,128)(2,1)S(1)}, bf16[1,32,4096]{2,1,0:T(8,128)(2,1)S(1)}, u32[]{:S(2)}, u32[]{:S(2)}) collective-permute-start(bf16[1,32,4096]{2,1,0:T(8,128)(2,1)S(1)} %get-tuple-element.38), channel_id=1, source_target_pairs={{0,1},{1,0},{2,3},{3,2},{4,5},{5,4},{6,7},{7,6},{8,9},{9,8},{10,11... | collective-permute-start | bytes 786440 | tf_op jit(solution)/shard_map/ppermute | solution.py:339
  29.4 1.9 %collective-permute-start.11 = (bf16[1,32,4096]{2,1,0:T(8,128)(2,1)S(1)}, bf16[1,32,4096]{2,1,0:T(8,128)(2,1)S(1)}, u32[]{:S(2)}, u32[]{:S(2)}) collective-permute-start(bf16[1,32,4096]{2,1,0:T(8,128)(2,1)S(1)} %get-tuple-element.37), channel_id=1, source_target_pairs={{0,1},{1,0},{2,3},{3,2},{4,5},{5,4},{6,7},{7,6},{8,9},{9,8},{10,11... | collective-permute-start | bytes 786440 | tf_op jit(solution)/shard_map/ppermute | solution.py:339
  32.6 5.6 %collective-permute-start.14 = (bf16[128,512]{1,0:T(8,128)(2,1)S(1)}, bf16[128,512]{1,0:T(8,128)(2,1)S(1)}, u32[]{:S(2)}, u32[]{:S(2)}) collective-permute-start(bf16[128,512]{1,0:T(8,128)(2,1)S(1)} %get-tuple-element.22), channel_id=1, source_target_pairs={{0,16},{1,17},{2,18},{3,19},{4,20},{5,21},{6,22},{7,23},{8,24},{9,... | collective-permute-start | bytes 393224 | tf_op jit(solution)/shard_map/ppermute | solution.py:339
  34.2 6.3 %collective-permute-start.15 = (bf16[2,32,4096]{2,1,0:T(8,128)(2,1)S(1)}, bf16[2,32,4096]{2,1,0:T(8,128)(2,1)S(1)}, u32[]{:S(2)}, u32[]{:S(2)}) collective-permute-start(bf16[2,32,4096]{2,1,0:T(8,128)(2,1)S(1)} %collective-permute-done.2.refs_0_), channel_id=1, source_target_pairs={{0,1},{1,0},{2,3},{3,2},{4,5},{5,4},{6,7},{7,6},{8,9},{9,8},{10,11... | collective-permute-start | bytes 1572872 | tf_op jit(solution)/shard_map/ppermute | solution.py:339
  34.2 9.9 %collective-permute-start.12 = (bf16[2,32,4096]{2,1,0:T(8,128)(2,1)S(1)}, bf16[2,32,4096]{2,1,0:T(8,128)(2,1)S(1)}, u32[]{:S(2)}, u32[]{:S(2)}) collective-permute-start(bf16[2,32,4096]{2,1,0:T(8,128)(2,1)S(1)} %collective-permute-done.2.refs_0_), channel_id=1, source_target_pairs={{0,4},{1,3},{2,0},{3,7},{4,8},{5,1},{6,2},{7,11},{8,12},{9,5},{10,... | collective-permute-start | bytes 1572872 | tf_op jit(solution)/shard_map/ppermute | solution.py:339
  38.4 1.6 %collective-permute-start.16 = (bf16[1,32,4096]{2,1,0:T(8,128)(2,1)S(1)}, bf16[1,32,4096]{2,1,0:T(8,128)(2,1)S(1)}, u32[]{:S(2)}, u32[]{:S(2)}) collective-permute-start(bf16[1,32,4096]{2,1,0:T(8,128)(2,1)S(1)} %get-tuple-element.36), channel_id=1, source_target_pairs={{0,1},{1,0},{2,3},{3,2},{4,5},{5,4},{6,7},{7,6},{8,9},{9,8},{10,11... | collective-permute-start | bytes 786440 | tf_op jit(solution)/shard_map/ppermute | solution.py:339
  38.5 1.9 %collective-permute-start.17 = (bf16[1,32,4096]{2,1,0:T(8,128)(2,1)S(1)}, bf16[1,32,4096]{2,1,0:T(8,128)(2,1)S(1)}, u32[]{:S(2)}, u32[]{:S(2)}) collective-permute-start(bf16[1,32,4096]{2,1,0:T(8,128)(2,1)S(1)} %get-tuple-element.35), channel_id=1, source_target_pairs={{0,1},{1,0},{2,3},{3,2},{4,5},{5,4},{6,7},{7,6},{8,9},{9,8},{10,11... | collective-permute-start | bytes 786440 | tf_op jit(solution)/shard_map/ppermute | solution.py:339
  41.9 6.7 %collective-permute-start.23 = (bf16[160,512]{1,0:T(8,128)(2,1)S(1)}, bf16[160,512]{1,0:T(8,128)(2,1)S(1)}, u32[]{:S(2)}, u32[]{:S(2)}) collective-permute-start(bf16[160,512]{1,0:T(8,128)(2,1)S(1)} %get-tuple-element.26), channel_id=1, source_target_pairs={{0,16},{1,17},{2,18},{3,19},{4,20},{5,21},{6,22},{7,23},{8,24},{9,... | collective-permute-start | bytes 491528 | tf_op jit(solution)/shard_map/ppermute | solution.py:339
  44.1 1.4 %collective-permute-start.18 = (bf16[1,16,4096]{2,1,0:T(8,128)(2,1)S(1)}, bf16[1,16,4096]{2,1,0:T(8,128)(2,1)S(1)}, u32[]{:S(2)}, u32[]{:S(2)}) collective-permute-start(bf16[1,16,4096]{2,1,0:T(8,128)(2,1)S(1)} %get-tuple-element.34), channel_id=1, source_target_pairs={{0,1},{1,0},{2,3},{3,2},{4,5},{5,4},{6,7},{7,6},{8,9},{9,8},{10,11... | collective-permute-start | bytes 393224 | tf_op jit(solution)/shard_map/ppermute | solution.py:339
  44.1 1.5 %collective-permute-start.19 = (bf16[1,16,4096]{2,1,0:T(8,128)(2,1)S(1)}, bf16[1,16,4096]{2,1,0:T(8,128)(2,1)S(1)}, u32[]{:S(2)}, u32[]{:S(2)}) collective-permute-start(bf16[1,16,4096]{2,1,0:T(8,128)(2,1)S(1)} %get-tuple-element.33), channel_id=1, source_target_pairs={{0,1},{1,0},{2,3},{3,2},{4,5},{5,4},{6,7},{7,6},{8,9},{9,8},{10,11... | collective-permute-start | bytes 393224 | tf_op jit(solution)/shard_map/ppermute | solution.py:339
  44.6 1.7 %collective-permute-start.20 = (bf16[1,16,4096]{2,1,0:T(8,128)(2,1)S(1)}, bf16[1,16,4096]{2,1,0:T(8,128)(2,1)S(1)}, u32[]{:S(2)}, u32[]{:S(2)}) collective-permute-start(bf16[1,16,4096]{2,1,0:T(8,128)(2,1)S(1)} %get-tuple-element.32), channel_id=1, source_target_pairs={{0,1},{1,0},{2,3},{3,2},{4,5},{5,4},{6,7},{7,6},{8,9},{9,8},{10,11... | collective-permute-start | bytes 393224 | tf_op jit(solution)/shard_map/ppermute | solution.py:339
  44.7 1.7 %collective-permute-start.21 = (bf16[1,16,4096]{2,1,0:T(8,128)(2,1)S(1)}, bf16[1,16,4096]{2,1,0:T(8,128)(2,1)S(1)}, u32[]{:S(2)}, u32[]{:S(2)}) collective-permute-start(bf16[1,16,4096]{2,1,0:T(8,128)(2,1)S(1)} %get-tuple-element.31), channel_id=1, source_target_pairs={{0,1},{1,0},{2,3},{3,2},{4,5},{5,4},{6,7},{7,6},{8,9},{9,8},{10,11... | collective-permute-start | bytes 393224 | tf_op jit(solution)/shard_map/ppermute | solution.py:339
  47.2 4.4 %collective-permute-start.22 = (bf16[64,512]{1,0:T(8,128)(2,1)S(1)}, bf16[64,512]{1,0:T(8,128)(2,1)S(1)}, u32[]{:S(2)}, u32[]{:S(2)}) collective-permute-start(bf16[64,512]{1,0:T(8,128)(2,1)S(1)} %scores_5.1), channel_id=1, source_target_pairs={{0,16},{1,17},{2,18},{3,19},{4,20},{5,21},{6,22},{7,23},{8,24},{9,... | collective-permute-start | bytes 196616 | tf_op jit(solution)/shard_map/ppermute | solution.py:339
  (2 other events, 5.4 us)
